TPU v7x, 32 devices: a whole 2x2x4 slice. The times are simulated.
32 devices in a mesh: ctx: 8 (over z, x), head: 4 (over y, core).
Axes of the slice: x: 2, y: 2, z: 4, core: 2. Of those that a mesh axis runs over, the one named last changes fastest.
Arguments:
- queries: bfloat16 [1024, 8192], P('ctx', 'head'), may hold values from -7 to 7
- span_kv: bfloat16 [1024, 8, 256], P('ctx', 'head'), may hold values from -7 to 7
- cache_kv: bfloat16 [32768, 8, 256], P('ctx', 'head'), may hold values from -6 to 6
- verticals: int32 [8, 64], P('head'), may hold values from 0 to 511, as said below
- offsets: int32 [8, 8], P('head'), may hold values from 0 to 7, as said below
Outputs:
- attended: bfloat16 [1024, 8192], P(('ctx', 'head'))
Inputs may be any that keep to these rules, and one draw needn't show every extreme that they name: `verticals`: each row holds 64 distinct cache blocks. Cache block b lies in the cache of index b // 64 of ctx; at most 16 blocks of one row lie in one index's cache, and in every row some index holds exactly 16. Each row holds 8 distinct offsets, 0 among them; some row holds 7.
All inputs are finite; a program needn't handle non-finite values.
Results may differ from a plain program's by a relative error of at most 0.0065.
Values may be sent and summed in bfloat16 or wider, within the bound.
No kernel may reach another device: no remote copies, remote signals or barrier semaphores. Data moves between devices by JAX's collectives and lax.ppermute only.
A program may use at most 192 MiB of HBM per device.

v0:
```python
import functools

import jax
import jax.numpy as jnp
from jax import lax
from jax.experimental import pallas as pl
from jax.experimental.pallas import tpu as pltpu
from jax.sharding import PartitionSpec as P

BLK = 64
NV = 64
MASKED = -1e30
CHUNK = 8
LOG2E = 1.4426950408889634


def collect_kernel(owners, cap, verticals, cache, span, mine, theirs, theirs_rest, raw, sem):
    me = lax.axis_index("ctx")
    upper = me // (owners // 2)
    cache_blocks = cache.shape[0] // BLK
    first = me * cache_blocks

    def block_copy(block, place, slot):
        return pltpu.make_async_copy(
            cache.at[pl.ds(pl.multiple_of(block * BLK, BLK), BLK)], raw.at[place, slot], sem.at[place, slot]
        )

    found = []
    for place in range(2):
        head = upper if place == 0 else 1 - upper

        def visit(n, count):
            block = verticals[head, n] - first
            hit = (block >= 0) & (block < cache_blocks) & (count < cap)

            @pl.when(hit)
            def _():
                block_copy(block, place, count).start()

            return count + hit.astype(jnp.int32)

        found.append(lax.fori_loop(0, NV, visit, jnp.int32(0)))
    split = cap // 2
    for own in range(2):

        @pl.when(upper == own)
        def _():
            mine[cap * BLK :, :] = span[:, own, :]
            theirs[split * BLK :, :] = span[:, 1 - own, :]
            for place, target, start, stop in ((1, theirs, 0, split), (1, theirs_rest, split, cap), (0, mine, 0, cap)):
                head = own if place == 0 else 1 - own

                def unpack(slot, carry):
                    block_copy(0, place, slot).wait()
                    at = pl.ds(pl.multiple_of((slot - start) * BLK, BLK), BLK)
                    target[at, :] = raw[place, slot, :, head, :]
                    return carry

                lax.fori_loop(start, jnp.minimum(found[place], stop), unpack, 0)


class Stage:
    def __init__(self, owners, group, depth, tokens, width, parts, pieces, known, late, first, last):
        self.owners, self.group, self.depth = owners, group, depth
        self.tokens, self.width, self.parts = tokens, width, parts
        self.pieces, self.known, self.late = pieces, known, late
        self.first, self.last = first, last
        self.half = owners // 2
        self.blocks = tokens // BLK
        self.rows = group * BLK
        self.state_rows = 2 * self.blocks * self.rows
        self.slash = bool(late) and not last

    def owner(self, far, m, *_):
        me = lax.axis_index("ctx")
        upper = me // self.half
        return ((1 - upper) if far else upper) * self.half + ((me % self.half) ^ m)


def attend_kernel(stage, scalars, offsets, *refs):
    refs = list(refs)

    def take(count):
        taken, refs[:count] = refs[:count], []
        return taken

    half, blocks, rows, depth, tokens = stage.half, stage.blocks, stage.rows, stage.depth, stage.tokens
    me = lax.axis_index("ctx")
    upper = me // half
    head = upper
    width_kv = 2 * depth
    factor = LOG2E * depth**-0.5
    if stage.first:
        q_near, q_far = take(2)
    else:
        (queries,) = take(1)
    sources = take(len(stage.pieces))
    if stage.first:
        top, acc, queries, counts = take(4)
    else:
        take(2)
        top, acc = take(2)
        counts = scalars
    outs = take(stage.parts) if stage.last else []
    keys, sem = take(2)

    if stage.first:

        def clear(n, carry):
            counts[n] = 0
            return carry

        lax.fori_loop(0, stage.owners, clear, 0)

        def tally(n, carry):
            owner = scalars[head, n] // stage.width
            counts[owner] = counts[owner] + 1
            return carry

        lax.fori_loop(0, NV, tally, 0)

    held = [
        jnp.clip(counts[stage.owner(*piece)] - piece[2][0], 0, piece[2][1] - piece[2][0]) for piece in stage.pieces
    ]
    seen = sum(held[: stage.known], jnp.int32(0))
    present = sum(held[stage.known :], seen)
    begin = seen // CHUNK * CHUNK
    end = jnp.int32(NV) if stage.last else present // CHUNK * CHUNK
    place = jnp.int32(0)
    for source, live in zip(sources, held):

        def fetch(n, carry, place=place, source=source):
            at = place + n - begin
            pltpu.make_async_copy(
                source.at[pl.ds(pl.multiple_of(n * BLK, BLK), BLK)],
                keys.at[pl.ds(pl.multiple_of(at * BLK, BLK), BLK), pl.ds(0, width_kv)],
                sem.at[at // CHUNK],
            ).start()
            return carry

        lax.fori_loop(jnp.clip(begin - place, 0, live), jnp.clip(end - place, 0, live), fetch, 0)
        place = place + live

    span_copies = []
    if stage.slash or stage.last:
        span, bias, span_sem = take(3)
        wanted = stage.late if stage.last else [piece for piece in stage.pieces if piece[3]]
        for n, piece in enumerate(wanted):
            at = n if stage.last else stage.owner(*piece)
            slots = piece[2][1] - piece[2][0]
            copy = pltpu.make_async_copy(
                sources[stage.pieces.index(piece)].at[pl.ds(slots * BLK, tokens)],
                span.at[pl.ds(pl.multiple_of(at * tokens, BLK), tokens), pl.ds(0, width_kv)],
                span_sem,
            )
            copy.start()
            span_copies.append(copy)
    keys[:, width_kv:] = jnp.ones((keys.shape[0], depth), keys.dtype)
    if stage.first:
        for tile in range(2 * blocks):
            q_ref, block = (q_near, tile) if tile < blocks else (q_far, tile - blocks)
            for j in range(stage.group):
                queries[tile * rows + j * BLK : tile * rows + (j + 1) * BLK, :] = q_ref[
                    block * BLK : (block + 1) * BLK, j * depth : (j + 1) * depth
                ]
        top[...] = jnp.full(top.shape, MASKED, jnp.float32)
        acc[...] = jnp.zeros(acc.shape, jnp.float32)

    def fold(at, scores, values):
        old = top[at, :]
        new = jnp.maximum(old, jnp.max(scores, axis=1, keepdims=True))
        wide = jnp.concatenate([new] * (scores.shape[1] // depth), 1)
        weights = jnp.exp2((scores - wide) * factor).astype(jnp.bfloat16)
        keep = jnp.exp2((old - new) * factor)
        top[at, :] = new
        acc[at, :] = acc[at, :] * jnp.concatenate([keep, keep], 1) + jnp.dot(
            weights, values, preferred_element_type=jnp.float32
        )

    def products(at, rows_k):
        return lax.dot_general(
            queries[at, :], rows_k, (((1,), (1,)), ((), ())), preferred_element_type=jnp.float32
        )

    tiles = [slice(tile * rows, (tile + 1) * rows) for tile in range(2 * blocks)]

    def step(c, carry):
        part = pl.ds(pl.multiple_of(c * (CHUNK * BLK), CHUNK * BLK), CHUNK * BLK)
        chunk = keys.at[part, pl.ds(0, width_kv)]
        pltpu.make_async_copy(chunk, chunk, sem.at[c]).wait()
        scores = products(tiles[0], keys[part, :depth])
        for at, following in zip(tiles, tiles[1:] + [None]):
            ahead = products(following, keys[part, :depth]) if following else None
            fold(at, scores, keys[part, depth:])
            scores = ahead
        return carry

    lax.fori_loop(0, (end - begin) // CHUNK, step, 0)

    if span_copies:
        for copy in span_copies:
            copy.wait()
        slash_count = offsets.shape[1]
        q_at = lax.broadcasted_iota(jnp.int32, (BLK, BLK), 0)
        k_at = lax.broadcasted_iota(jnp.int32, (BLK, BLK), 1)
        behind = k_at <= q_at
        late_owners = [stage.owner(*piece) for piece in stage.late]

        def masked(at, tile, rows_k, values):
            scores = products(at, rows_k)
            scores = scores.reshape(stage.group, BLK, rows_k.shape[0]) + bias[tile][None]
            fold(at, scores.reshape(rows, rows_k.shape[0]), values)

        if stage.slash:
            (slash,) = take(1)
            slash[:, :, width_kv:] = jnp.ones((2 * blocks, slash_count * BLK, depth), slash.dtype)
        else:
            span[:, width_kv:] = jnp.ones((span.shape[0], depth), span.dtype)
        for tile, at in enumerate(tiles):
            index = me if tile < blocks else (me + half) % stage.owners
            position = index * blocks + tile % blocks
            if stage.slash:
                for s in range(slash_count):
                    offset = offsets[head, s]
                    block = position - offset
                    here = block >= 0
                    for owner in late_owners:
                        here = here & (block // blocks != owner)
                    start = pl.multiple_of(jnp.where(here, block, position) * BLK, BLK)
                    slash[tile, s * BLK : (s + 1) * BLK, :width_kv] = span[pl.ds(start, BLK), :]
                    allowed = here & ((offset > 0) | behind)
                    bias[tile, :, s * BLK : (s + 1) * BLK] = jnp.where(allowed, 0.0, MASKED)
                masked(at, tile, slash[tile, :, :depth], slash[tile, :, depth:])
            else:
                for n, owner in enumerate(late_owners):
                    for k in range(blocks):
                        distance = position - (owner * blocks + k)
                        chosen = distance == offsets[head, 0]
                        for s in range(1, slash_count):
                            chosen = chosen | (distance == offsets[head, s])
                        allowed = chosen & ((distance > 0) | behind)
                        column = n * tokens + k * BLK
                        bias[tile, :, column : column + BLK] = jnp.where(allowed, 0.0, MASKED)
                masked(at, tile, span[:, :depth], span[:, depth:])

    if stage.last:
        lane = lax.axis_index("head")
        for k, out in enumerate(outs):
            part_rows = out.shape[0]
            token = (lane ^ (k >> 1)) * part_rows
            base = ((k & 1) * blocks + token // BLK) * rows + token % BLK
            for j in range(stage.group):
                at = pl.ds(pl.multiple_of(base + j * BLK, part_rows), part_rows)
                both = acc[at, :]
                out[:, j * depth : (j + 1) * depth] = (both[:, :depth] / both[:, depth:]).astype(out.dtype)


def attend(stage, scalars, offsets, queries, pieces, state, name):
    depth, rows, blocks = stage.depth, stage.state_rows, stage.blocks
    kind = jnp.bfloat16
    held = [jax.ShapeDtypeStruct((rows, depth), jnp.float32), jax.ShapeDtypeStruct((rows, 2 * depth), jnp.float32)]
    vmem, smem = pl.BlockSpec(memory_space=pltpu.VMEM), pl.BlockSpec(memory_space=pltpu.SMEM)
    out_shape, out_specs = list(held), [vmem] * 2
    if stage.first:
        out_shape += [
            jax.ShapeDtypeStruct((rows, depth), kind),
            jax.ShapeDtypeStruct((stage.owners,), jnp.int32),
        ]
        out_specs += [vmem, smem]
    if stage.last:
        part = jax.ShapeDtypeStruct((2 * stage.tokens // stage.parts, stage.group * depth), kind)
        out_shape += [part] * stage.parts
        out_specs += [vmem] * stage.parts
    scratch = [pltpu.VMEM((NV * BLK, 3 * depth), kind), pltpu.SemaphoreType.DMA((NV // CHUNK,))]
    share = sum(piece[3] for piece in stage.pieces[stage.known :]) * NV // stage.owners * BLK
    if stage.slash:
        keys = offsets.shape[1] * BLK
        scratch += [
            pltpu.VMEM((stage.owners * stage.tokens, 2 * depth), kind),
            pltpu.VMEM((2 * blocks, BLK, keys), jnp.float32),
            pltpu.SemaphoreType.DMA,
            pltpu.VMEM((2 * blocks, keys, 3 * depth), kind),
        ]
        share += keys
    elif stage.last:
        keys = len(stage.late) * stage.tokens
        scratch += [
            pltpu.VMEM((keys, 3 * depth), kind),
            pltpu.VMEM((2 * blocks, BLK, keys), jnp.float32),
            pltpu.SemaphoreType.DMA,
        ]
    operands = [scalars, offsets, *queries, *pieces, *state]
    in_specs = [vmem] * len(queries) + [pl.BlockSpec(memory_space=pl.ANY)] * len(pieces) + [vmem] * len(state)
    return pl.pallas_call(
        functools.partial(attend_kernel, stage),
        out_shape=out_shape,
        grid_spec=pltpu.PrefetchScalarGridSpec(
            num_scalar_prefetch=2, grid=(1,), in_specs=in_specs, out_specs=out_specs, scratch_shapes=scratch
        ),
        input_output_aliases={len(operands) - len(state) + n: n for n in range(len(state))},
        compiler_params=pltpu.CompilerParams(vmem_limit_bytes=28 * 1024 * 1024),
        cost_estimate=pl.CostEstimate(
            flops=2 * rows * depth * share // 4, bytes_accessed=share * 4 * depth, transcendentals=0
        ),
        name=name,
    )(*operands)


def place_kernel(head_groups, half, *refs):
    *parts, out, sem = refs
    here = lax.axis_index("head") * 2 + lax.axis_index("ctx") // half
    copies = []
    for k, part in enumerate(parts):
        columns = part.shape[1]
        start = pl.multiple_of((here ^ k) * columns, columns)
        copies.append(pltpu.make_async_copy(part, out.at[:, pl.ds(start, columns)], sem.at[k]))
        copies[-1].start()
    for copy in copies:
        copy.wait()


def body(queries, span_kv, cache_kv, verticals, offsets):
    tokens = queries.shape[0]
    heads_kv, row_width = span_kv.shape[1:]
    depth = row_width // 2
    columns = queries.shape[1] // heads_kv
    group = columns // depth
    owners = lax.axis_size("ctx")
    head_groups = lax.axis_size("head")
    half = owners // 2
    cache_blocks = cache_kv.shape[0] // BLK
    cap = max(2, 2 * NV // owners)
    upper = lax.axis_index("ctx") // half

    across = [(i, (i + half) % owners) for i in range(owners)]
    send_q = lax.dynamic_slice_in_dim(queries, (1 - upper) * columns, columns, 1)
    q_near = lax.dynamic_slice_in_dim(queries, upper * columns, columns, 1)
    q_far = lax.ppermute(send_q, "ctx", across)
    split = cap // 2

    def rows_of(count):
        return jax.ShapeDtypeStruct((count, row_width), queries.dtype)

    mine, theirs, theirs_rest = pl.pallas_call(
        functools.partial(collect_kernel, owners, cap),
        out_shape=(rows_of(cap * BLK + tokens), rows_of(split * BLK + tokens), rows_of((cap - split) * BLK)),
        grid_spec=pltpu.PrefetchScalarGridSpec(
            num_scalar_prefetch=1,
            grid=(1,),
            in_specs=[pl.BlockSpec(memory_space=pl.ANY), pl.BlockSpec(memory_space=pltpu.VMEM)],
            out_specs=[pl.BlockSpec(memory_space=pltpu.VMEM)] * 3,
            scratch_shapes=[
                pltpu.VMEM((2, cap, BLK, heads_kv, row_width), queries.dtype),
                pltpu.SemaphoreType.DMA((2, cap)),
            ],
        ),
        compiler_params=pltpu.CompilerParams(vmem_limit_bytes=60 * 1024 * 1024),
        cost_estimate=pl.CostEstimate(
            flops=0, bytes_accessed=4 * cap * BLK * heads_kv * row_width, transcendentals=0
        ),
        name="collect_slots",
    )(verticals, cache_kv, span_kv)

    def swap(x, bit):
        return lax.ppermute(x, "ctx", [(i, i ^ bit) for i in range(owners)])

    bits = []
    bit = half // 2
    while bit:
        bits.append(bit)
        bit //= 2
    parts = 2 * head_groups
    whole, low, high = (0, cap), (0, split), (split, cap)
    last_bit = bits[-1]
    late = [(True, m | last_bit, low, True) for m in range(1, half) if not m & last_bit]
    places, values = [], []
    state, operands, scalars = [], [q_near, q_far], verticals

    def stage(name, *arrived, slash=False, last=False):
        nonlocal state, operands, scalars
        known, first = len(places), not places
        for far_side, slots, tail, sides in arrived:
            places.extend((far_side, m, slots, tail) for m in sides)
            values.extend(sides.values())
        kind = Stage(
            owners, group, depth, tokens, cache_blocks, parts, list(places), known,
            late if slash or last else [], first, last,
        )
        top, acc, *more = attend(kind, scalars, offsets, operands, values, state, name)
        state = [top, acc]
        if first:
            operands, scalars = [more[0]], more[1]
        return more

    theirs, q_far = lax.optimization_barrier((theirs, q_far))
    operands[1] = q_far
    near = {0: mine}
    far = {0: lax.ppermute(theirs, "ctx", across)}
    rest = {0: lax.ppermute(theirs_rest, "ctx", across)}
    own = swap(mine, last_bit)
    for bit in bits[:-1]:
        near.update({m | bit: swap(x, bit) for m, x in near.items()})
    del near[0]
    forwarded = {m | last_bit: swap(x, last_bit) for m, x in near.items()}
    stage("attend_own", (False, whole, True, {0: mine}))
    first_far, own, state = lax.optimization_barrier((far[0], own, state))
    far_own = swap(first_far, last_bit)
    rest[0], far_own = lax.optimization_barrier((rest[0], far_own))
    stage("attend_near", (False, whole, True, {last_bit: own} | near), (True, low, True, {0: first_far}))
    rest[0], state = lax.optimization_barrier((rest[0], state))
    for bit in bits[:-1]:
        far.update({m | bit: swap(x, bit) for m, x in far.items()})
        rest.update({m | bit: swap(x, bit) for m, x in rest.items()})
    far.pop(0)
    last_far = {m | last_bit: swap(x, last_bit) for m, x in far.items()}
    rest_own = swap(rest[0], last_bit)
    stage("attend_forwarded", (False, whole, True, forwarded), (True, low, True, {last_bit: far_own}))
    first_rest = rest.pop(0)
    last_rest = {m | last_bit: swap(x, last_bit) for m, x in rest.items()}
    stage(
        "attend_far", (True, low, True, far), (True, high, False, {0: first_rest, last_bit: rest_own}),
        (True, high, False, rest), slash=True,
    )
    sent = stage("attend_last", (True, low, True, last_far), (True, high, False, last_rest), last=True)

    def partner(device, k):
        index, lane = divmod(device, head_groups)
        place = (lane * 2 + index // half) ^ k
        return (place % 2 * half + index % half) * head_groups + place // 2

    devices = range(owners * head_groups)
    placed = {0: sent[0]}
    for k in sorted(range(1, parts), key=lambda k: (1 - k % 2, k)):
        placed[k] = lax.ppermute(sent[k], ("ctx", "head"), [(d, partner(d, k)) for d in devices])
    return pl.pallas_call(
        functools.partial(place_kernel, head_groups, half),
        out_shape=jax.ShapeDtypeStruct((tokens // head_groups, parts * columns), queries.dtype),
        in_specs=[pl.BlockSpec(memory_space=pltpu.VMEM)] * parts,
        out_specs=pl.BlockSpec(memory_space=pl.ANY),
        scratch_shapes=[pltpu.SemaphoreType.DMA((parts,))],
        name="place_parts",
    )(*[placed[k] for k in range(parts)])


def solution(mesh):
    in_specs = (
        P("ctx", "head"),
        P("ctx", "head", None),
        P("ctx", "head", None),
        P("head", None),
        P("head", None),
    )
    out_specs = P(("ctx", "head"), None)
    return jax.shard_map(body, mesh=mesh, in_specs=in_specs, out_specs=out_specs, check_vma=False)
```

profile of v0, /device:TPU:0, one launch (start us, length us, event | category | flops | bytes accessed | tf_op | source)
XLA Modules:
  0.0 99.5 jit_solution(10035023488633586943)
XLA Ops:
  0.0 1.1 %constant_dynamic-slice_fusion = (bf16[128,1024]{1,0:T(8,128)(2,1)S(1)}, bf16[128,1024]{1,0:T(8,128)(2,1)S(1)}) fusion(bf16[128,2048]{1,0:T(8,128)(2,1)} %param.5, s32[]{:T(128)S(6)} %select_n.13, s32[]{:T(128)S(6)} %select_n.12), kind=kLoop, calls=%fused_computation | loop fusion | bytes 1048584 | tf_op jit(solution)/shard_map/dynamic_slice | solution.py:336
  1.1 0.0 copy-start.3
  1.1 0.0 copy-start.4
  1.1 4.1 %collective-permute-start = (bf16[128,1024]{1,0:T(8,128)(2,1)S(1)}, bf16[128,1024]{1,0:T(8,128)(2,1)S(1)}, u32[]{:S(2)}, u32[]{:S(2)}) collective-permute-start(bf16[128,1024]{1,0:T(8,128)(2,1)S(1)} %get-tuple-element.69), channel_id=1, source_target_pairs={{0,16},{4,20},{8,24},{12,28},{16,0},{20,4},{24,8},{28,12},{1,17},{... | collective-permute-start | bytes 786440 | tf_op jit(solution)/shard_map/ppermute | solution.py:338
  5.2 5.0 %collect_slots.1 = (bf16[1152,256]{1,0:T(8,128)(2,1)}, bf16[640,256]{1,0:T(8,128)(2,1)}, bf16[512,256]{1,0:T(8,128)(2,1)}) custom-call(s32[2,64]{1,0:T(2,128)} %scalars.1, bf16[4096,2,256]{2,1,0:T(2,128)(2,1)} %cache.1, bf16[128,2,256]{2,1,0:T(2,128)(2,1)} %span.1), custom_call_target="tpu_custom_call" | custom-call | bytes 2097152 | tf_op jit(solution)/shard_map/collect_slots/pallas_call | solution.py:344
  10.2 2.0 %collective-permute-start.2 = (bf16[1152,256]{1,0:T(8,128)(2,1)}, bf16[1152,256]{1,0:T(8,128)(2,1)S(1)}, u32[]{:S(2)}, u32[]{:S(2)}) collective-permute-start(bf16[1152,256]{1,0:T(8,128)(2,1)} %get-tuple-element.39.refs_2_.refs_1_), channel_id=1, source_target_pairs={{0,4},{4,0},{8,12},{12,8},{16,20},{20,16},{24,28},{28,24},{1,5},{5... | collective-permute-start | bytes 1769480 | tf_op jit(solution)/shard_map/ppermute | solution.py:365
  12.3 1.9 %collective-permute-start.3 = (bf16[1152,256]{1,0:T(8,128)(2,1)}, bf16[1152,256]{1,0:T(8,128)(2,1)S(1)}, u32[]{:S(2)}, u32[]{:S(2)}) collective-permute-start(bf16[1152,256]{1,0:T(8,128)(2,1)} %get-tuple-element.39.refs_2_.refs_1_), channel_id=1, source_target_pairs={{0,8},{4,12},{8,0},{12,4},{16,24},{20,28},{24,16},{28,20},{1,9},{5... | collective-permute-start | bytes 1769480 | tf_op jit(solution)/shard_map/ppermute | solution.py:365
  14.2 3.0 %collective-permute-done.refs_1_ = bf16[128,1024]{1,0:T(8,128)(2,1)S(1)} collective-permute-done((bf16[128,1024]{1,0:T(8,128)(2,1)S(1)}, bf16[128,1024]{1,0:T(8,128)(2,1)S(1)}, u32[]{:S(2)}, u32[]{:S(2)}) %collective-permute-start) | collective-permute-done | bytes 262176 | tf_op jit(solution)/shard_map/ppermute | solution.py:338
  17.2 0.0 collective-permute-start.1
  17.2 0.0 copy-done.3
  17.2 0.0 copy-done.4
  17.2 0.0 copy-start
  17.2 1.1 %copy-done = bf16[1152,256]{1,0:T(8,128)(2,1)S(1)} copy-done((bf16[1152,256]{1,0:T(8,128)(2,1)S(1)}, bf16[1152,256]{1,0:T(8,128)(2,1)}, u32[]{:S(2)}) %copy-start) | copy-done | bytes 589848
  18.3 2.7 %attend_own.1 = (f32[2048,128]{1,0:T(8,128)S(1)}, f32[2048,256]{1,0:T(8,128)S(1)}, bf16[2048,128]{1,0:T(8,128)(2,1)S(1)}, s32[8]{0:T(128)S(1)}) custom-call(s32[2,64]{1,0:T(2,128)S(1)} %copy-done.4, s32[2,8]{1,0:T(2,128)S(1)} %copy-done.3, bf16[128,1024]{1,0:T(8,128)(2,1)S(1)} %get-tuple-element.70.refs_0_, ...), custom_call_target="tpu_custom_call" | custom-call | flops 67108864 | bytes 262144 | tf_op jit(solution)/shard_map/attend_own/pallas_call | solution.py:294
  21.0 13.3 %collective-permute-done.1.refs_4_ = bf16[640,256]{1,0:T(8,128)(2,1)S(1)} collective-permute-done((bf16[640,256]{1,0:T(8,128)(2,1)}, bf16[640,256]{1,0:T(8,128)(2,1)S(1)}, u32[]{:S(2)}, u32[]{:S(2)}) %collective-permute-start.1) | collective-permute-done | bytes 327712 | tf_op jit(solution)/shard_map/ppermute | solution.py:398
  34.3 0.0 collective-permute-done.2.refs_2_
  34.3 1.2 %collective-permute-start.6 = (bf16[640,256]{1,0:T(8,128)(2,1)S(1)}, bf16[640,256]{1,0:T(8,128)(2,1)S(1)}, u32[]{:S(2)}, u32[]{:S(2)}) collective-permute-start(bf16[640,256]{1,0:T(8,128)(2,1)S(1)} %collective-permute-done.1.refs_4_), channel_id=1, source_target_pairs={{0,4},{4,0},{8,12},{12,8},{16,20},{20,16},{24,28},{28,24},{1,5},{5... | collective-permute-start | bytes 983048 | tf_op jit(solution)/shard_map/ppermute | solution.py:365
  35.6 1.0 %collective-permute-start.5 = (bf16[512,256]{1,0:T(8,128)(2,1)}, bf16[512,256]{1,0:T(8,128)(2,1)S(1)}, u32[]{:S(2)}, u32[]{:S(2)}) collective-permute-start(bf16[512,256]{1,0:T(8,128)(2,1)} %get-tuple-element.47), channel_id=1, source_target_pairs={{0,16},{4,20},{8,24},{12,28},{16,0},{20,4},{24,8},{28,12},{1,17},{... | collective-permute-start | bytes 786440 | tf_op jit(solution)/shard_map/ppermute | solution.py:399
  36.6 6.9 %collective-permute-start.7 = (bf16[640,256]{1,0:T(8,128)(2,1)S(1)}, bf16[640,256]{1,0:T(8,128)(2,1)S(1)}, u32[]{:S(2)}, u32[]{:S(2)}) collective-permute-start(bf16[640,256]{1,0:T(8,128)(2,1)S(1)} %collective-permute-done.1.refs_4_), channel_id=1, source_target_pairs={{0,8},{4,12},{8,0},{12,4},{16,24},{20,28},{24,16},{28,20},{1,9},{5... | collective-permute-start | bytes 983048 | tf_op jit(solution)/shard_map/ppermute | solution.py:365
  43.5 0.0 collective-permute-done.3.refs_3_
  43.5 0.0 collective-permute-start.4
  43.5 0.0 copy-start.1
  43.5 1.1 %copy-done.1 = bf16[1152,256]{1,0:T(8,128)(2,1)S(1)} copy-done((bf16[1152,256]{1,0:T(8,128)(2,1)S(1)}, bf16[1152,256]{1,0:T(8,128)(2,1)}, u32[]{:S(2)}) %copy-start.1) | copy-done | bytes 589848
  44.6 6.3 %attend_near.1 = (f32[2048,128]{1,0:T(8,128)S(1)}, f32[2048,256]{1,0:T(8,128)S(1)}) custom-call(s32[8]{0:T(128)S(1)} %get-tuple-element.40.scalars, s32[2,8]{1,0:T(2,128)S(1)} %copy-done.3, bf16[2048,128]{1,0:T(8,128)(2,1)S(1)} %get-tuple-element.41.refs_0_, bf16[1152,256]{1,0:T(8,128)(2,1)S(1)} %copy-done.1, ...), custom_call_target="tpu_custom_call", output_to_operand_aliasing={{0}: (7, {}), {1}: (8, {})} | custom-call | flops 201326592 | bytes 786432 | tf_op jit(solution)/shard_map/attend_near/pallas_call | solution.py:294
  50.9 0.0 collective-permute-done.5.refs_8_
  50.9 0.0 collective-permute-done.6.refs_6_
  50.9 0.1 collective-permute-start.9
  51.0 0.0 collective-permute-done.7.refs_7_
  51.0 3.9 %collective-permute-start.10 = (bf16[640,256]{1,0:T(8,128)(2,1)S(1)}, bf16[640,256]{1,0:T(8,128)(2,1)S(1)}, u32[]{:S(2)}, u32[]{:S(2)}) collective-permute-start(bf16[640,256]{1,0:T(8,128)(2,1)S(1)} %collective-permute-done.7.refs_7_), channel_id=1, source_target_pairs={{0,4},{4,0},{8,12},{12,8},{16,20},{20,16},{24,28},{28,24},{1,5},{5... | collective-permute-start | bytes 983048 | tf_op jit(solution)/shard_map/ppermute | solution.py:365
  54.9 0.1 collective-permute-start.8
  55.0 2.4 %collective-permute-done.9.refs_10_ = bf16[512,256]{1,0:T(8,128)(2,1)S(1)} collective-permute-done((bf16[512,256]{1,0:T(8,128)(2,1)S(1)}, bf16[512,256]{1,0:T(8,128)(2,1)S(1)}, u32[]{:S(2)}, u32[]{:S(2)}) %collective-permute-start.9) | collective-permute-done | bytes 262176 | tf_op jit(solution)/shard_map/ppermute | solution.py:365
  57.3 3.8 %collective-permute-start.11 = (bf16[512,256]{1,0:T(8,128)(2,1)S(1)}, bf16[512,256]{1,0:T(8,128)(2,1)S(1)}, u32[]{:S(2)}, u32[]{:S(2)}) collective-permute-start(bf16[512,256]{1,0:T(8,128)(2,1)S(1)} %collective-permute-done.9.refs_10_), channel_id=1, source_target_pairs={{0,4},{4,0},{8,12},{12,8},{16,20},{20,16},{24,28},{28,24},{1,5},{5... | collective-permute-start | bytes 786440 | tf_op jit(solution)/shard_map/ppermute | solution.py:365
  61.2 0.0 collective-permute-done.4.refs_5_
  61.2 6.3 %attend_forwarded.1 = (f32[2048,128]{1,0:T(8,128)S(1)}, f32[2048,256]{1,0:T(8,128)S(1)}) custom-call(s32[8]{0:T(128)S(1)} %get-tuple-element.40.scalars, s32[2,8]{1,0:T(2,128)S(1)} %copy-done.3, bf16[2048,128]{1,0:T(8,128)(2,1)S(1)} %get-tuple-element.41.refs_0_, bf16[1152,256]{1,0:T(8,128)(2,1)S(1)} %copy-done.1, ...), custom_call_target="tpu_custom_call", output_to_operand_aliasing={{0}: (9, {}), {1}: (10, {})} | custom-call | flops 134217728 | bytes 524288 | tf_op jit(solution)/shard_map/attend_forwarded/pallas_call | solution.py:294
  67.5 2.6 %collective-permute-done.8.refs_9_ = bf16[512,256]{1,0:T(8,128)(2,1)S(1)} collective-permute-done((bf16[512,256]{1,0:T(8,128)(2,1)S(1)}, bf16[512,256]{1,0:T(8,128)(2,1)S(1)}, u32[]{:S(2)}, u32[]{:S(2)}) %collective-permute-start.8) | collective-permute-done | bytes 262176 | tf_op jit(solution)/shard_map/ppermute | solution.py:365
  70.1 5.5 %attend_far.1 = (f32[2048,128]{1,0:T(8,128)S(1)}, f32[2048,256]{1,0:T(8,128)S(1)}) custom-call(s32[8]{0:T(128)S(1)} %get-tuple-element.40.scalars, s32[2,8]{1,0:T(2,128)S(1)} %copy-done.3, bf16[2048,128]{1,0:T(8,128)(2,1)S(1)} %get-tuple-element.41.refs_0_, bf16[1152,256]{1,0:T(8,128)(2,1)S(1)} %copy-done.1, ...), custom_call_target="tpu_custom_call", output_to_operand_aliasing={{0}: (13, {}), {1}: (14, {})} | custom-call | flops 134217728 | bytes 524288 | tf_op jit(solution)/shard_map/attend_far/pallas_call | solution.py:294
  75.6 0.0 collective-permute-done.10.refs_11_
  75.6 0.0 collective-permute-done.11.refs_12_
  75.6 4.4 %attend_last.1 = (f32[2048,128]{1,0:T(8,128)S(1)}, f32[2048,256]{1,0:T(8,128)S(1)}, bf16[32,1024]{1,0:T(8,128)(2,1)S(1)}, bf16[32,1024]{1,0:T(8,128)(2,1)S(1)}, ...) custom-call(s32[8]{0:T(128)S(1)} %get-tuple-element.40.scalars, ...), custom_call_target="tpu_custom_call", output_to_operand_aliasing={{0}: (15, {}), {1}: (16, {})} | custom-call | flops 67108864 | bytes 262144 | tf_op jit(solution)/shard_map/attend_last/pallas_call | solution.py:294
  80.0 0.0 copy-start.2
  80.0 0.6 copy-done.2
  80.6 3.0 %collective-permute-start.12 = (bf16[32,1024]{1,0:T(8,128)(2,1)S(1)}, bf16[32,1024]{1,0:T(8,128)(2,1)S(1)}, u32[]{:S(2)}, u32[]{:S(2)}) collective-permute-start(bf16[32,1024]{1,0:T(8,128)(2,1)S(1)} %get-tuple-element.62), channel_id=1, source_target_pairs={{0,16},{1,17},{2,18},{3,19},{4,20},{5,21},{6,22},{7,23},{8,24},{9,... | collective-permute-start | bytes 196616 | tf_op jit(solution)/shard_map/ppermute | solution.py:434
  83.6 0.0 collective-permute-start.13
  83.6 0.1 collective-permute-start.14
  83.7 4.7 %collective-permute-start.15 = (bf16[32,1024]{1,0:T(8,128)(2,1)S(1)}, bf16[32,1024]{1,0:T(8,128)(2,1)S(1)}, u32[]{:S(2)}, u32[]{:S(2)}) collective-permute-start(bf16[32,1024]{1,0:T(8,128)(2,1)S(1)} %get-tuple-element.65), channel_id=1, source_target_pairs={{0,2},{1,3},{2,0},{3,1},{4,6},{5,7},{6,4},{7,5},{8,10},{9,11},{10,... | collective-permute-start | bytes 196616 | tf_op jit(solution)/shard_map/ppermute | solution.py:434
  88.4 0.0 collective-permute-start.16
  88.4 0.0 collective-permute-done.12.refs_1_
  88.4 0.9 collective-permute-start.17
  89.3 0.0 collective-permute-done.13.refs_2_
  89.3 2.6 %collective-permute-start.18 = (bf16[32,1024]{1,0:T(8,128)(2,1)S(1)}, bf16[32,1024]{1,0:T(8,128)(2,1)S(1)}, u32[]{:S(2)}, u32[]{:S(2)}) collective-permute-start(bf16[32,1024]{1,0:T(8,128)(2,1)S(1)} %get-tuple-element.68), channel_id=1, source_target_pairs={{0,19},{1,18},{2,17},{3,16},{4,23},{5,22},{6,21},{7,20},{8,27},{9,... | collective-permute-start | bytes 196616 | tf_op jit(solution)/shard_map/ppermute | solution.py:434
  91.9 0.0 collective-permute-done.14.refs_3_
  91.9 0.0 collective-permute-done.15.refs_4_
  91.9 0.0 copy-start.8
  92.0 4.7 %collective-permute-done.16.refs_5_ = bf16[32,1024]{1,0:T(8,128)(2,1)S(1)} collective-permute-done((bf16[32,1024]{1,0:T(8,128)(2,1)S(1)}, bf16[32,1024]{1,0:T(8,128)(2,1)S(1)}, u32[]{:S(2)}, u32[]{:S(2)}) %collective-permute-start.16) | collective-permute-done | bytes 65568 | tf_op jit(solution)/shard_map/ppermute | solution.py:434
  96.7 0.0 collective-permute-done.17.refs_6_
  96.7 0.1 collective-permute-done.18.refs_7_
  96.8 0.0 copy-done.5
  96.8 0.0 copy-done.6
  96.8 0.0 copy-done.7
  96.8 0.0 copy-done.8
  96.8 0.5 copy-done.9
  97.3 0.0 copy-done.10
  97.3 0.1 copy-done.11
  97.4 1.9 %place_parts.1 = bf16[32,8192]{1,0:T(8,128)(2,1)} custom-call(bf16[32,1024]{1,0:T(8,128)(2,1)} %copy-done.2, bf16[32,1024]{1,0:T(8,128)(2,1)} %copy-done.5, bf16[32,1024]{1,0:T(8,128)(2,1)} %copy-done.6, bf16[32,1024]{1,0:T(8,128)(2,1)} %copy-done.7, bf16[32,1024]{1,0:T(8,128)(2,1)} %copy-done.8, bf16[32,1024]{1,0:T(8,128)(2,1)} %copy-done.9, ...), custom_call_target="tpu_custom_call" | custom-call | tf_op jit(solution)/shard_map/place_parts/pallas_call | solution.py:435
  (6 shorter events, 0.0 us)
Async XLA Ops:
  1.1 16.2 %copy-start.3 = (s32[2,8]{1,0:T(2,128)S(1)}, s32[2,8]{1,0:T(2,128)}, u32[]{:S(2)}) copy-start(s32[2,8]{1,0:T(2,128)} %offsets.9) | copy-start | bytes 196
  1.1 16.1 %copy-start.4 = (s32[2,64]{1,0:T(2,128)S(1)}, s32[2,64]{1,0:T(2,128)}, u32[]{:S(2)}) copy-start(s32[2,64]{1,0:T(2,128)} %scalars.1) | copy-start | bytes 1540
  1.1 16.1 %collective-permute-start = (bf16[128,1024]{1,0:T(8,128)(2,1)S(1)}, bf16[128,1024]{1,0:T(8,128)(2,1)S(1)}, u32[]{:S(2)}, u32[]{:S(2)}) collective-permute-start(bf16[128,1024]{1,0:T(8,128)(2,1)S(1)} %get-tuple-element.69), channel_id=1, source_target_pairs={{0,16},{4,20},{8,24},{12,28},{16,0},{20,4},{24,8},{28,12},{1,17},{... | collective-permute-start | bytes 786440 | tf_op jit(solution)/shard_map/ppermute | solution.py:338
  10.2 24.1 %collective-permute-start.2 = (bf16[1152,256]{1,0:T(8,128)(2,1)}, bf16[1152,256]{1,0:T(8,128)(2,1)S(1)}, u32[]{:S(2)}, u32[]{:S(2)}) collective-permute-start(bf16[1152,256]{1,0:T(8,128)(2,1)} %get-tuple-element.39.refs_2_.refs_1_), channel_id=1, source_target_pairs={{0,4},{4,0},{8,12},{12,8},{16,20},{20,16},{24,28},{28,24},{1,5},{5... | collective-permute-start | bytes 1769480 | tf_op jit(solution)/shard_map/ppermute | solution.py:365
  12.3 31.2 %collective-permute-start.3 = (bf16[1152,256]{1,0:T(8,128)(2,1)}, bf16[1152,256]{1,0:T(8,128)(2,1)S(1)}, u32[]{:S(2)}, u32[]{:S(2)}) collective-permute-start(bf16[1152,256]{1,0:T(8,128)(2,1)} %get-tuple-element.39.refs_2_.refs_1_), channel_id=1, source_target_pairs={{0,8},{4,12},{8,0},{12,4},{16,24},{20,28},{24,16},{28,20},{1,9},{5... | collective-permute-start | bytes 1769480 | tf_op jit(solution)/shard_map/ppermute | solution.py:365
  17.2 17.1 %collective-permute-start.1 = (bf16[640,256]{1,0:T(8,128)(2,1)}, bf16[640,256]{1,0:T(8,128)(2,1)S(1)}, u32[]{:S(2)}, u32[]{:S(2)}) collective-permute-start(bf16[640,256]{1,0:T(8,128)(2,1)} %get-tuple-element.42), channel_id=1, source_target_pairs={{0,16},{4,20},{8,24},{12,28},{16,0},{20,4},{24,8},{28,12},{1,17},{... | collective-permute-start | bytes 983048 | tf_op jit(solution)/shard_map/ppermute | solution.py:398
  17.2 1.1 %copy-start = (bf16[1152,256]{1,0:T(8,128)(2,1)S(1)}, bf16[1152,256]{1,0:T(8,128)(2,1)}, u32[]{:S(2)}) copy-start(bf16[1152,256]{1,0:T(8,128)(2,1)} %get-tuple-element.39.refs_2_.refs_1_) | copy-start | bytes 1769476
  34.3 16.6 %collective-permute-start.6 = (bf16[640,256]{1,0:T(8,128)(2,1)S(1)}, bf16[640,256]{1,0:T(8,128)(2,1)S(1)}, u32[]{:S(2)}, u32[]{:S(2)}) collective-permute-start(bf16[640,256]{1,0:T(8,128)(2,1)S(1)} %collective-permute-done.1.refs_4_), channel_id=1, source_target_pairs={{0,4},{4,0},{8,12},{12,8},{16,20},{20,16},{24,28},{28,24},{1,5},{5... | collective-permute-start | bytes 983048 | tf_op jit(solution)/shard_map/ppermute | solution.py:365
  35.6 15.3 %collective-permute-start.5 = (bf16[512,256]{1,0:T(8,128)(2,1)}, bf16[512,256]{1,0:T(8,128)(2,1)S(1)}, u32[]{:S(2)}, u32[]{:S(2)}) collective-permute-start(bf16[512,256]{1,0:T(8,128)(2,1)} %get-tuple-element.47), channel_id=1, source_target_pairs={{0,16},{4,20},{8,24},{12,28},{16,0},{20,4},{24,8},{28,12},{1,17},{... | collective-permute-start | bytes 786440 | tf_op jit(solution)/shard_map/ppermute | solution.py:399
  36.6 14.4 %collective-permute-start.7 = (bf16[640,256]{1,0:T(8,128)(2,1)S(1)}, bf16[640,256]{1,0:T(8,128)(2,1)S(1)}, u32[]{:S(2)}, u32[]{:S(2)}) collective-permute-start(bf16[640,256]{1,0:T(8,128)(2,1)S(1)} %collective-permute-done.1.refs_4_), channel_id=1, source_target_pairs={{0,8},{4,12},{8,0},{12,4},{16,24},{20,28},{24,16},{28,20},{1,9},{5... | collective-permute-start | bytes 983048 | tf_op jit(solution)/shard_map/ppermute | solution.py:365
  43.5 17.7 %collective-permute-start.4 = (bf16[1152,256]{1,0:T(8,128)(2,1)S(1)}, bf16[1152,256]{1,0:T(8,128)(2,1)S(1)}, u32[]{:S(2)}, u32[]{:S(2)}) collective-permute-start(bf16[1152,256]{1,0:T(8,128)(2,1)S(1)} %collective-permute-done.3.refs_3_), channel_id=1, source_target_pairs={{0,4},{4,0},{8,12},{12,8},{16,20},{20,16},{24,28},{28,24},{1,5},{5... | collective-permute-start | bytes 1769480 | tf_op jit(solution)/shard_map/ppermute | solution.py:365
  43.5 1.1 %copy-start.1 = (bf16[1152,256]{1,0:T(8,128)(2,1)S(1)}, bf16[1152,256]{1,0:T(8,128)(2,1)}, u32[]{:S(2)}) copy-start(bf16[1152,256]{1,0:T(8,128)(2,1)} %get-tuple-element.39.refs_2_.refs_1_) | copy-start | bytes 1769476
  50.9 6.4 %collective-permute-start.9 = (bf16[512,256]{1,0:T(8,128)(2,1)S(1)}, bf16[512,256]{1,0:T(8,128)(2,1)S(1)}, u32[]{:S(2)}, u32[]{:S(2)}) collective-permute-start(bf16[512,256]{1,0:T(8,128)(2,1)S(1)} %collective-permute-done.5.refs_8_), channel_id=1, source_target_pairs={{0,8},{4,12},{8,0},{12,4},{16,24},{20,28},{24,16},{28,20},{1,9},{5... | collective-permute-start | bytes 786440 | tf_op jit(solution)/shard_map/ppermute | solution.py:365
  51.0 24.6 %collective-permute-start.10 = (bf16[640,256]{1,0:T(8,128)(2,1)S(1)}, bf16[640,256]{1,0:T(8,128)(2,1)S(1)}, u32[]{:S(2)}, u32[]{:S(2)}) collective-permute-start(bf16[640,256]{1,0:T(8,128)(2,1)S(1)} %collective-permute-done.7.refs_7_), channel_id=1, source_target_pairs={{0,4},{4,0},{8,12},{12,8},{16,20},{20,16},{24,28},{28,24},{1,5},{5... | collective-permute-start | bytes 983048 | tf_op jit(solution)/shard_map/ppermute | solution.py:365
  54.9 15.2 %collective-permute-start.8 = (bf16[512,256]{1,0:T(8,128)(2,1)S(1)}, bf16[512,256]{1,0:T(8,128)(2,1)S(1)}, u32[]{:S(2)}, u32[]{:S(2)}) collective-permute-start(bf16[512,256]{1,0:T(8,128)(2,1)S(1)} %collective-permute-done.5.refs_8_), channel_id=1, source_target_pairs={{0,4},{4,0},{8,12},{12,8},{16,20},{20,16},{24,28},{28,24},{1,5},{5... | collective-permute-start | bytes 786440 | tf_op jit(solution)/shard_map/ppermute | solution.py:365
  57.3 18.3 %collective-permute-start.11 = (bf16[512,256]{1,0:T(8,128)(2,1)S(1)}, bf16[512,256]{1,0:T(8,128)(2,1)S(1)}, u32[]{:S(2)}, u32[]{:S(2)}) collective-permute-start(bf16[512,256]{1,0:T(8,128)(2,1)S(1)} %collective-permute-done.9.refs_10_), channel_id=1, source_target_pairs={{0,4},{4,0},{8,12},{12,8},{16,20},{20,16},{24,28},{28,24},{1,5},{5... | collective-permute-start | bytes 786440 | tf_op jit(solution)/shard_map/ppermute | solution.py:365
  80.0 0.6 copy-start.2
  80.6 7.8 %collective-permute-start.12 = (bf16[32,1024]{1,0:T(8,128)(2,1)S(1)}, bf16[32,1024]{1,0:T(8,128)(2,1)S(1)}, u32[]{:S(2)}, u32[]{:S(2)}) collective-permute-start(bf16[32,1024]{1,0:T(8,128)(2,1)S(1)} %get-tuple-element.62), channel_id=1, source_target_pairs={{0,16},{1,17},{2,18},{3,19},{4,20},{5,21},{6,22},{7,23},{8,24},{9,... | collective-permute-start | bytes 196616 | tf_op jit(solution)/shard_map/ppermute | solution.py:434
  83.6 5.7 %collective-permute-start.13 = (bf16[32,1024]{1,0:T(8,128)(2,1)S(1)}, bf16[32,1024]{1,0:T(8,128)(2,1)S(1)}, u32[]{:S(2)}, u32[]{:S(2)}) collective-permute-start(bf16[32,1024]{1,0:T(8,128)(2,1)S(1)} %get-tuple-element.63), channel_id=1, source_target_pairs={{0,1},{1,0},{2,3},{3,2},{4,5},{5,4},{6,7},{7,6},{8,9},{9,8},{10,11... | collective-permute-start | bytes 196616 | tf_op jit(solution)/shard_map/ppermute | solution.py:434
  83.6 8.4 %collective-permute-start.14 = (bf16[32,1024]{1,0:T(8,128)(2,1)S(1)}, bf16[32,1024]{1,0:T(8,128)(2,1)S(1)}, u32[]{:S(2)}, u32[]{:S(2)}) collective-permute-start(bf16[32,1024]{1,0:T(8,128)(2,1)S(1)} %get-tuple-element.64), channel_id=1, source_target_pairs={{0,17},{1,16},{2,19},{3,18},{4,21},{5,20},{6,23},{7,22},{8,25},{9,... | collective-permute-start | bytes 196616 | tf_op jit(solution)/shard_map/ppermute | solution.py:434
  83.7 8.2 %collective-permute-start.15 = (bf16[32,1024]{1,0:T(8,128)(2,1)S(1)}, bf16[32,1024]{1,0:T(8,128)(2,1)S(1)}, u32[]{:S(2)}, u32[]{:S(2)}) collective-permute-start(bf16[32,1024]{1,0:T(8,128)(2,1)S(1)} %get-tuple-element.65), channel_id=1, source_target_pairs={{0,2},{1,3},{2,0},{3,1},{4,6},{5,7},{6,4},{7,5},{8,10},{9,11},{10,... | collective-permute-start | bytes 196616 | tf_op jit(solution)/shard_map/ppermute | solution.py:434
  88.4 8.3 %collective-permute-start.16 = (bf16[32,1024]{1,0:T(8,128)(2,1)S(1)}, bf16[32,1024]{1,0:T(8,128)(2,1)S(1)}, u32[]{:S(2)}, u32[]{:S(2)}) collective-permute-start(bf16[32,1024]{1,0:T(8,128)(2,1)S(1)} %get-tuple-element.66), channel_id=1, source_target_pairs={{0,18},{1,19},{2,16},{3,17},{4,22},{5,23},{6,20},{7,21},{8,26},{9,... | collective-permute-start | bytes 196616 | tf_op jit(solution)/shard_map/ppermute | solution.py:434
  88.4 8.4 %copy-start.5 = (bf16[32,1024]{1,0:T(8,128)(2,1)}, bf16[32,1024]{1,0:T(8,128)(2,1)S(1)}, u32[]{:S(2)}) copy-start(bf16[32,1024]{1,0:T(8,128)(2,1)S(1)} %collective-permute-done.12.refs_1_) | copy-start | bytes 196612
  88.4 8.3 %collective-permute-start.17 = (bf16[32,1024]{1,0:T(8,128)(2,1)S(1)}, bf16[32,1024]{1,0:T(8,128)(2,1)S(1)}, u32[]{:S(2)}, u32[]{:S(2)}) collective-permute-start(bf16[32,1024]{1,0:T(8,128)(2,1)S(1)} %get-tuple-element.67), channel_id=1, source_target_pairs={{0,3},{1,2},{2,1},{3,0},{4,7},{5,6},{6,5},{7,4},{8,11},{9,10},{10,... | collective-permute-start | bytes 196616 | tf_op jit(solution)/shard_map/ppermute | solution.py:434
  89.3 7.5 %copy-start.6 = (bf16[32,1024]{1,0:T(8,128)(2,1)}, bf16[32,1024]{1,0:T(8,128)(2,1)S(1)}, u32[]{:S(2)}) copy-start(bf16[32,1024]{1,0:T(8,128)(2,1)S(1)} %collective-permute-done.13.refs_2_) | copy-start | bytes 196612
  89.3 7.5 %collective-permute-start.18 = (bf16[32,1024]{1,0:T(8,128)(2,1)S(1)}, bf16[32,1024]{1,0:T(8,128)(2,1)S(1)}, u32[]{:S(2)}, u32[]{:S(2)}) collective-permute-start(bf16[32,1024]{1,0:T(8,128)(2,1)S(1)} %get-tuple-element.68), channel_id=1, source_target_pairs={{0,19},{1,18},{2,17},{3,16},{4,23},{5,22},{6,21},{7,20},{8,27},{9,... | collective-permute-start | bytes 196616 | tf_op jit(solution)/shard_map/ppermute | solution.py:434
  91.9 4.8 %copy-start.7 = (bf16[32,1024]{1,0:T(8,128)(2,1)}, bf16[32,1024]{1,0:T(8,128)(2,1)S(1)}, u32[]{:S(2)}) copy-start(bf16[32,1024]{1,0:T(8,128)(2,1)S(1)} %collective-permute-done.14.refs_3_) | copy-start | bytes 196612
  91.9 4.8 %copy-start.8 = (bf16[32,1024]{1,0:T(8,128)(2,1)}, bf16[32,1024]{1,0:T(8,128)(2,1)S(1)}, u32[]{:S(2)}) copy-start(bf16[32,1024]{1,0:T(8,128)(2,1)S(1)} %collective-permute-done.15.refs_4_) | copy-start | bytes 196612
  96.7 0.6 copy-start.9
  96.7 0.6 copy-start.10
  96.8 0.6 copy-start.11
where the time goes:
time: 101 us; the launch traced here: 99.5 us
  starting transfers between devices  36.5 us (36%)
  Pallas kernels  32.1 us (32%)
  waiting for transfers between devices  26.1 us (26%)
  local copies, waits for them, and re-layouts  4.43 us (4%)
    pallas_call x5, Pallas kernels, attend(): pl.pallas_call(functools.partial(attend_kernel, stage), out_shape=out_sha...  25.2 us
    ppermute x9, starting transfers between devices, swap(): return lax.ppermute(x, 'ctx', [(i, i ^ bit) for i in range(owners)])  20.1 us
    ppermute x1, waiting for transfers between devices, body(): far = {0: lax.ppermute(theirs, 'ctx', across)}  13.3 us
    ppermute x7, starting transfers between devices, body(): lax.ppermute(sent[k], ('ctx', 'head'), [(d, partner(d, k)) for d in devic...  11.3 us
    pallas_call x1, Pallas kernels, body(): pl.pallas_call(functools.partial(collect_kernel, owners, cap), out_shape=...  5.04 us
    ppermute x9, waiting for transfers between devices, swap(): return lax.ppermute(x, 'ctx', [(i, i ^ bit) for i in range(owners)])  4.98 us
    ppermute x7, waiting for transfers between devices, body(): lax.ppermute(sent[k], ('ctx', 'head'), [(d, partner(d, k)) for d in devic...  4.83 us
    ppermute x1, starting transfers between devices, body(): q_far = lax.ppermute(send_q, 'ctx', across)  4.1 us
  transfers between devices with their start and end apart: 19, of which 6 were waited for; matrix products, arithmetic and copies ran while one was open for 0% of the time, Pallas kernels for 26%

commit v1 on v0

--- a/solution.py
+++ b/solution.py
@@ -392,8 +392,6 @@
             operands, scalars = [more[0]], more[1]
         return more
 
-    theirs, q_far = lax.optimization_barrier((theirs, q_far))
-    operands[1] = q_far
     near = {0: mine}
     far = {0: lax.ppermute(theirs, "ctx", across)}
     rest = {0: lax.ppermute(theirs_rest, "ctx", across)}
@@ -402,19 +400,21 @@
         near.update({m | bit: swap(x, bit) for m, x in near.items()})
     del near[0]
     forwarded = {m | last_bit: swap(x, last_bit) for m, x in near.items()}
-    stage("attend_own", (False, whole, True, {0: mine}))
-    first_far, own, state = lax.optimization_barrier((far[0], own, state))
+    first_far, own, q_far = lax.optimization_barrier((far[0], own, q_far))
+    operands[1] = q_far
     far_own = swap(first_far, last_bit)
-    rest[0], far_own = lax.optimization_barrier((rest[0], far_own))
-    stage("attend_near", (False, whole, True, {last_bit: own} | near), (True, low, True, {0: first_far}))
-    rest[0], state = lax.optimization_barrier((rest[0], state))
+    stage("attend_near", (False, whole, True, {0: mine, last_bit: own} | near))
+    rest[0], far_own, state = lax.optimization_barrier((rest[0], far_own, state))
     for bit in bits[:-1]:
         far.update({m | bit: swap(x, bit) for m, x in far.items()})
         rest.update({m | bit: swap(x, bit) for m, x in rest.items()})
     far.pop(0)
+    far, forwarded = lax.optimization_barrier((far, forwarded))
     last_far = {m | last_bit: swap(x, last_bit) for m, x in far.items()}
     rest_own = swap(rest[0], last_bit)
-    stage("attend_forwarded", (False, whole, True, forwarded), (True, low, True, {last_bit: far_own}))
+    stage(
+        "attend_forwarded", (False, whole, True, forwarded), (True, low, True, {0: first_far, last_bit: far_own})
+    )
     first_rest = rest.pop(0)
     last_rest = {m | last_bit: swap(x, last_bit) for m, x in rest.items()}
     stage(

time: 101 us -> 103 us (1.020); the launches traced: 99.5 us -> 104 us
  waiting for transfers between devices: 26.1 us -> 41.3 us
  starting transfers between devices: 36.5 us -> 29 us
  local copies, waits for them, and re-layouts: 4.43 us -> 2.33 us
    ppermute x9, waiting for transfers between devices: 4.98 us -> 29.5 us  [swap(): return lax.ppermute(x, 'ctx', [(i, i ^ bit) for i in range(owners)])]
    ppermute x1, waiting for transfers between devices: 13.3 us -> 0.01 us  [body(): far = {0: lax.ppermute(theirs, 'ctx', across)}]
    ppermute x9, starting transfers between devices: 20.1 us -> 12.8 us  [swap(): return lax.ppermute(x, 'ctx', [(i, i ^ bit) for i in range(owners)])]
    ppermute x1, starting transfers between devices: 4.1 us -> 0.54 us  [body(): q_far = lax.ppermute(send_q, 'ctx', across)]
    ppermute x1, waiting for transfers between devices: 0.01 us -> 3.52 us  [body(): rest = {0: lax.ppermute(theirs_rest, 'ctx', across)}]
    ppermute x1, starting transfers between devices: 0.01 us -> 2.45 us  [body(): far = {0: lax.ppermute(theirs, 'ctx', across)}]
    ppermute x7, starting transfers between devices: 11.3 us -> 13.3 us  [body(): lax.ppermute(sent[k], ('ctx', 'head'), [(d, partner(d, k)) for d in devic...]
    unnamed x24 -> x26, local copies, waits for them, and re-layouts: 3.37 us -> 2.3 us
  transfers between devices with their start and end apart: 19 -> 19, of which waited for: 6 -> 10; matrix products, arithmetic and copies ran while one was open for 0% -> 0% of each run, Pallas kernels for 26% -> 19%
where the time goes in v1:
time: 103 us; the launch traced here: 104 us
  waiting for transfers between devices  41.3 us (40%)
  Pallas kernels  31.5 us (31%)
  starting transfers between devices  29 us (28%)
  local copies, waits for them, and re-layouts  2.33 us (2%)
    ppermute x9, waiting for transfers between devices, swap(): return lax.ppermute(x, 'ctx', [(i, i ^ bit) for i in range(owners)])  29.5 us
    pallas_call x4, Pallas kernels, attend(): pl.pallas_call(functools.partial(attend_kernel, stage), out_shape=out_sha...  24.2 us
    ppermute x7, starting transfers between devices, body(): lax.ppermute(sent[k], ('ctx', 'head'), [(d, partner(d, k)) for d in devic...  13.3 us
    ppermute x9, starting transfers between devices, swap(): return lax.ppermute(x, 'ctx', [(i, i ^ bit) for i in range(owners)])  12.8 us
    pallas_call x1, Pallas kernels, body(): pl.pallas_call(functools.partial(collect_kernel, owners, cap), out_shape=...  5.39 us
    ppermute x7, waiting for transfers between devices, body(): lax.ppermute(sent[k], ('ctx', 'head'), [(d, partner(d, k)) for d in devic...  4.62 us
    ppermute x1, waiting for transfers between devices, body(): q_far = lax.ppermute(send_q, 'ctx', across)  3.59 us
    ppermute x1, waiting for transfers between devices, body(): rest = {0: lax.ppermute(theirs_rest, 'ctx', across)}  3.52 us
  transfers between devices with their start and end apart: 19, of which 10 were waited for; matrix products, arithmetic and copies ran while one was open for 0% of the time, Pallas kernels for 19%

profile of v1, /device:TPU:0, one launch (start us, length us, event | category | flops | bytes accessed | tf_op | source)
XLA Modules:
  0.0 104.3 jit_solution(10641584740382403977)
XLA Ops:
  0.0 0.0 copy-start.4
  0.0 0.0 copy-start.5
  0.0 0.0 copy-start.3
  0.0 5.4 %collect_slots.1 = (bf16[1152,256]{1,0:T(8,128)(2,1)}, bf16[640,256]{1,0:T(8,128)(2,1)}, bf16[512,256]{1,0:T(8,128)(2,1)}) custom-call(s32[2,64]{1,0:T(2,128)} %scalars.1, bf16[4096,2,256]{2,1,0:T(2,128)(2,1)} %cache.1, bf16[128,2,256]{2,1,0:T(2,128)(2,1)} %span.1), custom_call_target="tpu_custom_call" | custom-call | bytes 2097152 | tf_op jit(solution)/shard_map/collect_slots/pallas_call | solution.py:344
  5.4 0.0 copy-start.1
  5.4 3.0 %collective-permute-start.3 = (bf16[1152,256]{1,0:T(8,128)(2,1)}, bf16[1152,256]{1,0:T(8,128)(2,1)S(1)}, u32[]{:S(2)}, u32[]{:S(2)}) collective-permute-start(bf16[1152,256]{1,0:T(8,128)(2,1)} %get-tuple-element.34.refs_2_.refs_1_), channel_id=1, source_target_pairs={{0,8},{4,12},{8,0},{12,4},{16,24},{20,28},{24,16},{28,20},{1,9},{5... | collective-permute-start | bytes 1769480 | tf_op jit(solution)/shard_map/ppermute | solution.py:365
  8.5 1.3 %collective-permute-start.1 = (bf16[1152,256]{1,0:T(8,128)(2,1)}, bf16[1152,256]{1,0:T(8,128)(2,1)S(1)}, u32[]{:S(2)}, u32[]{:S(2)}) collective-permute-start(bf16[1152,256]{1,0:T(8,128)(2,1)} %get-tuple-element.34.refs_2_.refs_1_), channel_id=1, source_target_pairs={{0,4},{4,0},{8,12},{12,8},{16,20},{20,16},{24,28},{28,24},{1,5},{5... | collective-permute-start | bytes 1769480 | tf_op jit(solution)/shard_map/ppermute | solution.py:365
  9.8 2.4 %collective-permute-start = (bf16[640,256]{1,0:T(8,128)(2,1)}, bf16[640,256]{1,0:T(8,128)(2,1)S(1)}, u32[]{:S(2)}, u32[]{:S(2)}) collective-permute-start(bf16[640,256]{1,0:T(8,128)(2,1)} %get-tuple-element.33), channel_id=1, source_target_pairs={{0,16},{4,20},{8,24},{12,28},{16,0},{20,4},{24,8},{28,12},{1,17},{... | collective-permute-start | bytes 983048 | tf_op jit(solution)/shard_map/ppermute | solution.py:396
  12.2 0.0 copy-done.5
  12.3 0.5 collective-permute-start.2
  12.8 20.7 %collective-permute-done.3.refs_4_.refs_3_ = bf16[1152,256]{1,0:T(8,128)(2,1)S(1)} collective-permute-done((bf16[1152,256]{1,0:T(8,128)(2,1)}, bf16[1152,256]{1,0:T(8,128)(2,1)S(1)}, u32[]{:S(2)}, u32[]{:S(2)}) %collective-permute-start.3) | collective-permute-done | bytes 589856 | tf_op jit(solution)/shard_map/ppermute | solution.py:365
  33.5 1.9 %collective-permute-start.5 = (bf16[1152,256]{1,0:T(8,128)(2,1)S(1)}, bf16[1152,256]{1,0:T(8,128)(2,1)S(1)}, u32[]{:S(2)}, u32[]{:S(2)}) collective-permute-start(bf16[1152,256]{1,0:T(8,128)(2,1)S(1)} %collective-permute-done.3.refs_4_.refs_3_), channel_id=1, source_target_pairs={{0,4},{4,0},{8,12},{12,8},{16,20},{20,16},{24,28},{28,24},{1,5},{5... | collective-permute-start | bytes 1769480 | tf_op jit(solution)/shard_map/ppermute | solution.py:365
  35.4 3.6 %collective-permute-done.2.refs_1_ = bf16[128,1024]{1,0:T(8,128)(2,1)S(1)} collective-permute-done((bf16[128,1024]{1,0:T(8,128)(2,1)S(1)}, bf16[128,1024]{1,0:T(8,128)(2,1)S(1)}, u32[]{:S(2)}, u32[]{:S(2)}) %collective-permute-start.2) | collective-permute-done | bytes 262176 | tf_op jit(solution)/shard_map/ppermute | solution.py:338
  39.0 0.0 collective-permute-done.refs_5_
  39.0 0.0 collective-permute-done.1.refs_3_.refs_2_
  39.0 0.7 collective-permute-start.7
  39.7 0.0 collective-permute-start.6
  39.7 3.0 %collective-permute-start.4 = (bf16[640,256]{1,0:T(8,128)(2,1)S(1)}, bf16[640,256]{1,0:T(8,128)(2,1)S(1)}, u32[]{:S(2)}, u32[]{:S(2)}) collective-permute-start(bf16[640,256]{1,0:T(8,128)(2,1)S(1)} %collective-permute-done.refs_5_), channel_id=1, source_target_pairs={{0,8},{4,12},{8,0},{12,4},{16,24},{20,28},{24,16},{28,20},{1,9},{5... | collective-permute-start | bytes 983048 | tf_op jit(solution)/shard_map/ppermute | solution.py:365
  42.7 0.0 copy-done.4
  42.7 0.0 copy-done.3
  42.7 0.0 copy-start
  42.7 1.1 %copy-done = bf16[1152,256]{1,0:T(8,128)(2,1)S(1)} copy-done((bf16[1152,256]{1,0:T(8,128)(2,1)S(1)}, bf16[1152,256]{1,0:T(8,128)(2,1)}, u32[]{:S(2)}) %copy-start) | copy-done | bytes 589848
  43.8 6.4 %attend_near.1 = (f32[2048,128]{1,0:T(8,128)S(1)}, f32[2048,256]{1,0:T(8,128)S(1)}, bf16[2048,128]{1,0:T(8,128)(2,1)S(1)}, s32[8]{0:T(128)S(1)}) custom-call(s32[2,64]{1,0:T(2,128)S(1)} %copy-done.4, s32[2,8]{1,0:T(2,128)S(1)} %copy-done.3, bf16[128,1024]{1,0:T(8,128)(2,1)S(1)} %get-tuple-element.62.refs_0_, ...), custom_call_target="tpu_custom_call" | custom-call | flops 201326592 | bytes 786432 | tf_op jit(solution)/shard_map/attend_near/pallas_call | solution.py:294
  50.2 3.5 %collective-permute-done.6.refs_8_ = bf16[512,256]{1,0:T(8,128)(2,1)S(1)} collective-permute-done((bf16[512,256]{1,0:T(8,128)(2,1)}, bf16[512,256]{1,0:T(8,128)(2,1)S(1)}, u32[]{:S(2)}, u32[]{:S(2)}) %collective-permute-start.6) | collective-permute-done | bytes 262176 | tf_op jit(solution)/shard_map/ppermute | solution.py:397
  53.7 1.6 %collective-permute-done.7.refs_6_ = bf16[640,256]{1,0:T(8,128)(2,1)S(1)} collective-permute-done((bf16[640,256]{1,0:T(8,128)(2,1)S(1)}, bf16[640,256]{1,0:T(8,128)(2,1)S(1)}, u32[]{:S(2)}, u32[]{:S(2)}) %collective-permute-start.7) | collective-permute-done | bytes 327712 | tf_op jit(solution)/shard_map/ppermute | solution.py:365
  55.3 0.0 collective-permute-start.9
  55.3 0.0 collective-permute-done.4.refs_7_
  55.3 0.0 collective-permute-done.5.refs_4_
  55.3 1.2 %collective-permute-start.10 = (bf16[640,256]{1,0:T(8,128)(2,1)S(1)}, bf16[640,256]{1,0:T(8,128)(2,1)S(1)}, u32[]{:S(2)}, u32[]{:S(2)}) collective-permute-start(bf16[640,256]{1,0:T(8,128)(2,1)S(1)} %collective-permute-done.4.refs_7_), channel_id=1, source_target_pairs={{0,4},{4,0},{8,12},{12,8},{16,20},{20,16},{24,28},{28,24},{1,5},{5... | collective-permute-start | bytes 983048 | tf_op jit(solution)/shard_map/ppermute | solution.py:365
  56.5 0.9 collective-permute-start.8
  57.4 4.7 %collective-permute-done.9.refs_10_ = bf16[512,256]{1,0:T(8,128)(2,1)S(1)} collective-permute-done((bf16[512,256]{1,0:T(8,128)(2,1)S(1)}, bf16[512,256]{1,0:T(8,128)(2,1)S(1)}, u32[]{:S(2)}, u32[]{:S(2)}) %collective-permute-start.9) | collective-permute-done | bytes 262176 | tf_op jit(solution)/shard_map/ppermute | solution.py:365
  62.0 0.7 collective-permute-start.11
  62.8 0.0 copy-done.1
  62.8 6.3 %attend_forwarded.1 = (f32[2048,128]{1,0:T(8,128)S(1)}, f32[2048,256]{1,0:T(8,128)S(1)}) custom-call(s32[8]{0:T(128)S(1)} %get-tuple-element.37.scalars, s32[2,8]{1,0:T(2,128)S(1)} %copy-done.3, bf16[2048,128]{1,0:T(8,128)(2,1)S(1)} %get-tuple-element.38.refs_0_, bf16[1152,256]{1,0:T(8,128)(2,1)S(1)} %copy-done.1, ...), custom_call_target="tpu_custom_call", output_to_operand_aliasing={{0}: (9, {}), {1}: (10, {})} | custom-call | flops 201326592 | bytes 786432 | tf_op jit(solution)/shard_map/attend_forwarded/pallas_call | solution.py:294
  69.1 2.5 %collective-permute-done.8.refs_9_ = bf16[512,256]{1,0:T(8,128)(2,1)S(1)} collective-permute-done((bf16[512,256]{1,0:T(8,128)(2,1)S(1)}, bf16[512,256]{1,0:T(8,128)(2,1)S(1)}, u32[]{:S(2)}, u32[]{:S(2)}) %collective-permute-start.8) | collective-permute-done | bytes 262176 | tf_op jit(solution)/shard_map/ppermute | solution.py:365
  71.6 7.4 %attend_far.1 = (f32[2048,128]{1,0:T(8,128)S(1)}, f32[2048,256]{1,0:T(8,128)S(1)}) custom-call(s32[8]{0:T(128)S(1)} %get-tuple-element.37.scalars, s32[2,8]{1,0:T(2,128)S(1)} %copy-done.3, bf16[2048,128]{1,0:T(8,128)(2,1)S(1)} %get-tuple-element.38.refs_0_, bf16[1152,256]{1,0:T(8,128)(2,1)S(1)} %copy-done.1, ...), custom_call_target="tpu_custom_call", output_to_operand_aliasing={{0}: (13, {}), {1}: (14, {})} | custom-call | flops 134217728 | bytes 524288 | tf_op jit(solution)/shard_map/attend_far/pallas_call | solution.py:294
  79.0 0.0 collective-permute-done.11.refs_12_
  79.0 0.0 collective-permute-done.10.refs_11_
  79.0 4.2 %attend_last.1 = (f32[2048,128]{1,0:T(8,128)S(1)}, f32[2048,256]{1,0:T(8,128)S(1)}, bf16[32,1024]{1,0:T(8,128)(2,1)S(1)}, bf16[32,1024]{1,0:T(8,128)(2,1)S(1)}, ...) custom-call(s32[8]{0:T(128)S(1)} %get-tuple-element.37.scalars, ...), custom_call_target="tpu_custom_call", output_to_operand_aliasing={{0}: (15, {}), {1}: (16, {})} | custom-call | flops 67108864 | bytes 262144 | tf_op jit(solution)/shard_map/attend_last/pallas_call | solution.py:294
  83.2 0.0 copy-start.2
  83.2 0.6 copy-done.2
  83.8 6.3 %collective-permute-start.12 = (bf16[32,1024]{1,0:T(8,128)(2,1)S(1)}, bf16[32,1024]{1,0:T(8,128)(2,1)S(1)}, u32[]{:S(2)}, u32[]{:S(2)}) collective-permute-start(bf16[32,1024]{1,0:T(8,128)(2,1)S(1)} %get-tuple-element.54), channel_id=1, source_target_pairs={{0,16},{1,17},{2,18},{3,19},{4,20},{5,21},{6,22},{7,23},{8,24},{9,... | collective-permute-start | bytes 196616 | tf_op jit(solution)/shard_map/ppermute | solution.py:434
  90.1 0.0 collective-permute-start.13
  90.1 0.1 collective-permute-start.14
  90.3 0.7 collective-permute-start.15
  90.9 3.7 %collective-permute-start.16 = (bf16[32,1024]{1,0:T(8,128)(2,1)S(1)}, bf16[32,1024]{1,0:T(8,128)(2,1)S(1)}, u32[]{:S(2)}, u32[]{:S(2)}) collective-permute-start(bf16[32,1024]{1,0:T(8,128)(2,1)S(1)} %get-tuple-element.58), channel_id=1, source_target_pairs={{0,18},{1,19},{2,16},{3,17},{4,22},{5,23},{6,20},{7,21},{8,26},{9,... | collective-permute-start | bytes 196616 | tf_op jit(solution)/shard_map/ppermute | solution.py:434
  94.6 0.0 collective-permute-done.12.refs_1_
  94.7 0.0 collective-permute-start.17
  94.7 0.0 collective-permute-done.13.refs_2_
  94.7 0.0 copy-start.7
  94.7 2.4 %collective-permute-start.18 = (bf16[32,1024]{1,0:T(8,128)(2,1)S(1)}, bf16[32,1024]{1,0:T(8,128)(2,1)S(1)}, u32[]{:S(2)}, u32[]{:S(2)}) collective-permute-start(bf16[32,1024]{1,0:T(8,128)(2,1)S(1)} %get-tuple-element.60), channel_id=1, source_target_pairs={{0,19},{1,18},{2,17},{3,16},{4,23},{5,22},{6,21},{7,20},{8,27},{9,... | collective-permute-start | bytes 196616 | tf_op jit(solution)/shard_map/ppermute | solution.py:434
  97.1 0.6 collective-permute-done.14.refs_3_
  97.7 0.0 collective-permute-done.15.refs_4_
  97.7 0.8 collective-permute-done.16.refs_5_
  98.4 1.1 %collective-permute-done.17.refs_6_ = bf16[32,1024]{1,0:T(8,128)(2,1)S(1)} collective-permute-done((bf16[32,1024]{1,0:T(8,128)(2,1)S(1)}, bf16[32,1024]{1,0:T(8,128)(2,1)S(1)}, u32[]{:S(2)}, u32[]{:S(2)}) %collective-permute-start.17) | collective-permute-done | bytes 65568 | tf_op jit(solution)/shard_map/ppermute | solution.py:434
  99.6 2.2 %collective-permute-done.18.refs_7_ = bf16[32,1024]{1,0:T(8,128)(2,1)S(1)} collective-permute-done((bf16[32,1024]{1,0:T(8,128)(2,1)S(1)}, bf16[32,1024]{1,0:T(8,128)(2,1)S(1)}, u32[]{:S(2)}, u32[]{:S(2)}) %collective-permute-start.18) | collective-permute-done | bytes 65568 | tf_op jit(solution)/shard_map/ppermute | solution.py:434
  101.8 0.0 copy-done.6
  101.8 0.0 copy-done.7
  101.8 0.0 copy-done.8
  101.8 0.0 copy-done.9
  101.8 0.0 copy-done.10
  101.8 0.0 copy-done.11
  101.8 0.6 copy-done.12
  102.4 1.9 %place_parts.1 = bf16[32,8192]{1,0:T(8,128)(2,1)} custom-call(bf16[32,1024]{1,0:T(8,128)(2,1)} %copy-done.2, bf16[32,1024]{1,0:T(8,128)(2,1)} %copy-done.6, bf16[32,1024]{1,0:T(8,128)(2,1)} %copy-done.7, bf16[32,1024]{1,0:T(8,128)(2,1)} %copy-done.8, bf16[32,1024]{1,0:T(8,128)(2,1)} %copy-done.9, bf16[32,1024]{1,0:T(8,128)(2,1)} %copy-done.10, ...), custom_call_target="tpu_custom_call" | custom-call | tf_op jit(solution)/shard_map/place_parts/pallas_call | solution.py:435
  (7 shorter events, 0.0 us)
Async XLA Ops:
  0.0 42.7 %copy-start.4 = (s32[2,64]{1,0:T(2,128)S(1)}, s32[2,64]{1,0:T(2,128)}, u32[]{:S(2)}) copy-start(s32[2,64]{1,0:T(2,128)} %scalars.1) | copy-start | bytes 1540
  0.0 12.2 %copy-start.5 = (bf16[128,2048]{1,0:T(8,128)(2,1)S(1)}, bf16[128,2048]{1,0:T(8,128)(2,1)}, u32[]{:S(2)}) copy-start(bf16[128,2048]{1,0:T(8,128)(2,1)} %param.5) | copy-start | bytes 1572868
  0.0 42.7 %copy-start.3 = (s32[2,8]{1,0:T(2,128)S(1)}, s32[2,8]{1,0:T(2,128)}, u32[]{:S(2)}) copy-start(s32[2,8]{1,0:T(2,128)} %offsets.7) | copy-start | bytes 196
  5.4 57.4 %copy-start.1 = (bf16[1152,256]{1,0:T(8,128)(2,1)S(1)}, bf16[1152,256]{1,0:T(8,128)(2,1)}, u32[]{:S(2)}) copy-start(bf16[1152,256]{1,0:T(8,128)(2,1)} %get-tuple-element.34.refs_2_.refs_1_) | copy-start | bytes 1769476
  5.4 28.1 %collective-permute-start.3 = (bf16[1152,256]{1,0:T(8,128)(2,1)}, bf16[1152,256]{1,0:T(8,128)(2,1)S(1)}, u32[]{:S(2)}, u32[]{:S(2)}) collective-permute-start(bf16[1152,256]{1,0:T(8,128)(2,1)} %get-tuple-element.34.refs_2_.refs_1_), channel_id=1, source_target_pairs={{0,8},{4,12},{8,0},{12,4},{16,24},{20,28},{24,16},{28,20},{1,9},{5... | collective-permute-start | bytes 1769480 | tf_op jit(solution)/shard_map/ppermute | solution.py:365
  8.5 30.5 %collective-permute-start.1 = (bf16[1152,256]{1,0:T(8,128)(2,1)}, bf16[1152,256]{1,0:T(8,128)(2,1)S(1)}, u32[]{:S(2)}, u32[]{:S(2)}) collective-permute-start(bf16[1152,256]{1,0:T(8,128)(2,1)} %get-tuple-element.34.refs_2_.refs_1_), channel_id=1, source_target_pairs={{0,4},{4,0},{8,12},{12,8},{16,20},{20,16},{24,28},{28,24},{1,5},{5... | collective-permute-start | bytes 1769480 | tf_op jit(solution)/shard_map/ppermute | solution.py:365
  9.8 29.2 %collective-permute-start = (bf16[640,256]{1,0:T(8,128)(2,1)}, bf16[640,256]{1,0:T(8,128)(2,1)S(1)}, u32[]{:S(2)}, u32[]{:S(2)}) collective-permute-start(bf16[640,256]{1,0:T(8,128)(2,1)} %get-tuple-element.33), channel_id=1, source_target_pairs={{0,16},{4,20},{8,24},{12,28},{16,0},{20,4},{24,8},{28,12},{1,17},{... | collective-permute-start | bytes 983048 | tf_op jit(solution)/shard_map/ppermute | solution.py:396
  12.3 26.7 %collective-permute-start.2 = (bf16[128,1024]{1,0:T(8,128)(2,1)S(1)}, bf16[128,1024]{1,0:T(8,128)(2,1)S(1)}, u32[]{:S(2)}, u32[]{:S(2)}) collective-permute-start(bf16[128,1024]{1,0:T(8,128)(2,1)S(1)} %get-tuple-element.61), channel_id=1, source_target_pairs={{0,16},{4,20},{8,24},{12,28},{16,0},{20,4},{24,8},{28,12},{1,17},{... | collective-permute-start | bytes 786440 | tf_op jit(solution)/shard_map/ppermute | solution.py:338
  33.5 21.7 %collective-permute-start.5 = (bf16[1152,256]{1,0:T(8,128)(2,1)S(1)}, bf16[1152,256]{1,0:T(8,128)(2,1)S(1)}, u32[]{:S(2)}, u32[]{:S(2)}) collective-permute-start(bf16[1152,256]{1,0:T(8,128)(2,1)S(1)} %collective-permute-done.3.refs_4_.refs_3_), channel_id=1, source_target_pairs={{0,4},{4,0},{8,12},{12,8},{16,20},{20,16},{24,28},{28,24},{1,5},{5... | collective-permute-start | bytes 1769480 | tf_op jit(solution)/shard_map/ppermute | solution.py:365
  39.0 16.3 %collective-permute-start.7 = (bf16[640,256]{1,0:T(8,128)(2,1)S(1)}, bf16[640,256]{1,0:T(8,128)(2,1)S(1)}, u32[]{:S(2)}, u32[]{:S(2)}) collective-permute-start(bf16[640,256]{1,0:T(8,128)(2,1)S(1)} %collective-permute-done.refs_5_), channel_id=1, source_target_pairs={{0,4},{4,0},{8,12},{12,8},{16,20},{20,16},{24,28},{28,24},{1,5},{5... | collective-permute-start | bytes 983048 | tf_op jit(solution)/shard_map/ppermute | solution.py:365
  39.7 14.0 %collective-permute-start.6 = (bf16[512,256]{1,0:T(8,128)(2,1)}, bf16[512,256]{1,0:T(8,128)(2,1)S(1)}, u32[]{:S(2)}, u32[]{:S(2)}) collective-permute-start(bf16[512,256]{1,0:T(8,128)(2,1)} %get-tuple-element.41), channel_id=1, source_target_pairs={{0,16},{4,20},{8,24},{12,28},{16,0},{20,4},{24,8},{28,12},{1,17},{... | collective-permute-start | bytes 786440 | tf_op jit(solution)/shard_map/ppermute | solution.py:397
  39.7 15.6 %collective-permute-start.4 = (bf16[640,256]{1,0:T(8,128)(2,1)S(1)}, bf16[640,256]{1,0:T(8,128)(2,1)S(1)}, u32[]{:S(2)}, u32[]{:S(2)}) collective-permute-start(bf16[640,256]{1,0:T(8,128)(2,1)S(1)} %collective-permute-done.refs_5_), channel_id=1, source_target_pairs={{0,8},{4,12},{8,0},{12,4},{16,24},{20,28},{24,16},{28,20},{1,9},{5... | collective-permute-start | bytes 983048 | tf_op jit(solution)/shard_map/ppermute | solution.py:365
  42.7 1.1 %copy-start = (bf16[1152,256]{1,0:T(8,128)(2,1)S(1)}, bf16[1152,256]{1,0:T(8,128)(2,1)}, u32[]{:S(2)}) copy-start(bf16[1152,256]{1,0:T(8,128)(2,1)} %get-tuple-element.34.refs_2_.refs_1_) | copy-start | bytes 1769476
  55.3 6.8 %collective-permute-start.9 = (bf16[512,256]{1,0:T(8,128)(2,1)S(1)}, bf16[512,256]{1,0:T(8,128)(2,1)S(1)}, u32[]{:S(2)}, u32[]{:S(2)}) collective-permute-start(bf16[512,256]{1,0:T(8,128)(2,1)S(1)} %collective-permute-done.6.refs_8_), channel_id=1, source_target_pairs={{0,8},{4,12},{8,0},{12,4},{16,24},{20,28},{24,16},{28,20},{1,9},{5... | collective-permute-start | bytes 786440 | tf_op jit(solution)/shard_map/ppermute | solution.py:365
  55.3 23.7 %collective-permute-start.10 = (bf16[640,256]{1,0:T(8,128)(2,1)S(1)}, bf16[640,256]{1,0:T(8,128)(2,1)S(1)}, u32[]{:S(2)}, u32[]{:S(2)}) collective-permute-start(bf16[640,256]{1,0:T(8,128)(2,1)S(1)} %collective-permute-done.4.refs_7_), channel_id=1, source_target_pairs={{0,4},{4,0},{8,12},{12,8},{16,20},{20,16},{24,28},{28,24},{1,5},{5... | collective-permute-start | bytes 983048 | tf_op jit(solution)/shard_map/ppermute | solution.py:365
  56.5 15.1 %collective-permute-start.8 = (bf16[512,256]{1,0:T(8,128)(2,1)S(1)}, bf16[512,256]{1,0:T(8,128)(2,1)S(1)}, u32[]{:S(2)}, u32[]{:S(2)}) collective-permute-start(bf16[512,256]{1,0:T(8,128)(2,1)S(1)} %collective-permute-done.6.refs_8_), channel_id=1, source_target_pairs={{0,4},{4,0},{8,12},{12,8},{16,20},{20,16},{24,28},{28,24},{1,5},{5... | collective-permute-start | bytes 786440 | tf_op jit(solution)/shard_map/ppermute | solution.py:365
  62.0 16.9 %collective-permute-start.11 = (bf16[512,256]{1,0:T(8,128)(2,1)S(1)}, bf16[512,256]{1,0:T(8,128)(2,1)S(1)}, u32[]{:S(2)}, u32[]{:S(2)}) collective-permute-start(bf16[512,256]{1,0:T(8,128)(2,1)S(1)} %collective-permute-done.9.refs_10_), channel_id=1, source_target_pairs={{0,4},{4,0},{8,12},{12,8},{16,20},{20,16},{24,28},{28,24},{1,5},{5... | collective-permute-start | bytes 786440 | tf_op jit(solution)/shard_map/ppermute | solution.py:365
  83.2 0.6 copy-start.2
  83.8 10.8 %collective-permute-start.12 = (bf16[32,1024]{1,0:T(8,128)(2,1)S(1)}, bf16[32,1024]{1,0:T(8,128)(2,1)S(1)}, u32[]{:S(2)}, u32[]{:S(2)}) collective-permute-start(bf16[32,1024]{1,0:T(8,128)(2,1)S(1)} %get-tuple-element.54), channel_id=1, source_target_pairs={{0,16},{1,17},{2,18},{3,19},{4,20},{5,21},{6,22},{7,23},{8,24},{9,... | collective-permute-start | bytes 196616 | tf_op jit(solution)/shard_map/ppermute | solution.py:434
  90.1 4.5 %collective-permute-start.13 = (bf16[32,1024]{1,0:T(8,128)(2,1)S(1)}, bf16[32,1024]{1,0:T(8,128)(2,1)S(1)}, u32[]{:S(2)}, u32[]{:S(2)}) collective-permute-start(bf16[32,1024]{1,0:T(8,128)(2,1)S(1)} %get-tuple-element.55), channel_id=1, source_target_pairs={{0,1},{1,0},{2,3},{3,2},{4,5},{5,4},{6,7},{7,6},{8,9},{9,8},{10,11... | collective-permute-start | bytes 196616 | tf_op jit(solution)/shard_map/ppermute | solution.py:434
  90.1 7.5 %collective-permute-start.14 = (bf16[32,1024]{1,0:T(8,128)(2,1)S(1)}, bf16[32,1024]{1,0:T(8,128)(2,1)S(1)}, u32[]{:S(2)}, u32[]{:S(2)}) collective-permute-start(bf16[32,1024]{1,0:T(8,128)(2,1)S(1)} %get-tuple-element.56), channel_id=1, source_target_pairs={{0,17},{1,16},{2,19},{3,18},{4,21},{5,20},{6,23},{7,22},{8,25},{9,... | collective-permute-start | bytes 196616 | tf_op jit(solution)/shard_map/ppermute | solution.py:434
  90.3 7.4 %collective-permute-start.15 = (bf16[32,1024]{1,0:T(8,128)(2,1)S(1)}, bf16[32,1024]{1,0:T(8,128)(2,1)S(1)}, u32[]{:S(2)}, u32[]{:S(2)}) collective-permute-start(bf16[32,1024]{1,0:T(8,128)(2,1)S(1)} %get-tuple-element.57), channel_id=1, source_target_pairs={{0,2},{1,3},{2,0},{3,1},{4,6},{5,7},{6,4},{7,5},{8,10},{9,11},{10,... | collective-permute-start | bytes 196616 | tf_op jit(solution)/shard_map/ppermute | solution.py:434
  90.9 7.5 %collective-permute-start.16 = (bf16[32,1024]{1,0:T(8,128)(2,1)S(1)}, bf16[32,1024]{1,0:T(8,128)(2,1)S(1)}, u32[]{:S(2)}, u32[]{:S(2)}) collective-permute-start(bf16[32,1024]{1,0:T(8,128)(2,1)S(1)} %get-tuple-element.58), channel_id=1, source_target_pairs={{0,18},{1,19},{2,16},{3,17},{4,22},{5,23},{6,20},{7,21},{8,26},{9,... | collective-permute-start | bytes 196616 | tf_op jit(solution)/shard_map/ppermute | solution.py:434
  94.7 7.1 %copy-start.6 = (bf16[32,1024]{1,0:T(8,128)(2,1)}, bf16[32,1024]{1,0:T(8,128)(2,1)S(1)}, u32[]{:S(2)}) copy-start(bf16[32,1024]{1,0:T(8,128)(2,1)S(1)} %collective-permute-done.12.refs_1_) | copy-start | bytes 196612
  94.7 4.9 %collective-permute-start.17 = (bf16[32,1024]{1,0:T(8,128)(2,1)S(1)}, bf16[32,1024]{1,0:T(8,128)(2,1)S(1)}, u32[]{:S(2)}, u32[]{:S(2)}) collective-permute-start(bf16[32,1024]{1,0:T(8,128)(2,1)S(1)} %get-tuple-element.59), channel_id=1, source_target_pairs={{0,3},{1,2},{2,1},{3,0},{4,7},{5,6},{6,5},{7,4},{8,11},{9,10},{10,... | collective-permute-start | bytes 196616 | tf_op jit(solution)/shard_map/ppermute | solution.py:434
  94.7 7.1 %copy-start.7 = (bf16[32,1024]{1,0:T(8,128)(2,1)}, bf16[32,1024]{1,0:T(8,128)(2,1)S(1)}, u32[]{:S(2)}) copy-start(bf16[32,1024]{1,0:T(8,128)(2,1)S(1)} %collective-permute-done.13.refs_2_) | copy-start | bytes 196612
  94.7 7.1 %collective-permute-start.18 = (bf16[32,1024]{1,0:T(8,128)(2,1)S(1)}, bf16[32,1024]{1,0:T(8,128)(2,1)S(1)}, u32[]{:S(2)}, u32[]{:S(2)}) collective-permute-start(bf16[32,1024]{1,0:T(8,128)(2,1)S(1)} %get-tuple-element.60), channel_id=1, source_target_pairs={{0,19},{1,18},{2,17},{3,16},{4,23},{5,22},{6,21},{7,20},{8,27},{9,... | collective-permute-start | bytes 196616 | tf_op jit(solution)/shard_map/ppermute | solution.py:434
  97.7 4.1 %copy-start.8 = (bf16[32,1024]{1,0:T(8,128)(2,1)}, bf16[32,1024]{1,0:T(8,128)(2,1)S(1)}, u32[]{:S(2)}) copy-start(bf16[32,1024]{1,0:T(8,128)(2,1)S(1)} %collective-permute-done.14.refs_3_) | copy-start | bytes 196612
  97.7 4.1 %copy-start.9 = (bf16[32,1024]{1,0:T(8,128)(2,1)}, bf16[32,1024]{1,0:T(8,128)(2,1)S(1)}, u32[]{:S(2)}) copy-start(bf16[32,1024]{1,0:T(8,128)(2,1)S(1)} %collective-permute-done.15.refs_4_) | copy-start | bytes 196612
  98.4 3.3 %copy-start.10 = (bf16[32,1024]{1,0:T(8,128)(2,1)}, bf16[32,1024]{1,0:T(8,128)(2,1)S(1)}, u32[]{:S(2)}) copy-start(bf16[32,1024]{1,0:T(8,128)(2,1)S(1)} %collective-permute-done.16.refs_5_) | copy-start | bytes 196612
  99.6 2.2 %copy-start.11 = (bf16[32,1024]{1,0:T(8,128)(2,1)}, bf16[32,1024]{1,0:T(8,128)(2,1)S(1)}, u32[]{:S(2)}) copy-start(bf16[32,1024]{1,0:T(8,128)(2,1)S(1)} %collective-permute-done.17.refs_6_) | copy-start | bytes 196612
  101.8 0.6 copy-start.12

commit v2 on v0

--- a/solution.py
+++ b/solution.py
@@ -300,7 +300,7 @@
         input_output_aliases={len(operands) - len(state) + n: n for n in range(len(state))},
         compiler_params=pltpu.CompilerParams(vmem_limit_bytes=28 * 1024 * 1024),
         cost_estimate=pl.CostEstimate(
-            flops=2 * rows * depth * share // 4, bytes_accessed=share * 4 * depth, transcendentals=0
+            flops=8 * rows * depth * share, bytes_accessed=share * 4 * depth, transcendentals=0
         ),
         name=name,
     )(*operands)
@@ -414,14 +414,15 @@
     far.pop(0)
     last_far = {m | last_bit: swap(x, last_bit) for m, x in far.items()}
     rest_own = swap(rest[0], last_bit)
-    stage("attend_forwarded", (False, whole, True, forwarded), (True, low, True, {last_bit: far_own}))
     first_rest = rest.pop(0)
     last_rest = {m | last_bit: swap(x, last_bit) for m, x in rest.items()}
     stage(
-        "attend_far", (True, low, True, far), (True, high, False, {0: first_rest, last_bit: rest_own}),
-        (True, high, False, rest), slash=True,
+        "attend_far", (False, whole, True, forwarded), (True, low, True, {last_bit: far_own} | far),
+        (True, high, False, {0: first_rest} | rest), slash=True,
     )
-    sent = stage("attend_last", (True, low, True, last_far), (True, high, False, last_rest), last=True)
+    sent = stage(
+        "attend_last", (True, low, True, last_far), (True, high, False, {last_bit: rest_own} | last_rest), last=True
+    )
 
     def partner(device, k):
         index, lane = divmod(device, head_groups)
@@ -438,6 +439,7 @@
         in_specs=[pl.BlockSpec(memory_space=pltpu.VMEM)] * parts,
         out_specs=pl.BlockSpec(memory_space=pl.ANY),
         scratch_shapes=[pltpu.SemaphoreType.DMA((parts,))],
+        compiler_params=pltpu.CompilerParams(vmem_limit_bytes=8 * 1024 * 1024),
         name="place_parts",
     )(*[placed[k] for k in range(parts)])
 

time: 101 us -> 95.7 us (0.948); the launches traced: 99.5 us -> 95.7 us
  waiting for transfers between devices: 26.1 us -> 32.4 us
  starting transfers between devices: 36.5 us -> 31.1 us
  local copies, waits for them, and re-layouts: 4.43 us -> 2.14 us
  Pallas kernels: 32.1 us -> 29.9 us
    ppermute x9, starting transfers between devices: 20.1 us -> 11.3 us  [swap(): return lax.ppermute(x, 'ctx', [(i, i ^ bit) for i in range(owners)])]
    ppermute x1, waiting for transfers between devices: 0.01 us -> 4.33 us  [body(): rest = {0: lax.ppermute(theirs_rest, 'ctx', across)}]
    ppermute x9, waiting for transfers between devices: 4.98 us -> 9 us  [swap(): return lax.ppermute(x, 'ctx', [(i, i ^ bit) for i in range(owners)])]
    ppermute x7, starting transfers between devices: 11.3 us -> 14.1 us  [body(): lax.ppermute(sent[k], ('ctx', 'head'), [(d, partner(d, k)) for d in devic...]
    unnamed x24 -> x10, local copies, waits for them, and re-layouts: 3.37 us -> 1.08 us
    ppermute x7, waiting for transfers between devices: 4.83 us -> 3.59 us  [body(): lax.ppermute(sent[k], ('ctx', 'head'), [(d, partner(d, k)) for d in devic...]
    pallas_call x1, Pallas kernels: 1.91 us -> 0.85 us  [body(): pl.pallas_call(functools.partial(place_kernel, head_groups, half), out_sh...]
    pallas_call x5 -> x4, Pallas kernels: 25.2 us -> 24.2 us  [attend(): pl.pallas_call(functools.partial(attend_kernel, stage), out_shape=out_sha...]
  transfers between devices with their start and end apart: 19 -> 19, of which waited for: 6 -> 10; matrix products, arithmetic and copies ran while one was open for 0% -> 0% of each run, Pallas kernels for 26% -> 26%
where the time goes in v2:
time: 95.7 us
  waiting for transfers between devices  32.4 us (34%)
  starting transfers between devices  31.1 us (32%)
  Pallas kernels  29.9 us (31%)
  local copies, waits for them, and re-layouts  2.14 us (2%)
    pallas_call x4, Pallas kernels, attend(): pl.pallas_call(functools.partial(attend_kernel, stage), out_shape=out_sha...  24.2 us
    ppermute x7, starting transfers between devices, body(): lax.ppermute(sent[k], ('ctx', 'head'), [(d, partner(d, k)) for d in devic...  14.1 us
    ppermute x1, waiting for transfers between devices, body(): far = {0: lax.ppermute(theirs, 'ctx', across)}  12.5 us
    ppermute x9, starting transfers between devices, swap(): return lax.ppermute(x, 'ctx', [(i, i ^ bit) for i in range(owners)])  11.3 us
    ppermute x9, waiting for transfers between devices, swap(): return lax.ppermute(x, 'ctx', [(i, i ^ bit) for i in range(owners)])  9 us
    pallas_call x1, Pallas kernels, body(): pl.pallas_call(functools.partial(collect_kernel, owners, cap), out_shape=...  4.88 us
    ppermute x1, waiting for transfers between devices, body(): rest = {0: lax.ppermute(theirs_rest, 'ctx', across)}  4.33 us
    ppermute x1, starting transfers between devices, body(): q_far = lax.ppermute(send_q, 'ctx', across)  4.1 us
  transfers between devices with their start and end apart: 19, of which 10 were waited for; matrix products, arithmetic and copies ran while one was open for 0% of the time, Pallas kernels for 26%

profile of v2, /device:TPU:0, one launch (start us, length us, event | category | flops | bytes accessed | tf_op | source)
XLA Modules:
  0.0 95.7 jit_solution(5838172061772579875)
XLA Ops:
  0.0 1.1 %constant_dynamic-slice_fusion = (bf16[128,1024]{1,0:T(8,128)(2,1)S(1)}, bf16[128,1024]{1,0:T(8,128)(2,1)S(1)}) fusion(bf16[128,2048]{1,0:T(8,128)(2,1)} %param.5, s32[]{:T(128)S(6)} %select_n.13, s32[]{:T(128)S(6)} %select_n.12), kind=kLoop, calls=%fused_computation | loop fusion | bytes 1048584 | tf_op jit(solution)/shard_map/dynamic_slice | solution.py:336
  1.1 0.0 copy-start.2
  1.1 0.0 copy-start.3
  1.1 4.1 %collective-permute-start = (bf16[128,1024]{1,0:T(8,128)(2,1)S(1)}, bf16[128,1024]{1,0:T(8,128)(2,1)S(1)}, u32[]{:S(2)}, u32[]{:S(2)}) collective-permute-start(bf16[128,1024]{1,0:T(8,128)(2,1)S(1)} %get-tuple-element.65), channel_id=1, source_target_pairs={{0,16},{4,20},{8,24},{12,28},{16,0},{20,4},{24,8},{28,12},{1,17},{... | collective-permute-start | bytes 786440 | tf_op jit(solution)/shard_map/ppermute | solution.py:338
  5.2 4.9 %collect_slots.1 = (bf16[1152,256]{1,0:T(8,128)(2,1)}, bf16[640,256]{1,0:T(8,128)(2,1)}, bf16[512,256]{1,0:T(8,128)(2,1)}) custom-call(s32[2,64]{1,0:T(2,128)} %scalars.1, bf16[4096,2,256]{2,1,0:T(2,128)(2,1)} %cache.1, bf16[128,2,256]{2,1,0:T(2,128)(2,1)} %span.1), custom_call_target="tpu_custom_call" | custom-call | bytes 2097152 | tf_op jit(solution)/shard_map/collect_slots/pallas_call | solution.py:344
  10.1 1.9 %collective-permute-start.2 = (bf16[1152,256]{1,0:T(8,128)(2,1)}, bf16[1152,256]{1,0:T(8,128)(2,1)S(1)}, u32[]{:S(2)}, u32[]{:S(2)}) collective-permute-start(bf16[1152,256]{1,0:T(8,128)(2,1)} %get-tuple-element.37.refs_2_.refs_1_), channel_id=1, source_target_pairs={{0,4},{4,0},{8,12},{12,8},{16,20},{20,16},{24,28},{28,24},{1,5},{5... | collective-permute-start | bytes 1769480 | tf_op jit(solution)/shard_map/ppermute | solution.py:365
  12.0 2.2 %collective-permute-start.3 = (bf16[1152,256]{1,0:T(8,128)(2,1)}, bf16[1152,256]{1,0:T(8,128)(2,1)S(1)}, u32[]{:S(2)}, u32[]{:S(2)}) collective-permute-start(bf16[1152,256]{1,0:T(8,128)(2,1)} %get-tuple-element.37.refs_2_.refs_1_), channel_id=1, source_target_pairs={{0,8},{4,12},{8,0},{12,4},{16,24},{20,28},{24,16},{28,20},{1,9},{5... | collective-permute-start | bytes 1769480 | tf_op jit(solution)/shard_map/ppermute | solution.py:365
  14.2 3.0 %collective-permute-done.refs_1_ = bf16[128,1024]{1,0:T(8,128)(2,1)S(1)} collective-permute-done((bf16[128,1024]{1,0:T(8,128)(2,1)S(1)}, bf16[128,1024]{1,0:T(8,128)(2,1)S(1)}, u32[]{:S(2)}, u32[]{:S(2)}) %collective-permute-start) | collective-permute-done | bytes 262176 | tf_op jit(solution)/shard_map/ppermute | solution.py:338
  17.2 0.0 collective-permute-start.1
  17.2 0.0 copy-done.2
  17.2 0.0 copy-done.3
  17.2 0.0 copy-start
  17.2 1.1 %copy-done = bf16[1152,256]{1,0:T(8,128)(2,1)S(1)} copy-done((bf16[1152,256]{1,0:T(8,128)(2,1)S(1)}, bf16[1152,256]{1,0:T(8,128)(2,1)}, u32[]{:S(2)}) %copy-start) | copy-done | bytes 589848
  18.3 0.0 copy-start.4
  18.3 0.0 copy-start.1
  18.3 2.7 %attend_own.1 = (f32[2048,128]{1,0:T(8,128)S(1)}, f32[2048,256]{1,0:T(8,128)S(1)}, bf16[2048,128]{1,0:T(8,128)(2,1)S(1)}, s32[8]{0:T(128)S(1)}) custom-call(s32[2,64]{1,0:T(2,128)S(1)} %copy-done.2, s32[2,8]{1,0:T(2,128)S(1)} %copy-done.3, bf16[128,1024]{1,0:T(8,128)(2,1)S(1)} %get-tuple-element.66.refs_0_, ...), custom_call_target="tpu_custom_call" | custom-call | flops 1073741824 | bytes 262144 | tf_op jit(solution)/shard_map/attend_own/pallas_call | solution.py:294
  21.0 12.5 %collective-permute-done.1.refs_4_ = bf16[640,256]{1,0:T(8,128)(2,1)S(1)} collective-permute-done((bf16[640,256]{1,0:T(8,128)(2,1)}, bf16[640,256]{1,0:T(8,128)(2,1)S(1)}, u32[]{:S(2)}, u32[]{:S(2)}) %collective-permute-start.1) | collective-permute-done | bytes 327712 | tf_op jit(solution)/shard_map/ppermute | solution.py:398
  33.5 0.0 collective-permute-done.2.refs_2_
  33.5 2.0 %collective-permute-start.6 = (bf16[640,256]{1,0:T(8,128)(2,1)S(1)}, bf16[640,256]{1,0:T(8,128)(2,1)S(1)}, u32[]{:S(2)}, u32[]{:S(2)}) collective-permute-start(bf16[640,256]{1,0:T(8,128)(2,1)S(1)} %collective-permute-done.1.refs_4_), channel_id=1, source_target_pairs={{0,4},{4,0},{8,12},{12,8},{16,20},{20,16},{24,28},{28,24},{1,5},{5... | collective-permute-start | bytes 983048 | tf_op jit(solution)/shard_map/ppermute | solution.py:365
  35.6 1.2 %collective-permute-done.3.refs_3_ = bf16[1152,256]{1,0:T(8,128)(2,1)S(1)} collective-permute-done((bf16[1152,256]{1,0:T(8,128)(2,1)}, bf16[1152,256]{1,0:T(8,128)(2,1)S(1)}, u32[]{:S(2)}, u32[]{:S(2)}) %collective-permute-start.3) | collective-permute-done | bytes 589856 | tf_op jit(solution)/shard_map/ppermute | solution.py:365
  36.8 1.5 %collective-permute-start.4 = (bf16[1152,256]{1,0:T(8,128)(2,1)S(1)}, bf16[1152,256]{1,0:T(8,128)(2,1)S(1)}, u32[]{:S(2)}, u32[]{:S(2)}) collective-permute-start(bf16[1152,256]{1,0:T(8,128)(2,1)S(1)} %collective-permute-done.3.refs_3_), channel_id=1, source_target_pairs={{0,4},{4,0},{8,12},{12,8},{16,20},{20,16},{24,28},{28,24},{1,5},{5... | collective-permute-start | bytes 1769480 | tf_op jit(solution)/shard_map/ppermute | solution.py:365
  38.3 0.0 copy-done.4
  38.3 1.6 %collective-permute-start.5 = (bf16[512,256]{1,0:T(8,128)(2,1)S(1)}, bf16[512,256]{1,0:T(8,128)(2,1)S(1)}, u32[]{:S(2)}, u32[]{:S(2)}) collective-permute-start(bf16[512,256]{1,0:T(8,128)(2,1)S(1)} %copy-done.4), channel_id=1, source_target_pairs={{0,16},{4,20},{8,24},{12,28},{16,0},{20,4},{24,8},{28,12},{1,17},{... | collective-permute-start | bytes 786440 | tf_op jit(solution)/shard_map/ppermute | solution.py:399
  39.9 2.4 %collective-permute-start.7 = (bf16[640,256]{1,0:T(8,128)(2,1)S(1)}, bf16[640,256]{1,0:T(8,128)(2,1)S(1)}, u32[]{:S(2)}, u32[]{:S(2)}) collective-permute-start(bf16[640,256]{1,0:T(8,128)(2,1)S(1)} %collective-permute-done.1.refs_4_), channel_id=1, source_target_pairs={{0,8},{4,12},{8,0},{12,4},{16,24},{20,28},{24,16},{28,20},{1,9},{5... | collective-permute-start | bytes 983048 | tf_op jit(solution)/shard_map/ppermute | solution.py:365
  42.3 0.0 copy-done.1
  42.3 6.3 %attend_near.1 = (f32[2048,128]{1,0:T(8,128)S(1)}, f32[2048,256]{1,0:T(8,128)S(1)}) custom-call(s32[8]{0:T(128)S(1)} %get-tuple-element.38.scalars, s32[2,8]{1,0:T(2,128)S(1)} %copy-done.3, bf16[2048,128]{1,0:T(8,128)(2,1)S(1)} %get-tuple-element.39.refs_0_, bf16[1152,256]{1,0:T(8,128)(2,1)S(1)} %copy-done.1, ...), custom_call_target="tpu_custom_call", output_to_operand_aliasing={{0}: (7, {}), {1}: (8, {})} | custom-call | flops 3221225472 | bytes 786432 | tf_op jit(solution)/shard_map/attend_near/pallas_call | solution.py:294
  48.6 4.3 %collective-permute-done.5.refs_8_ = bf16[512,256]{1,0:T(8,128)(2,1)S(1)} collective-permute-done((bf16[512,256]{1,0:T(8,128)(2,1)S(1)}, bf16[512,256]{1,0:T(8,128)(2,1)S(1)}, u32[]{:S(2)}, u32[]{:S(2)}) %collective-permute-start.5) | collective-permute-done | bytes 262176 | tf_op jit(solution)/shard_map/ppermute | solution.py:399
  52.9 0.0 collective-permute-done.6.refs_6_
  52.9 0.0 collective-permute-start.8
  52.9 0.5 collective-permute-start.10
  53.4 1.0 %collective-permute-done.7.refs_7_ = bf16[640,256]{1,0:T(8,128)(2,1)S(1)} collective-permute-done((bf16[640,256]{1,0:T(8,128)(2,1)S(1)}, bf16[640,256]{1,0:T(8,128)(2,1)S(1)}, u32[]{:S(2)}, u32[]{:S(2)}) %collective-permute-start.7) | collective-permute-done | bytes 327712 | tf_op jit(solution)/shard_map/ppermute | solution.py:365
  54.4 0.6 collective-permute-start.9
  54.9 5.4 %collective-permute-done.8.refs_9_ = bf16[512,256]{1,0:T(8,128)(2,1)S(1)} collective-permute-done((bf16[512,256]{1,0:T(8,128)(2,1)S(1)}, bf16[512,256]{1,0:T(8,128)(2,1)S(1)}, u32[]{:S(2)}, u32[]{:S(2)}) %collective-permute-start.8) | collective-permute-done | bytes 262176 | tf_op jit(solution)/shard_map/ppermute | solution.py:365
  60.4 0.2 collective-permute-start.11
  60.6 0.0 collective-permute-done.4.refs_5_
  60.6 11.0 %attend_far.1 = (f32[2048,128]{1,0:T(8,128)S(1)}, f32[2048,256]{1,0:T(8,128)S(1)}) custom-call(s32[8]{0:T(128)S(1)} %get-tuple-element.38.scalars, s32[2,8]{1,0:T(2,128)S(1)} %copy-done.3, bf16[2048,128]{1,0:T(8,128)(2,1)S(1)} %get-tuple-element.39.refs_0_, bf16[1152,256]{1,0:T(8,128)(2,1)S(1)} %copy-done.1, ...), custom_call_target="tpu_custom_call", output_to_operand_aliasing={{0}: (12, {}), {1}: (13, {})} | custom-call | flops 4294967296 | bytes 1048576 | tf_op jit(solution)/shard_map/attend_far/pallas_call | solution.py:294
  71.6 0.0 collective-permute-done.10.refs_11_
  71.6 0.0 collective-permute-done.9.refs_10_
  71.7 1.4 %collective-permute-done.11.refs_12_ = bf16[512,256]{1,0:T(8,128)(2,1)S(1)} collective-permute-done((bf16[512,256]{1,0:T(8,128)(2,1)S(1)}, bf16[512,256]{1,0:T(8,128)(2,1)S(1)}, u32[]{:S(2)}, u32[]{:S(2)}) %collective-permute-start.11) | collective-permute-done | bytes 262176 | tf_op jit(solution)/shard_map/ppermute | solution.py:365
  73.0 4.2 %attend_last.1 = (f32[2048,128]{1,0:T(8,128)S(1)}, f32[2048,256]{1,0:T(8,128)S(1)}, bf16[32,1024]{1,0:T(8,128)(2,1)S(1)}, bf16[32,1024]{1,0:T(8,128)(2,1)S(1)}, ...) custom-call(s32[8]{0:T(128)S(1)} %get-tuple-element.38.scalars, ...), custom_call_target="tpu_custom_call", output_to_operand_aliasing={{0}: (15, {}), {1}: (16, {})} | custom-call | flops 1073741824 | bytes 262144 | tf_op jit(solution)/shard_map/attend_last/pallas_call | solution.py:294
  77.2 7.1 %collective-permute-start.12 = (bf16[32,1024]{1,0:T(8,128)(2,1)S(1)}, bf16[32,1024]{1,0:T(8,128)(2,1)S(1)}, u32[]{:S(2)}, u32[]{:S(2)}) collective-permute-start(bf16[32,1024]{1,0:T(8,128)(2,1)S(1)} %get-tuple-element.58), channel_id=1, source_target_pairs={{0,16},{1,17},{2,18},{3,19},{4,20},{5,21},{6,22},{7,23},{8,24},{9,... | collective-permute-start | bytes 196616 | tf_op jit(solution)/shard_map/ppermute | solution.py:435
  84.3 0.0 collective-permute-start.13
  84.3 0.2 collective-permute-start.14
  84.5 0.0 collective-permute-start.15
  84.5 4.3 %collective-permute-start.16 = (bf16[32,1024]{1,0:T(8,128)(2,1)S(1)}, bf16[32,1024]{1,0:T(8,128)(2,1)S(1)}, u32[]{:S(2)}, u32[]{:S(2)}) collective-permute-start(bf16[32,1024]{1,0:T(8,128)(2,1)S(1)} %get-tuple-element.62), channel_id=1, source_target_pairs={{0,18},{1,19},{2,16},{3,17},{4,22},{5,23},{6,20},{7,21},{8,26},{9,... | collective-permute-start | bytes 196616 | tf_op jit(solution)/shard_map/ppermute | solution.py:435
  88.8 0.0 collective-permute-done.12.refs_1_
  88.8 0.0 collective-permute-start.17
  88.8 0.0 collective-permute-done.13.refs_2_
  88.8 2.4 %collective-permute-start.18 = (bf16[32,1024]{1,0:T(8,128)(2,1)S(1)}, bf16[32,1024]{1,0:T(8,128)(2,1)S(1)}, u32[]{:S(2)}, u32[]{:S(2)}) collective-permute-start(bf16[32,1024]{1,0:T(8,128)(2,1)S(1)} %get-tuple-element.64), channel_id=1, source_target_pairs={{0,19},{1,18},{2,17},{3,16},{4,23},{5,22},{6,21},{7,20},{8,27},{9,... | collective-permute-start | bytes 196616 | tf_op jit(solution)/shard_map/ppermute | solution.py:435
  91.3 0.0 collective-permute-done.14.refs_3_
  91.3 0.0 collective-permute-done.15.refs_4_
  91.3 0.6 collective-permute-done.16.refs_5_
  91.8 1.0 %collective-permute-done.17.refs_6_ = bf16[32,1024]{1,0:T(8,128)(2,1)S(1)} collective-permute-done((bf16[32,1024]{1,0:T(8,128)(2,1)S(1)}, bf16[32,1024]{1,0:T(8,128)(2,1)S(1)}, u32[]{:S(2)}, u32[]{:S(2)}) %collective-permute-start.17) | collective-permute-done | bytes 65568 | tf_op jit(solution)/shard_map/ppermute | solution.py:435
  92.8 2.0 %collective-permute-done.18.refs_7_ = bf16[32,1024]{1,0:T(8,128)(2,1)S(1)} collective-permute-done((bf16[32,1024]{1,0:T(8,128)(2,1)S(1)}, bf16[32,1024]{1,0:T(8,128)(2,1)S(1)}, u32[]{:S(2)}, u32[]{:S(2)}) %collective-permute-start.18) | collective-permute-done | bytes 65568 | tf_op jit(solution)/shard_map/ppermute | solution.py:435
  94.8 0.8 place_parts.1
Async XLA Ops:
  1.1 16.2 %copy-start.2 = (s32[2,64]{1,0:T(2,128)S(1)}, s32[2,64]{1,0:T(2,128)}, u32[]{:S(2)}) copy-start(s32[2,64]{1,0:T(2,128)} %scalars.1) | copy-start | bytes 1540
  1.1 16.1 %copy-start.3 = (s32[2,8]{1,0:T(2,128)S(1)}, s32[2,8]{1,0:T(2,128)}, u32[]{:S(2)}) copy-start(s32[2,8]{1,0:T(2,128)} %offsets.7) | copy-start | bytes 196
  1.1 16.1 %collective-permute-start = (bf16[128,1024]{1,0:T(8,128)(2,1)S(1)}, bf16[128,1024]{1,0:T(8,128)(2,1)S(1)}, u32[]{:S(2)}, u32[]{:S(2)}) collective-permute-start(bf16[128,1024]{1,0:T(8,128)(2,1)S(1)} %get-tuple-element.65), channel_id=1, source_target_pairs={{0,16},{4,20},{8,24},{12,28},{16,0},{20,4},{24,8},{28,12},{1,17},{... | collective-permute-start | bytes 786440 | tf_op jit(solution)/shard_map/ppermute | solution.py:338
  10.1 23.5 %collective-permute-start.2 = (bf16[1152,256]{1,0:T(8,128)(2,1)}, bf16[1152,256]{1,0:T(8,128)(2,1)S(1)}, u32[]{:S(2)}, u32[]{:S(2)}) collective-permute-start(bf16[1152,256]{1,0:T(8,128)(2,1)} %get-tuple-element.37.refs_2_.refs_1_), channel_id=1, source_target_pairs={{0,4},{4,0},{8,12},{12,8},{16,20},{20,16},{24,28},{28,24},{1,5},{5... | collective-permute-start | bytes 1769480 | tf_op jit(solution)/shard_map/ppermute | solution.py:365
  12.0 24.8 %collective-permute-start.3 = (bf16[1152,256]{1,0:T(8,128)(2,1)}, bf16[1152,256]{1,0:T(8,128)(2,1)S(1)}, u32[]{:S(2)}, u32[]{:S(2)}) collective-permute-start(bf16[1152,256]{1,0:T(8,128)(2,1)} %get-tuple-element.37.refs_2_.refs_1_), channel_id=1, source_target_pairs={{0,8},{4,12},{8,0},{12,4},{16,24},{20,28},{24,16},{28,20},{1,9},{5... | collective-permute-start | bytes 1769480 | tf_op jit(solution)/shard_map/ppermute | solution.py:365
  17.2 16.3 %collective-permute-start.1 = (bf16[640,256]{1,0:T(8,128)(2,1)}, bf16[640,256]{1,0:T(8,128)(2,1)S(1)}, u32[]{:S(2)}, u32[]{:S(2)}) collective-permute-start(bf16[640,256]{1,0:T(8,128)(2,1)} %get-tuple-element.40), channel_id=1, source_target_pairs={{0,16},{4,20},{8,24},{12,28},{16,0},{20,4},{24,8},{28,12},{1,17},{... | collective-permute-start | bytes 983048 | tf_op jit(solution)/shard_map/ppermute | solution.py:398
  17.2 1.1 %copy-start = (bf16[1152,256]{1,0:T(8,128)(2,1)S(1)}, bf16[1152,256]{1,0:T(8,128)(2,1)}, u32[]{:S(2)}) copy-start(bf16[1152,256]{1,0:T(8,128)(2,1)} %get-tuple-element.37.refs_2_.refs_1_) | copy-start | bytes 1769476
  18.3 20.0 %copy-start.4 = (bf16[512,256]{1,0:T(8,128)(2,1)S(1)}, bf16[512,256]{1,0:T(8,128)(2,1)}, u32[]{:S(2)}) copy-start(bf16[512,256]{1,0:T(8,128)(2,1)} %get-tuple-element.45) | copy-start | bytes 786436
  18.3 24.0 %copy-start.1 = (bf16[1152,256]{1,0:T(8,128)(2,1)S(1)}, bf16[1152,256]{1,0:T(8,128)(2,1)}, u32[]{:S(2)}) copy-start(bf16[1152,256]{1,0:T(8,128)(2,1)} %get-tuple-element.37.refs_2_.refs_1_) | copy-start | bytes 1769476
  33.5 19.4 %collective-permute-start.6 = (bf16[640,256]{1,0:T(8,128)(2,1)S(1)}, bf16[640,256]{1,0:T(8,128)(2,1)S(1)}, u32[]{:S(2)}, u32[]{:S(2)}) collective-permute-start(bf16[640,256]{1,0:T(8,128)(2,1)S(1)} %collective-permute-done.1.refs_4_), channel_id=1, source_target_pairs={{0,4},{4,0},{8,12},{12,8},{16,20},{20,16},{24,28},{28,24},{1,5},{5... | collective-permute-start | bytes 983048 | tf_op jit(solution)/shard_map/ppermute | solution.py:365
  36.8 23.8 %collective-permute-start.4 = (bf16[1152,256]{1,0:T(8,128)(2,1)S(1)}, bf16[1152,256]{1,0:T(8,128)(2,1)S(1)}, u32[]{:S(2)}, u32[]{:S(2)}) collective-permute-start(bf16[1152,256]{1,0:T(8,128)(2,1)S(1)} %collective-permute-done.3.refs_3_), channel_id=1, source_target_pairs={{0,4},{4,0},{8,12},{12,8},{16,20},{20,16},{24,28},{28,24},{1,5},{5... | collective-permute-start | bytes 1769480 | tf_op jit(solution)/shard_map/ppermute | solution.py:365
  38.3 14.6 %collective-permute-start.5 = (bf16[512,256]{1,0:T(8,128)(2,1)S(1)}, bf16[512,256]{1,0:T(8,128)(2,1)S(1)}, u32[]{:S(2)}, u32[]{:S(2)}) collective-permute-start(bf16[512,256]{1,0:T(8,128)(2,1)S(1)} %copy-done.4), channel_id=1, source_target_pairs={{0,16},{4,20},{8,24},{12,28},{16,0},{20,4},{24,8},{28,12},{1,17},{... | collective-permute-start | bytes 786440 | tf_op jit(solution)/shard_map/ppermute | solution.py:399
  39.9 14.5 %collective-permute-start.7 = (bf16[640,256]{1,0:T(8,128)(2,1)S(1)}, bf16[640,256]{1,0:T(8,128)(2,1)S(1)}, u32[]{:S(2)}, u32[]{:S(2)}) collective-permute-start(bf16[640,256]{1,0:T(8,128)(2,1)S(1)} %collective-permute-done.1.refs_4_), channel_id=1, source_target_pairs={{0,8},{4,12},{8,0},{12,4},{16,24},{20,28},{24,16},{28,20},{1,9},{5... | collective-permute-start | bytes 983048 | tf_op jit(solution)/shard_map/ppermute | solution.py:365
  52.9 7.5 %collective-permute-start.8 = (bf16[512,256]{1,0:T(8,128)(2,1)S(1)}, bf16[512,256]{1,0:T(8,128)(2,1)S(1)}, u32[]{:S(2)}, u32[]{:S(2)}) collective-permute-start(bf16[512,256]{1,0:T(8,128)(2,1)S(1)} %collective-permute-done.5.refs_8_), channel_id=1, source_target_pairs={{0,8},{4,12},{8,0},{12,4},{16,24},{20,28},{24,16},{28,20},{1,9},{5... | collective-permute-start | bytes 786440 | tf_op jit(solution)/shard_map/ppermute | solution.py:365
  52.9 18.7 %collective-permute-start.10 = (bf16[512,256]{1,0:T(8,128)(2,1)S(1)}, bf16[512,256]{1,0:T(8,128)(2,1)S(1)}, u32[]{:S(2)}, u32[]{:S(2)}) collective-permute-start(bf16[512,256]{1,0:T(8,128)(2,1)S(1)} %collective-permute-done.5.refs_8_), channel_id=1, source_target_pairs={{0,4},{4,0},{8,12},{12,8},{16,20},{20,16},{24,28},{28,24},{1,5},{5... | collective-permute-start | bytes 786440 | tf_op jit(solution)/shard_map/ppermute | solution.py:365
  54.4 17.3 %collective-permute-start.9 = (bf16[640,256]{1,0:T(8,128)(2,1)S(1)}, bf16[640,256]{1,0:T(8,128)(2,1)S(1)}, u32[]{:S(2)}, u32[]{:S(2)}) collective-permute-start(bf16[640,256]{1,0:T(8,128)(2,1)S(1)} %collective-permute-done.7.refs_7_), channel_id=1, source_target_pairs={{0,4},{4,0},{8,12},{12,8},{16,20},{20,16},{24,28},{28,24},{1,5},{5... | collective-permute-start | bytes 983048 | tf_op jit(solution)/shard_map/ppermute | solution.py:365
  60.4 12.6 %collective-permute-start.11 = (bf16[512,256]{1,0:T(8,128)(2,1)S(1)}, bf16[512,256]{1,0:T(8,128)(2,1)S(1)}, u32[]{:S(2)}, u32[]{:S(2)}) collective-permute-start(bf16[512,256]{1,0:T(8,128)(2,1)S(1)} %collective-permute-done.8.refs_9_), channel_id=1, source_target_pairs={{0,4},{4,0},{8,12},{12,8},{16,20},{20,16},{24,28},{28,24},{1,5},{5... | collective-permute-start | bytes 786440 | tf_op jit(solution)/shard_map/ppermute | solution.py:365
  77.2 11.6 %collective-permute-start.12 = (bf16[32,1024]{1,0:T(8,128)(2,1)S(1)}, bf16[32,1024]{1,0:T(8,128)(2,1)S(1)}, u32[]{:S(2)}, u32[]{:S(2)}) collective-permute-start(bf16[32,1024]{1,0:T(8,128)(2,1)S(1)} %get-tuple-element.58), channel_id=1, source_target_pairs={{0,16},{1,17},{2,18},{3,19},{4,20},{5,21},{6,22},{7,23},{8,24},{9,... | collective-permute-start | bytes 196616 | tf_op jit(solution)/shard_map/ppermute | solution.py:435
  84.3 4.5 %collective-permute-start.13 = (bf16[32,1024]{1,0:T(8,128)(2,1)S(1)}, bf16[32,1024]{1,0:T(8,128)(2,1)S(1)}, u32[]{:S(2)}, u32[]{:S(2)}) collective-permute-start(bf16[32,1024]{1,0:T(8,128)(2,1)S(1)} %get-tuple-element.59), channel_id=1, source_target_pairs={{0,1},{1,0},{2,3},{3,2},{4,5},{5,4},{6,7},{7,6},{8,9},{9,8},{10,11... | collective-permute-start | bytes 196616 | tf_op jit(solution)/shard_map/ppermute | solution.py:435
  84.3 7.0 %collective-permute-start.14 = (bf16[32,1024]{1,0:T(8,128)(2,1)S(1)}, bf16[32,1024]{1,0:T(8,128)(2,1)S(1)}, u32[]{:S(2)}, u32[]{:S(2)}) collective-permute-start(bf16[32,1024]{1,0:T(8,128)(2,1)S(1)} %get-tuple-element.60), channel_id=1, source_target_pairs={{0,17},{1,16},{2,19},{3,18},{4,21},{5,20},{6,23},{7,22},{8,25},{9,... | collective-permute-start | bytes 196616 | tf_op jit(solution)/shard_map/ppermute | solution.py:435
  84.5 6.8 %collective-permute-start.15 = (bf16[32,1024]{1,0:T(8,128)(2,1)S(1)}, bf16[32,1024]{1,0:T(8,128)(2,1)S(1)}, u32[]{:S(2)}, u32[]{:S(2)}) collective-permute-start(bf16[32,1024]{1,0:T(8,128)(2,1)S(1)} %get-tuple-element.61), channel_id=1, source_target_pairs={{0,2},{1,3},{2,0},{3,1},{4,6},{5,7},{6,4},{7,5},{8,10},{9,11},{10,... | collective-permute-start | bytes 196616 | tf_op jit(solution)/shard_map/ppermute | solution.py:435
  84.5 7.3 %collective-permute-start.16 = (bf16[32,1024]{1,0:T(8,128)(2,1)S(1)}, bf16[32,1024]{1,0:T(8,128)(2,1)S(1)}, u32[]{:S(2)}, u32[]{:S(2)}) collective-permute-start(bf16[32,1024]{1,0:T(8,128)(2,1)S(1)} %get-tuple-element.62), channel_id=1, source_target_pairs={{0,18},{1,19},{2,16},{3,17},{4,22},{5,23},{6,20},{7,21},{8,26},{9,... | collective-permute-start | bytes 196616 | tf_op jit(solution)/shard_map/ppermute | solution.py:435
  88.8 4.0 %collective-permute-start.17 = (bf16[32,1024]{1,0:T(8,128)(2,1)S(1)}, bf16[32,1024]{1,0:T(8,128)(2,1)S(1)}, u32[]{:S(2)}, u32[]{:S(2)}) collective-permute-start(bf16[32,1024]{1,0:T(8,128)(2,1)S(1)} %get-tuple-element.63), channel_id=1, source_target_pairs={{0,3},{1,2},{2,1},{3,0},{4,7},{5,6},{6,5},{7,4},{8,11},{9,10},{10,... | collective-permute-start | bytes 196616 | tf_op jit(solution)/shard_map/ppermute | solution.py:435
  88.8 6.0 %collective-permute-start.18 = (bf16[32,1024]{1,0:T(8,128)(2,1)S(1)}, bf16[32,1024]{1,0:T(8,128)(2,1)S(1)}, u32[]{:S(2)}, u32[]{:S(2)}) collective-permute-start(bf16[32,1024]{1,0:T(8,128)(2,1)S(1)} %get-tuple-element.64), channel_id=1, source_target_pairs={{0,19},{1,18},{2,17},{3,16},{4,23},{5,22},{6,21},{7,20},{8,27},{9,... | collective-permute-start | bytes 196616 | tf_op jit(solution)/shard_map/ppermute | solution.py:435

commit v3 on v2

--- a/solution.py
+++ b/solution.py
@@ -60,16 +60,15 @@
 
 
 class Stage:
-    def __init__(self, owners, group, depth, tokens, width, parts, pieces, known, late, first, last):
+    def __init__(self, owners, group, depth, tokens, width, parts, pieces, known, late, first, slash, tail, last):
         self.owners, self.group, self.depth = owners, group, depth
         self.tokens, self.width, self.parts = tokens, width, parts
         self.pieces, self.known, self.late = pieces, known, late
-        self.first, self.last = first, last
+        self.first, self.slash, self.tail, self.last = first, slash, tail, last
         self.half = owners // 2
         self.blocks = tokens // BLK
         self.rows = group * BLK
         self.state_rows = 2 * self.blocks * self.rows
-        self.slash = bool(late) and not last
 
     def owner(self, far, m, *_):
         me = lax.axis_index("ctx")
@@ -142,11 +141,11 @@
         place = place + live
 
     span_copies = []
-    if stage.slash or stage.last:
+    if stage.slash or stage.tail:
         span, bias, span_sem = take(3)
-        wanted = stage.late if stage.last else [piece for piece in stage.pieces if piece[3]]
+        wanted = stage.late if stage.tail else [piece for piece in stage.pieces if piece[3]]
         for n, piece in enumerate(wanted):
-            at = n if stage.last else stage.owner(*piece)
+            at = n if stage.tail else stage.owner(*piece)
             slots = piece[2][1] - piece[2][0]
             copy = pltpu.make_async_copy(
                 sources[stage.pieces.index(piece)].at[pl.ds(slots * BLK, tokens)],
@@ -282,7 +281,7 @@
             pltpu.VMEM((2 * blocks, keys, 3 * depth), kind),
         ]
         share += keys
-    elif stage.last:
+    elif stage.tail:
         keys = len(stage.late) * stage.tokens
         scratch += [
             pltpu.VMEM((keys, 3 * depth), kind),
@@ -300,7 +299,7 @@
         input_output_aliases={len(operands) - len(state) + n: n for n in range(len(state))},
         compiler_params=pltpu.CompilerParams(vmem_limit_bytes=28 * 1024 * 1024),
         cost_estimate=pl.CostEstimate(
-            flops=8 * rows * depth * share, bytes_accessed=share * 4 * depth, transcendentals=0
+            flops=2 * rows * depth * share, bytes_accessed=share * 4 * depth, transcendentals=0
         ),
         name=name,
     )(*operands)
@@ -376,7 +375,7 @@
     places, values = [], []
     state, operands, scalars = [], [q_near, q_far], verticals
 
-    def stage(name, *arrived, slash=False, last=False):
+    def stage(name, *arrived, slash=False, late_span=False, last=False):
         nonlocal state, operands, scalars
         known, first = len(places), not places
         for far_side, slots, tail, sides in arrived:
@@ -384,7 +383,7 @@
             values.extend(sides.values())
         kind = Stage(
             owners, group, depth, tokens, cache_blocks, parts, list(places), known,
-            late if slash or last else [], first, last,
+            late if slash or late_span else [], first, slash, late_span, last,
         )
         top, acc, *more = attend(kind, scalars, offsets, operands, values, state, name)
         state = [top, acc]
@@ -420,9 +419,8 @@
         "attend_far", (False, whole, True, forwarded), (True, low, True, {last_bit: far_own} | far),
         (True, high, False, {0: first_rest} | rest), slash=True,
     )
-    sent = stage(
-        "attend_last", (True, low, True, last_far), (True, high, False, {last_bit: rest_own} | last_rest), last=True
-    )
+    stage("attend_tail", (True, low, True, last_far), (True, high, False, {last_bit: rest_own}), late_span=True)
+    sent = stage("attend_last", (True, high, False, last_rest), last=True)
 
     def partner(device, k):
         index, lane = divmod(device, head_groups)

time: 95.7 us -> 93.1 us (0.973)
  starting transfers between devices: 31.1 us -> 25.3 us
  local copies, waits for them, and re-layouts: 2.14 us -> 3.2 us
  Pallas kernels: 29.9 us -> 30.9 us
    ppermute x7, starting transfers between devices: 14.1 us -> 9.33 us  [body(): lax.ppermute(sent[k], ('ctx', 'head'), [(d, partner(d, k)) for d in devic...]
    ppermute x1, waiting for transfers between devices: 4.33 us -> 0.01 us  [body(): rest = {0: lax.ppermute(theirs_rest, 'ctx', across)}]
    ppermute x7, waiting for transfers between devices: 3.59 us -> 6.47 us  [body(): lax.ppermute(sent[k], ('ctx', 'head'), [(d, partner(d, k)) for d in devic...]
    ppermute x9, waiting for transfers between devices: 9 us -> 11 us  [swap(): return lax.ppermute(x, 'ctx', [(i, i ^ bit) for i in range(owners)])]
    pallas_call x4 -> x5, Pallas kernels: 24.2 us -> 25.3 us  [attend(): pl.pallas_call(functools.partial(attend_kernel, stage), out_shape=out_sha...]
    unnamed x10 -> x8, local copies, waits for them, and re-layouts: 1.08 us -> 2.13 us
  transfers between devices with their start and end apart: 19 -> 19, of which waited for: 10 -> 7; matrix products, arithmetic and copies ran while one was open for 0% -> 0% of each run, Pallas kernels for 26% -> 31%
where the time goes in v3:
time: 93.1 us; the launch traced here: 92.5 us
  waiting for transfers between devices  32.8 us (35%)
  Pallas kernels  30.9 us (33%)
  starting transfers between devices  25.3 us (27%)
  local copies, waits for them, and re-layouts  3.2 us (3%)
    pallas_call x5, Pallas kernels, attend(): pl.pallas_call(functools.partial(attend_kernel, stage), out_shape=out_sha...  25.3 us
    ppermute x1, waiting for transfers between devices, body(): far = {0: lax.ppermute(theirs, 'ctx', across)}  11.7 us
    ppermute x9, waiting for transfers between devices, swap(): return lax.ppermute(x, 'ctx', [(i, i ^ bit) for i in range(owners)])  11 us
    ppermute x9, starting transfers between devices, swap(): return lax.ppermute(x, 'ctx', [(i, i ^ bit) for i in range(owners)])  10.8 us
    ppermute x7, starting transfers between devices, body(): lax.ppermute(sent[k], ('ctx', 'head'), [(d, partner(d, k)) for d in devic...  9.33 us
    ppermute x7, waiting for transfers between devices, body(): lax.ppermute(sent[k], ('ctx', 'head'), [(d, partner(d, k)) for d in devic...  6.47 us
    pallas_call x1, Pallas kernels, body(): pl.pallas_call(functools.partial(collect_kernel, owners, cap), out_shape=...  4.71 us
    ppermute x1, starting transfers between devices, body(): q_far = lax.ppermute(send_q, 'ctx', across)  4.1 us
  transfers between devices with their start and end apart: 19, of which 7 were waited for; matrix products, arithmetic and copies ran while one was open for 0% of the time, Pallas kernels for 31%

profile of v3, /device:TPU:0, one launch (start us, length us, event | category | flops | bytes accessed | tf_op | source)
XLA Modules:
  0.0 92.5 jit_solution(16678992782845475299)
XLA Ops:
  0.0 1.1 %constant_dynamic-slice_fusion = (bf16[128,1024]{1,0:T(8,128)(2,1)S(1)}, bf16[128,1024]{1,0:T(8,128)(2,1)S(1)}) fusion(bf16[128,2048]{1,0:T(8,128)(2,1)} %param.5, s32[]{:T(128)S(6)} %select_n.13, s32[]{:T(128)S(6)} %select_n.12), kind=kLoop, calls=%fused_computation | loop fusion | bytes 1048584 | tf_op jit(solution)/shard_map/dynamic_slice | solution.py:335
  1.1 0.0 copy-start.2
  1.1 0.0 copy-start.3
  1.1 4.1 %collective-permute-start = (bf16[128,1024]{1,0:T(8,128)(2,1)S(1)}, bf16[128,1024]{1,0:T(8,128)(2,1)S(1)}, u32[]{:S(2)}, u32[]{:S(2)}) collective-permute-start(bf16[128,1024]{1,0:T(8,128)(2,1)S(1)} %get-tuple-element.69), channel_id=1, source_target_pairs={{0,16},{4,20},{8,24},{12,28},{16,0},{20,4},{24,8},{28,12},{1,17},{... | collective-permute-start | bytes 786440 | tf_op jit(solution)/shard_map/ppermute | solution.py:337
  5.2 4.7 %collect_slots.1 = (bf16[1152,256]{1,0:T(8,128)(2,1)}, bf16[640,256]{1,0:T(8,128)(2,1)}, bf16[512,256]{1,0:T(8,128)(2,1)}) custom-call(s32[2,64]{1,0:T(2,128)} %scalars.1, bf16[4096,2,256]{2,1,0:T(2,128)(2,1)} %cache.1, bf16[128,2,256]{2,1,0:T(2,128)(2,1)} %span.1), custom_call_target="tpu_custom_call" | custom-call | bytes 2097152 | tf_op jit(solution)/shard_map/collect_slots/pallas_call | solution.py:343
  9.9 1.8 %collective-permute-start.2 = (bf16[1152,256]{1,0:T(8,128)(2,1)}, bf16[1152,256]{1,0:T(8,128)(2,1)S(1)}, u32[]{:S(2)}, u32[]{:S(2)}) collective-permute-start(bf16[1152,256]{1,0:T(8,128)(2,1)} %get-tuple-element.39.refs_2_.refs_1_), channel_id=1, source_target_pairs={{0,4},{4,0},{8,12},{12,8},{16,20},{20,16},{24,28},{28,24},{1,5},{5... | collective-permute-start | bytes 1769480 | tf_op jit(solution)/shard_map/ppermute | solution.py:364
  11.7 1.9 %collective-permute-start.3 = (bf16[1152,256]{1,0:T(8,128)(2,1)}, bf16[1152,256]{1,0:T(8,128)(2,1)S(1)}, u32[]{:S(2)}, u32[]{:S(2)}) collective-permute-start(bf16[1152,256]{1,0:T(8,128)(2,1)} %get-tuple-element.39.refs_2_.refs_1_), channel_id=1, source_target_pairs={{0,8},{4,12},{8,0},{12,4},{16,24},{20,28},{24,16},{28,20},{1,9},{5... | collective-permute-start | bytes 1769480 | tf_op jit(solution)/shard_map/ppermute | solution.py:364
  13.6 3.6 %collective-permute-done.refs_1_ = bf16[128,1024]{1,0:T(8,128)(2,1)S(1)} collective-permute-done((bf16[128,1024]{1,0:T(8,128)(2,1)S(1)}, bf16[128,1024]{1,0:T(8,128)(2,1)S(1)}, u32[]{:S(2)}, u32[]{:S(2)}) %collective-permute-start) | collective-permute-done | bytes 262176 | tf_op jit(solution)/shard_map/ppermute | solution.py:337
  17.2 0.0 collective-permute-start.1
  17.2 0.0 copy-done.2
  17.2 0.0 copy-done.3
  17.2 0.0 copy-start
  17.2 1.1 %copy-done = bf16[1152,256]{1,0:T(8,128)(2,1)S(1)} copy-done((bf16[1152,256]{1,0:T(8,128)(2,1)S(1)}, bf16[1152,256]{1,0:T(8,128)(2,1)}, u32[]{:S(2)}) %copy-start) | copy-done | bytes 589848
  18.3 2.7 %attend_own.1 = (f32[2048,128]{1,0:T(8,128)S(1)}, f32[2048,256]{1,0:T(8,128)S(1)}, bf16[2048,128]{1,0:T(8,128)(2,1)S(1)}, s32[8]{0:T(128)S(1)}) custom-call(s32[2,64]{1,0:T(2,128)S(1)} %copy-done.3, s32[2,8]{1,0:T(2,128)S(1)} %copy-done.2, bf16[128,1024]{1,0:T(8,128)(2,1)S(1)} %get-tuple-element.70.refs_0_, ...), custom_call_target="tpu_custom_call" | custom-call | flops 268435456 | bytes 262144 | tf_op jit(solution)/shard_map/attend_own/pallas_call | solution.py:293
  21.0 11.7 %collective-permute-done.1.refs_4_ = bf16[640,256]{1,0:T(8,128)(2,1)S(1)} collective-permute-done((bf16[640,256]{1,0:T(8,128)(2,1)}, bf16[640,256]{1,0:T(8,128)(2,1)S(1)}, u32[]{:S(2)}, u32[]{:S(2)}) %collective-permute-start.1) | collective-permute-done | bytes 327712 | tf_op jit(solution)/shard_map/ppermute | solution.py:397
  32.7 0.0 collective-permute-done.2.refs_2_
  32.7 2.9 %collective-permute-start.6 = (bf16[640,256]{1,0:T(8,128)(2,1)S(1)}, bf16[640,256]{1,0:T(8,128)(2,1)S(1)}, u32[]{:S(2)}, u32[]{:S(2)}) collective-permute-start(bf16[640,256]{1,0:T(8,128)(2,1)S(1)} %collective-permute-done.1.refs_4_), channel_id=1, source_target_pairs={{0,4},{4,0},{8,12},{12,8},{16,20},{20,16},{24,28},{28,24},{1,5},{5... | collective-permute-start | bytes 983048 | tf_op jit(solution)/shard_map/ppermute | solution.py:364
  35.6 1.1 %collective-permute-start.5 = (bf16[512,256]{1,0:T(8,128)(2,1)}, bf16[512,256]{1,0:T(8,128)(2,1)S(1)}, u32[]{:S(2)}, u32[]{:S(2)}) collective-permute-start(bf16[512,256]{1,0:T(8,128)(2,1)} %get-tuple-element.47), channel_id=1, source_target_pairs={{0,16},{4,20},{8,24},{12,28},{16,0},{20,4},{24,8},{28,12},{1,17},{... | collective-permute-start | bytes 786440 | tf_op jit(solution)/shard_map/ppermute | solution.py:398
  36.7 2.9 %collective-permute-done.3.refs_3_ = bf16[1152,256]{1,0:T(8,128)(2,1)S(1)} collective-permute-done((bf16[1152,256]{1,0:T(8,128)(2,1)}, bf16[1152,256]{1,0:T(8,128)(2,1)S(1)}, u32[]{:S(2)}, u32[]{:S(2)}) %collective-permute-start.3) | collective-permute-done | bytes 589856 | tf_op jit(solution)/shard_map/ppermute | solution.py:364
  39.6 1.8 %collective-permute-start.4 = (bf16[1152,256]{1,0:T(8,128)(2,1)S(1)}, bf16[1152,256]{1,0:T(8,128)(2,1)S(1)}, u32[]{:S(2)}, u32[]{:S(2)}) collective-permute-start(bf16[1152,256]{1,0:T(8,128)(2,1)S(1)} %collective-permute-done.3.refs_3_), channel_id=1, source_target_pairs={{0,4},{4,0},{8,12},{12,8},{16,20},{20,16},{24,28},{28,24},{1,5},{5... | collective-permute-start | bytes 1769480 | tf_op jit(solution)/shard_map/ppermute | solution.py:364
  41.4 0.0 collective-permute-start.7
  41.4 0.0 copy-start.1
  41.4 1.1 %copy-done.1 = bf16[1152,256]{1,0:T(8,128)(2,1)S(1)} copy-done((bf16[1152,256]{1,0:T(8,128)(2,1)S(1)}, bf16[1152,256]{1,0:T(8,128)(2,1)}, u32[]{:S(2)}) %copy-start.1) | copy-done | bytes 589848
  42.5 6.3 %attend_near.1 = (f32[2048,128]{1,0:T(8,128)S(1)}, f32[2048,256]{1,0:T(8,128)S(1)}) custom-call(s32[8]{0:T(128)S(1)} %get-tuple-element.40.scalars, s32[2,8]{1,0:T(2,128)S(1)} %copy-done.2, bf16[2048,128]{1,0:T(8,128)(2,1)S(1)} %get-tuple-element.41.refs_0_, bf16[1152,256]{1,0:T(8,128)(2,1)S(1)} %copy-done.1, ...), custom_call_target="tpu_custom_call", output_to_operand_aliasing={{0}: (7, {}), {1}: (8, {})} | custom-call | flops 805306368 | bytes 786432 | tf_op jit(solution)/shard_map/attend_near/pallas_call | solution.py:293
  48.8 0.0 collective-permute-done.5.refs_8_
  48.8 0.0 collective-permute-done.6.refs_6_
  48.8 0.3 collective-permute-start.8
  49.1 4.9 %collective-permute-done.7.refs_7_ = bf16[640,256]{1,0:T(8,128)(2,1)S(1)} collective-permute-done((bf16[640,256]{1,0:T(8,128)(2,1)S(1)}, bf16[640,256]{1,0:T(8,128)(2,1)S(1)}, u32[]{:S(2)}, u32[]{:S(2)}) %collective-permute-start.7) | collective-permute-done | bytes 327712 | tf_op jit(solution)/shard_map/ppermute | solution.py:364
  53.9 0.3 collective-permute-start.9
  54.3 1.7 %collective-permute-start.10 = (bf16[512,256]{1,0:T(8,128)(2,1)S(1)}, bf16[512,256]{1,0:T(8,128)(2,1)S(1)}, u32[]{:S(2)}, u32[]{:S(2)}) collective-permute-start(bf16[512,256]{1,0:T(8,128)(2,1)S(1)} %collective-permute-done.5.refs_8_), channel_id=1, source_target_pairs={{0,4},{4,0},{8,12},{12,8},{16,20},{20,16},{24,28},{28,24},{1,5},{5... | collective-permute-start | bytes 786440 | tf_op jit(solution)/shard_map/ppermute | solution.py:364
  56.0 3.2 %collective-permute-done.8.refs_9_ = bf16[512,256]{1,0:T(8,128)(2,1)S(1)} collective-permute-done((bf16[512,256]{1,0:T(8,128)(2,1)S(1)}, bf16[512,256]{1,0:T(8,128)(2,1)S(1)}, u32[]{:S(2)}, u32[]{:S(2)}) %collective-permute-start.8) | collective-permute-done | bytes 262176 | tf_op jit(solution)/shard_map/ppermute | solution.py:364
  59.1 0.1 collective-permute-start.11
  59.2 0.0 collective-permute-done.4.refs_5_
  59.2 11.0 %attend_far.1 = (f32[2048,128]{1,0:T(8,128)S(1)}, f32[2048,256]{1,0:T(8,128)S(1)}) custom-call(s32[8]{0:T(128)S(1)} %get-tuple-element.40.scalars, s32[2,8]{1,0:T(2,128)S(1)} %copy-done.2, bf16[2048,128]{1,0:T(8,128)(2,1)S(1)} %get-tuple-element.41.refs_0_, bf16[1152,256]{1,0:T(8,128)(2,1)S(1)} %copy-done.1, ...), custom_call_target="tpu_custom_call", output_to_operand_aliasing={{0}: (12, {}), {1}: (13, {})} | custom-call | flops 1073741824 | bytes 1048576 | tf_op jit(solution)/shard_map/attend_far/pallas_call | solution.py:293
  70.3 0.0 collective-permute-done.10.refs_11_
  70.3 0.0 collective-permute-done.9.refs_10_
  70.3 4.2 %attend_tail.1 = (f32[2048,128]{1,0:T(8,128)S(1)}, f32[2048,256]{1,0:T(8,128)S(1)}) custom-call(s32[8]{0:T(128)S(1)} %get-tuple-element.40.scalars, s32[2,8]{1,0:T(2,128)S(1)} %copy-done.2, bf16[2048,128]{1,0:T(8,128)(2,1)S(1)} %get-tuple-element.41.refs_0_, bf16[1152,256]{1,0:T(8,128)(2,1)S(1)} %copy-done.1, ...), custom_call_target="tpu_custom_call", output_to_operand_aliasing={{0}: (14, {}), {1}: (15, {})} | custom-call | flops 268435456 | bytes 262144 | tf_op jit(solution)/shard_map/attend_tail/pallas_call | solution.py:293
  74.5 0.0 collective-permute-done.11.refs_12_
  74.5 1.1 %attend_last.1 = (f32[2048,128]{1,0:T(8,128)S(1)}, f32[2048,256]{1,0:T(8,128)S(1)}, bf16[32,1024]{1,0:T(8,128)(2,1)S(1)}, bf16[32,1024]{1,0:T(8,128)(2,1)S(1)}, ...) custom-call(s32[8]{0:T(128)S(1)} %get-tuple-element.40.scalars, ...), custom_call_target="tpu_custom_call", output_to_operand_aliasing={{0}: (15, {}), {1}: (16, {})} | custom-call | tf_op jit(solution)/shard_map/attend_last/pallas_call | solution.py:293
  75.6 1.4 %collective-permute-start.12 = (bf16[32,1024]{1,0:T(8,128)(2,1)S(1)}, bf16[32,1024]{1,0:T(8,128)(2,1)S(1)}, u32[]{:S(2)}, u32[]{:S(2)}) collective-permute-start(bf16[32,1024]{1,0:T(8,128)(2,1)S(1)} %get-tuple-element.62), channel_id=1, source_target_pairs={{0,16},{1,17},{2,18},{3,19},{4,20},{5,21},{6,22},{7,23},{8,24},{9,... | collective-permute-start | bytes 196616 | tf_op jit(solution)/shard_map/ppermute | solution.py:433
  77.0 0.0 collective-permute-start.13
  77.0 1.7 %collective-permute-start.14 = (bf16[32,1024]{1,0:T(8,128)(2,1)S(1)}, bf16[32,1024]{1,0:T(8,128)(2,1)S(1)}, u32[]{:S(2)}, u32[]{:S(2)}) collective-permute-start(bf16[32,1024]{1,0:T(8,128)(2,1)S(1)} %get-tuple-element.64), channel_id=1, source_target_pairs={{0,17},{1,16},{2,19},{3,18},{4,21},{5,20},{6,23},{7,22},{8,25},{9,... | collective-permute-start | bytes 196616 | tf_op jit(solution)/shard_map/ppermute | solution.py:433
  78.7 2.2 %collective-permute-start.15 = (bf16[32,1024]{1,0:T(8,128)(2,1)S(1)}, bf16[32,1024]{1,0:T(8,128)(2,1)S(1)}, u32[]{:S(2)}, u32[]{:S(2)}) collective-permute-start(bf16[32,1024]{1,0:T(8,128)(2,1)S(1)} %get-tuple-element.65), channel_id=1, source_target_pairs={{0,2},{1,3},{2,0},{3,1},{4,6},{5,7},{6,4},{7,5},{8,10},{9,11},{10,... | collective-permute-start | bytes 196616 | tf_op jit(solution)/shard_map/ppermute | solution.py:433
  80.9 2.3 %collective-permute-start.16 = (bf16[32,1024]{1,0:T(8,128)(2,1)S(1)}, bf16[32,1024]{1,0:T(8,128)(2,1)S(1)}, u32[]{:S(2)}, u32[]{:S(2)}) collective-permute-start(bf16[32,1024]{1,0:T(8,128)(2,1)S(1)} %get-tuple-element.66), channel_id=1, source_target_pairs={{0,18},{1,19},{2,16},{3,17},{4,22},{5,23},{6,20},{7,21},{8,26},{9,... | collective-permute-start | bytes 196616 | tf_op jit(solution)/shard_map/ppermute | solution.py:433
  83.2 0.0 collective-permute-done.12.refs_1_
  83.2 1.1 %collective-permute-start.17 = (bf16[32,1024]{1,0:T(8,128)(2,1)S(1)}, bf16[32,1024]{1,0:T(8,128)(2,1)S(1)}, u32[]{:S(2)}, u32[]{:S(2)}) collective-permute-start(bf16[32,1024]{1,0:T(8,128)(2,1)S(1)} %get-tuple-element.67), channel_id=1, source_target_pairs={{0,3},{1,2},{2,1},{3,0},{4,7},{5,6},{6,5},{7,4},{8,11},{9,10},{10,... | collective-permute-start | bytes 196616 | tf_op jit(solution)/shard_map/ppermute | solution.py:433
  84.3 0.0 collective-permute-done.13.refs_2_
  84.3 0.7 collective-permute-start.18
  85.0 0.0 collective-permute-done.14.refs_3_
  85.0 0.0 collective-permute-done.15.refs_4_
  85.0 5.6 %collective-permute-done.16.refs_5_ = bf16[32,1024]{1,0:T(8,128)(2,1)S(1)} collective-permute-done((bf16[32,1024]{1,0:T(8,128)(2,1)S(1)}, bf16[32,1024]{1,0:T(8,128)(2,1)S(1)}, u32[]{:S(2)}, u32[]{:S(2)}) %collective-permute-start.16) | collective-permute-done | bytes 65568 | tf_op jit(solution)/shard_map/ppermute | solution.py:433
  90.6 0.0 collective-permute-done.17.refs_6_
  90.6 0.9 collective-permute-done.18.refs_7_
  91.4 0.8 place_parts.1
Async XLA Ops:
  1.1 16.2 %copy-start.2 = (s32[2,8]{1,0:T(2,128)S(1)}, s32[2,8]{1,0:T(2,128)}, u32[]{:S(2)}) copy-start(s32[2,8]{1,0:T(2,128)} %offsets.9) | copy-start | bytes 196
  1.1 16.1 %copy-start.3 = (s32[2,64]{1,0:T(2,128)S(1)}, s32[2,64]{1,0:T(2,128)}, u32[]{:S(2)}) copy-start(s32[2,64]{1,0:T(2,128)} %scalars.1) | copy-start | bytes 1540
  1.1 16.1 %collective-permute-start = (bf16[128,1024]{1,0:T(8,128)(2,1)S(1)}, bf16[128,1024]{1,0:T(8,128)(2,1)S(1)}, u32[]{:S(2)}, u32[]{:S(2)}) collective-permute-start(bf16[128,1024]{1,0:T(8,128)(2,1)S(1)} %get-tuple-element.69), channel_id=1, source_target_pairs={{0,16},{4,20},{8,24},{12,28},{16,0},{20,4},{24,8},{28,12},{1,17},{... | collective-permute-start | bytes 786440 | tf_op jit(solution)/shard_map/ppermute | solution.py:337
  9.9 22.8 %collective-permute-start.2 = (bf16[1152,256]{1,0:T(8,128)(2,1)}, bf16[1152,256]{1,0:T(8,128)(2,1)S(1)}, u32[]{:S(2)}, u32[]{:S(2)}) collective-permute-start(bf16[1152,256]{1,0:T(8,128)(2,1)} %get-tuple-element.39.refs_2_.refs_1_), channel_id=1, source_target_pairs={{0,4},{4,0},{8,12},{12,8},{16,20},{20,16},{24,28},{28,24},{1,5},{5... | collective-permute-start | bytes 1769480 | tf_op jit(solution)/shard_map/ppermute | solution.py:364
  11.7 27.9 %collective-permute-start.3 = (bf16[1152,256]{1,0:T(8,128)(2,1)}, bf16[1152,256]{1,0:T(8,128)(2,1)S(1)}, u32[]{:S(2)}, u32[]{:S(2)}) collective-permute-start(bf16[1152,256]{1,0:T(8,128)(2,1)} %get-tuple-element.39.refs_2_.refs_1_), channel_id=1, source_target_pairs={{0,8},{4,12},{8,0},{12,4},{16,24},{20,28},{24,16},{28,20},{1,9},{5... | collective-permute-start | bytes 1769480 | tf_op jit(solution)/shard_map/ppermute | solution.py:364
  17.2 15.5 %collective-permute-start.1 = (bf16[640,256]{1,0:T(8,128)(2,1)}, bf16[640,256]{1,0:T(8,128)(2,1)S(1)}, u32[]{:S(2)}, u32[]{:S(2)}) collective-permute-start(bf16[640,256]{1,0:T(8,128)(2,1)} %get-tuple-element.42), channel_id=1, source_target_pairs={{0,16},{4,20},{8,24},{12,28},{16,0},{20,4},{24,8},{28,12},{1,17},{... | collective-permute-start | bytes 983048 | tf_op jit(solution)/shard_map/ppermute | solution.py:397
  17.2 1.1 %copy-start = (bf16[1152,256]{1,0:T(8,128)(2,1)S(1)}, bf16[1152,256]{1,0:T(8,128)(2,1)}, u32[]{:S(2)}) copy-start(bf16[1152,256]{1,0:T(8,128)(2,1)} %get-tuple-element.39.refs_2_.refs_1_) | copy-start | bytes 1769476
  32.7 16.1 %collective-permute-start.6 = (bf16[640,256]{1,0:T(8,128)(2,1)S(1)}, bf16[640,256]{1,0:T(8,128)(2,1)S(1)}, u32[]{:S(2)}, u32[]{:S(2)}) collective-permute-start(bf16[640,256]{1,0:T(8,128)(2,1)S(1)} %collective-permute-done.1.refs_4_), channel_id=1, source_target_pairs={{0,4},{4,0},{8,12},{12,8},{16,20},{20,16},{24,28},{28,24},{1,5},{5... | collective-permute-start | bytes 983048 | tf_op jit(solution)/shard_map/ppermute | solution.py:364
  35.6 13.2 %collective-permute-start.5 = (bf16[512,256]{1,0:T(8,128)(2,1)}, bf16[512,256]{1,0:T(8,128)(2,1)S(1)}, u32[]{:S(2)}, u32[]{:S(2)}) collective-permute-start(bf16[512,256]{1,0:T(8,128)(2,1)} %get-tuple-element.47), channel_id=1, source_target_pairs={{0,16},{4,20},{8,24},{12,28},{16,0},{20,4},{24,8},{28,12},{1,17},{... | collective-permute-start | bytes 786440 | tf_op jit(solution)/shard_map/ppermute | solution.py:398
  39.6 19.7 %collective-permute-start.4 = (bf16[1152,256]{1,0:T(8,128)(2,1)S(1)}, bf16[1152,256]{1,0:T(8,128)(2,1)S(1)}, u32[]{:S(2)}, u32[]{:S(2)}) collective-permute-start(bf16[1152,256]{1,0:T(8,128)(2,1)S(1)} %collective-permute-done.3.refs_3_), channel_id=1, source_target_pairs={{0,4},{4,0},{8,12},{12,8},{16,20},{20,16},{24,28},{28,24},{1,5},{5... | collective-permute-start | bytes 1769480 | tf_op jit(solution)/shard_map/ppermute | solution.py:364
  41.4 12.5 %collective-permute-start.7 = (bf16[640,256]{1,0:T(8,128)(2,1)S(1)}, bf16[640,256]{1,0:T(8,128)(2,1)S(1)}, u32[]{:S(2)}, u32[]{:S(2)}) collective-permute-start(bf16[640,256]{1,0:T(8,128)(2,1)S(1)} %collective-permute-done.1.refs_4_), channel_id=1, source_target_pairs={{0,8},{4,12},{8,0},{12,4},{16,24},{20,28},{24,16},{28,20},{1,9},{5... | collective-permute-start | bytes 983048 | tf_op jit(solution)/shard_map/ppermute | solution.py:364
  41.4 1.1 %copy-start.1 = (bf16[1152,256]{1,0:T(8,128)(2,1)S(1)}, bf16[1152,256]{1,0:T(8,128)(2,1)}, u32[]{:S(2)}) copy-start(bf16[1152,256]{1,0:T(8,128)(2,1)} %get-tuple-element.39.refs_2_.refs_1_) | copy-start | bytes 1769476
  48.8 10.4 %collective-permute-start.8 = (bf16[512,256]{1,0:T(8,128)(2,1)S(1)}, bf16[512,256]{1,0:T(8,128)(2,1)S(1)}, u32[]{:S(2)}, u32[]{:S(2)}) collective-permute-start(bf16[512,256]{1,0:T(8,128)(2,1)S(1)} %collective-permute-done.5.refs_8_), channel_id=1, source_target_pairs={{0,8},{4,12},{8,0},{12,4},{16,24},{20,28},{24,16},{28,20},{1,9},{5... | collective-permute-start | bytes 786440 | tf_op jit(solution)/shard_map/ppermute | solution.py:364
  53.9 16.4 %collective-permute-start.9 = (bf16[640,256]{1,0:T(8,128)(2,1)S(1)}, bf16[640,256]{1,0:T(8,128)(2,1)S(1)}, u32[]{:S(2)}, u32[]{:S(2)}) collective-permute-start(bf16[640,256]{1,0:T(8,128)(2,1)S(1)} %collective-permute-done.7.refs_7_), channel_id=1, source_target_pairs={{0,4},{4,0},{8,12},{12,8},{16,20},{20,16},{24,28},{28,24},{1,5},{5... | collective-permute-start | bytes 983048 | tf_op jit(solution)/shard_map/ppermute | solution.py:364
  54.3 16.0 %collective-permute-start.10 = (bf16[512,256]{1,0:T(8,128)(2,1)S(1)}, bf16[512,256]{1,0:T(8,128)(2,1)S(1)}, u32[]{:S(2)}, u32[]{:S(2)}) collective-permute-start(bf16[512,256]{1,0:T(8,128)(2,1)S(1)} %collective-permute-done.5.refs_8_), channel_id=1, source_target_pairs={{0,4},{4,0},{8,12},{12,8},{16,20},{20,16},{24,28},{28,24},{1,5},{5... | collective-permute-start | bytes 786440 | tf_op jit(solution)/shard_map/ppermute | solution.py:364
  59.1 15.4 %collective-permute-start.11 = (bf16[512,256]{1,0:T(8,128)(2,1)S(1)}, bf16[512,256]{1,0:T(8,128)(2,1)S(1)}, u32[]{:S(2)}, u32[]{:S(2)}) collective-permute-start(bf16[512,256]{1,0:T(8,128)(2,1)S(1)} %collective-permute-done.8.refs_9_), channel_id=1, source_target_pairs={{0,4},{4,0},{8,12},{12,8},{16,20},{20,16},{24,28},{28,24},{1,5},{5... | collective-permute-start | bytes 786440 | tf_op jit(solution)/shard_map/ppermute | solution.py:364
  75.6 7.6 %collective-permute-start.12 = (bf16[32,1024]{1,0:T(8,128)(2,1)S(1)}, bf16[32,1024]{1,0:T(8,128)(2,1)S(1)}, u32[]{:S(2)}, u32[]{:S(2)}) collective-permute-start(bf16[32,1024]{1,0:T(8,128)(2,1)S(1)} %get-tuple-element.62), channel_id=1, source_target_pairs={{0,16},{1,17},{2,18},{3,19},{4,20},{5,21},{6,22},{7,23},{8,24},{9,... | collective-permute-start | bytes 196616 | tf_op jit(solution)/shard_map/ppermute | solution.py:433
  77.0 7.3 %collective-permute-start.13 = (bf16[32,1024]{1,0:T(8,128)(2,1)S(1)}, bf16[32,1024]{1,0:T(8,128)(2,1)S(1)}, u32[]{:S(2)}, u32[]{:S(2)}) collective-permute-start(bf16[32,1024]{1,0:T(8,128)(2,1)S(1)} %get-tuple-element.63), channel_id=1, source_target_pairs={{0,1},{1,0},{2,3},{3,2},{4,5},{5,4},{6,7},{7,6},{8,9},{9,8},{10,11... | collective-permute-start | bytes 196616 | tf_op jit(solution)/shard_map/ppermute | solution.py:433
  77.0 7.9 %collective-permute-start.14 = (bf16[32,1024]{1,0:T(8,128)(2,1)S(1)}, bf16[32,1024]{1,0:T(8,128)(2,1)S(1)}, u32[]{:S(2)}, u32[]{:S(2)}) collective-permute-start(bf16[32,1024]{1,0:T(8,128)(2,1)S(1)} %get-tuple-element.64), channel_id=1, source_target_pairs={{0,17},{1,16},{2,19},{3,18},{4,21},{5,20},{6,23},{7,22},{8,25},{9,... | collective-permute-start | bytes 196616 | tf_op jit(solution)/shard_map/ppermute | solution.py:433
  78.7 6.2 %collective-permute-start.15 = (bf16[32,1024]{1,0:T(8,128)(2,1)S(1)}, bf16[32,1024]{1,0:T(8,128)(2,1)S(1)}, u32[]{:S(2)}, u32[]{:S(2)}) collective-permute-start(bf16[32,1024]{1,0:T(8,128)(2,1)S(1)} %get-tuple-element.65), channel_id=1, source_target_pairs={{0,2},{1,3},{2,0},{3,1},{4,6},{5,7},{6,4},{7,5},{8,10},{9,11},{10,... | collective-permute-start | bytes 196616 | tf_op jit(solution)/shard_map/ppermute | solution.py:433
  80.9 9.6 %collective-permute-start.16 = (bf16[32,1024]{1,0:T(8,128)(2,1)S(1)}, bf16[32,1024]{1,0:T(8,128)(2,1)S(1)}, u32[]{:S(2)}, u32[]{:S(2)}) collective-permute-start(bf16[32,1024]{1,0:T(8,128)(2,1)S(1)} %get-tuple-element.66), channel_id=1, source_target_pairs={{0,18},{1,19},{2,16},{3,17},{4,22},{5,23},{6,20},{7,21},{8,26},{9,... | collective-permute-start | bytes 196616 | tf_op jit(solution)/shard_map/ppermute | solution.py:433
  83.2 7.4 %collective-permute-start.17 = (bf16[32,1024]{1,0:T(8,128)(2,1)S(1)}, bf16[32,1024]{1,0:T(8,128)(2,1)S(1)}, u32[]{:S(2)}, u32[]{:S(2)}) collective-permute-start(bf16[32,1024]{1,0:T(8,128)(2,1)S(1)} %get-tuple-element.67), channel_id=1, source_target_pairs={{0,3},{1,2},{2,1},{3,0},{4,7},{5,6},{6,5},{7,4},{8,11},{9,10},{10,... | collective-permute-start | bytes 196616 | tf_op jit(solution)/shard_map/ppermute | solution.py:433
  84.3 7.1 %collective-permute-start.18 = (bf16[32,1024]{1,0:T(8,128)(2,1)S(1)}, bf16[32,1024]{1,0:T(8,128)(2,1)S(1)}, u32[]{:S(2)}, u32[]{:S(2)}) collective-permute-start(bf16[32,1024]{1,0:T(8,128)(2,1)S(1)} %get-tuple-element.68), channel_id=1, source_target_pairs={{0,19},{1,18},{2,17},{3,16},{4,23},{5,22},{6,21},{7,20},{8,27},{9,... | collective-permute-start | bytes 196616 | tf_op jit(solution)/shard_map/ppermute | solution.py:433

commit v4 on v3

--- a/solution.py
+++ b/solution.py
@@ -299,7 +299,7 @@
         input_output_aliases={len(operands) - len(state) + n: n for n in range(len(state))},
         compiler_params=pltpu.CompilerParams(vmem_limit_bytes=28 * 1024 * 1024),
         cost_estimate=pl.CostEstimate(
-            flops=2 * rows * depth * share, bytes_accessed=share * 4 * depth, transcendentals=0
+            flops=8 * rows * depth * share, bytes_accessed=share * 4 * depth, transcendentals=0
         ),
         name=name,
     )(*operands)
@@ -400,11 +400,16 @@
     for bit in bits[:-1]:
         near.update({m | bit: swap(x, bit) for m, x in near.items()})
     del near[0]
-    forwarded = {m | last_bit: swap(x, last_bit) for m, x in near.items()}
+    near, far[0] = lax.optimization_barrier((near, far[0]))
+    forwarded = {m | last_bit: swap(x[split * BLK :], last_bit) for m, x in near.items()}
+    turned = {last_bit: own[: split * BLK]}
+    for bit in bits[:-1]:
+        turned.update({m | bit: swap(x, bit) for m, x in turned.items()})
+    del turned[last_bit]
     stage("attend_own", (False, whole, True, {0: mine}))
     first_far, own, state = lax.optimization_barrier((far[0], own, state))
     far_own = swap(first_far, last_bit)
-    rest[0], far_own = lax.optimization_barrier((rest[0], far_own))
+    rest[0], far_own, turned = lax.optimization_barrier((rest[0], far_own, turned))
     stage("attend_near", (False, whole, True, {last_bit: own} | near), (True, low, True, {0: first_far}))
     rest[0], state = lax.optimization_barrier((rest[0], state))
     for bit in bits[:-1]:
@@ -416,7 +421,8 @@
     first_rest = rest.pop(0)
     last_rest = {m | last_bit: swap(x, last_bit) for m, x in rest.items()}
     stage(
-        "attend_far", (False, whole, True, forwarded), (True, low, True, {last_bit: far_own} | far),
+        "attend_far", (False, high, True, forwarded), (False, low, False, turned),
+        (True, low, True, {last_bit: far_own} | far),
         (True, high, False, {0: first_rest} | rest), slash=True,
     )
     stage("attend_tail", (True, low, True, last_far), (True, high, False, {last_bit: rest_own}), late_span=True)

time: 93.1 us -> 99.1 us (1.064)
  waiting for transfers between devices: 32.8 us -> 41.3 us
  starting transfers between devices: 25.3 us -> 22.8 us
  Pallas kernels: 30.9 us -> 32.2 us
  local copies, waits for them, and re-layouts: 3.2 us -> 2.18 us
    ppermute x1, waiting for transfers between devices: 0.01 us -> 5.71 us  [body(): rest = {0: lax.ppermute(theirs_rest, 'ctx', across)}]
    ppermute x9 -> x10, waiting for transfers between devices: 11 us -> 13.7 us  [swap(): return lax.ppermute(x, 'ctx', [(i, i ^ bit) for i in range(owners)])]
    ppermute x9 -> x10, starting transfers between devices: 10.8 us -> 9.22 us  [swap(): return lax.ppermute(x, 'ctx', [(i, i ^ bit) for i in range(owners)])]
    pallas_call x1, Pallas kernels: 4.71 us -> 5.94 us  [body(): pl.pallas_call(functools.partial(collect_kernel, owners, cap), out_shape=...]
    unnamed x8 -> x10, local copies, waits for them, and re-layouts: 2.13 us -> 1.08 us
  transfers between devices with their start and end apart: 19 -> 20, of which waited for: 7 -> 10; matrix products, arithmetic and copies ran while one was open for 0% -> 0% of each run, Pallas kernels for 31% -> 31%
where the time goes in v4:
time: 99.1 us; the launch traced here: 98.8 us
  waiting for transfers between devices  41.3 us (42%)
  Pallas kernels  32.2 us (32%)
  starting transfers between devices  22.8 us (23%)
  local copies, waits for them, and re-layouts  2.18 us (2%)
    pallas_call x5, Pallas kernels, attend(): pl.pallas_call(functools.partial(attend_kernel, stage), out_shape=out_sha...  25.4 us
    ppermute x10, waiting for transfers between devices, swap(): return lax.ppermute(x, 'ctx', [(i, i ^ bit) for i in range(owners)])  13.7 us
    ppermute x1, waiting for transfers between devices, body(): far = {0: lax.ppermute(theirs, 'ctx', across)}  11.5 us
    ppermute x10, starting transfers between devices, swap(): return lax.ppermute(x, 'ctx', [(i, i ^ bit) for i in range(owners)])  9.22 us
    ppermute x7, starting transfers between devices, body(): lax.ppermute(sent[k], ('ctx', 'head'), [(d, partner(d, k)) for d in devic...  8.67 us
    ppermute x7, waiting for transfers between devices, body(): lax.ppermute(sent[k], ('ctx', 'head'), [(d, partner(d, k)) for d in devic...  6.56 us
    pallas_call x1, Pallas kernels, body(): pl.pallas_call(functools.partial(collect_kernel, owners, cap), out_shape=...  5.94 us
    ppermute x1, waiting for transfers between devices, body(): rest = {0: lax.ppermute(theirs_rest, 'ctx', across)}  5.71 us
  transfers between devices with their start and end apart: 20, of which 10 were waited for; matrix products, arithmetic and copies ran while one was open for 0% of the time, Pallas kernels for 31%

profile of v4, /device:TPU:0, one launch (start us, length us, event | category | flops | bytes accessed | tf_op | source)
XLA Modules:
  0.0 98.8 jit_solution(7399273771292570521)
XLA Ops:
  0.0 1.1 %constant_dynamic-slice_fusion = (bf16[128,1024]{1,0:T(8,128)(2,1)S(1)}, bf16[128,1024]{1,0:T(8,128)(2,1)S(1)}) fusion(bf16[128,2048]{1,0:T(8,128)(2,1)} %param.5, s32[]{:T(128)S(6)} %select_n.13, s32[]{:T(128)S(6)} %select_n.12), kind=kLoop, calls=%fused_computation | loop fusion | bytes 1048584 | tf_op jit(solution)/shard_map/dynamic_slice | solution.py:335
  1.1 0.0 copy-start.2
  1.1 0.0 copy-start.3
  1.1 4.1 %collective-permute-start = (bf16[128,1024]{1,0:T(8,128)(2,1)S(1)}, bf16[128,1024]{1,0:T(8,128)(2,1)S(1)}, u32[]{:S(2)}, u32[]{:S(2)}) collective-permute-start(bf16[128,1024]{1,0:T(8,128)(2,1)S(1)} %get-tuple-element.75), channel_id=1, source_target_pairs={{0,16},{4,20},{8,24},{12,28},{16,0},{20,4},{24,8},{28,12},{1,17},{... | collective-permute-start | bytes 786440 | tf_op jit(solution)/shard_map/ppermute | solution.py:337
  5.2 5.9 %collect_slots.1 = (bf16[1152,256]{1,0:T(8,128)(2,1)}, bf16[640,256]{1,0:T(8,128)(2,1)}, bf16[512,256]{1,0:T(8,128)(2,1)}) custom-call(s32[2,64]{1,0:T(2,128)} %scalars.1, bf16[4096,2,256]{2,1,0:T(2,128)(2,1)} %cache.1, bf16[128,2,256]{2,1,0:T(2,128)(2,1)} %span.1), custom_call_target="tpu_custom_call" | custom-call | bytes 2097152 | tf_op jit(solution)/shard_map/collect_slots/pallas_call | solution.py:343
  11.1 0.6 collective-permute-start.1
  11.7 1.7 %collective-permute-start.3 = (bf16[1152,256]{1,0:T(8,128)(2,1)}, bf16[1152,256]{1,0:T(8,128)(2,1)S(1)}, u32[]{:S(2)}, u32[]{:S(2)}) collective-permute-start(bf16[1152,256]{1,0:T(8,128)(2,1)} %get-tuple-element.42.refs_2_.refs_1_), channel_id=1, source_target_pairs={{0,4},{4,0},{8,12},{12,8},{16,20},{20,16},{24,28},{28,24},{1,5},{5... | collective-permute-start | bytes 1769480 | tf_op jit(solution)/shard_map/ppermute | solution.py:364
  13.4 3.8 %collective-permute-done.refs_1_ = bf16[128,1024]{1,0:T(8,128)(2,1)S(1)} collective-permute-done((bf16[128,1024]{1,0:T(8,128)(2,1)S(1)}, bf16[128,1024]{1,0:T(8,128)(2,1)S(1)}, u32[]{:S(2)}, u32[]{:S(2)}) %collective-permute-start) | collective-permute-done | bytes 262176 | tf_op jit(solution)/shard_map/ppermute | solution.py:337
  17.2 0.0 collective-permute-start.2
  17.2 0.0 copy-done.2
  17.2 0.0 copy-done.3
  17.2 0.0 copy-start
  17.2 1.1 %copy-done = bf16[1152,256]{1,0:T(8,128)(2,1)S(1)} copy-done((bf16[1152,256]{1,0:T(8,128)(2,1)S(1)}, bf16[1152,256]{1,0:T(8,128)(2,1)}, u32[]{:S(2)}) %copy-start) | copy-done | bytes 589848
  18.3 0.0 copy-start.4
  18.3 0.0 copy-start.1
  18.3 4.5 %attend_own.1 = (f32[2048,128]{1,0:T(8,128)S(1)}, f32[2048,256]{1,0:T(8,128)S(1)}, bf16[2048,128]{1,0:T(8,128)(2,1)S(1)}, s32[8]{0:T(128)S(1)}) custom-call(s32[2,64]{1,0:T(2,128)S(1)} %copy-done.3, s32[2,8]{1,0:T(2,128)S(1)} %copy-done.2, bf16[128,1024]{1,0:T(8,128)(2,1)S(1)} %get-tuple-element.76.refs_0_, ...), custom_call_target="tpu_custom_call" | custom-call | flops 1073741824 | bytes 262144 | tf_op jit(solution)/shard_map/attend_own/pallas_call | solution.py:293
  22.8 11.5 %collective-permute-done.2.refs_4_ = bf16[640,256]{1,0:T(8,128)(2,1)S(1)} collective-permute-done((bf16[640,256]{1,0:T(8,128)(2,1)}, bf16[640,256]{1,0:T(8,128)(2,1)S(1)}, u32[]{:S(2)}, u32[]{:S(2)}) %collective-permute-start.2) | collective-permute-done | bytes 327712 | tf_op jit(solution)/shard_map/ppermute | solution.py:397
  34.3 2.4 %collective-permute-done.1.refs_3_ = bf16[1152,256]{1,0:T(8,128)(2,1)S(1)} collective-permute-done((bf16[1152,256]{1,0:T(8,128)(2,1)}, bf16[1152,256]{1,0:T(8,128)(2,1)S(1)}, u32[]{:S(2)}, u32[]{:S(2)}) %collective-permute-start.1) | collective-permute-done | bytes 589856 | tf_op jit(solution)/shard_map/ppermute | solution.py:364
  36.8 0.0 collective-permute-done.3.refs_2_
  36.8 1.5 %collective-permute-start.6 = (bf16[640,256]{1,0:T(8,128)(2,1)S(1)}, bf16[640,256]{1,0:T(8,128)(2,1)S(1)}, u32[]{:S(2)}, u32[]{:S(2)}) collective-permute-start(bf16[640,256]{1,0:T(8,128)(2,1)S(1)} %collective-permute-done.2.refs_4_), channel_id=1, source_target_pairs={{0,4},{4,0},{8,12},{12,8},{16,20},{20,16},{24,28},{28,24},{1,5},{5... | collective-permute-start | bytes 983048 | tf_op jit(solution)/shard_map/ppermute | solution.py:364
  38.3 0.0 copy-done.4
  38.3 0.8 collective-permute-start.5
  39.2 2.4 %collective-permute-start.8 = (bf16[640,256]{1,0:T(8,128)(2,1)S(1)}, bf16[640,256]{1,0:T(8,128)(2,1)S(1)}, u32[]{:S(2)}, u32[]{:S(2)}) collective-permute-start(bf16[640,256]{1,0:T(8,128)(2,1)S(1)} %collective-permute-done.2.refs_4_), channel_id=1, source_target_pairs={{0,8},{4,12},{8,0},{12,4},{16,24},{20,28},{24,16},{28,20},{1,9},{5... | collective-permute-start | bytes 983048 | tf_op jit(solution)/shard_map/ppermute | solution.py:364
  41.6 0.1 collective-permute-start.7
  41.7 0.1 collective-permute-start.4
  41.8 0.0 copy-done.1
  41.8 4.5 %attend_near.1 = (f32[2048,128]{1,0:T(8,128)S(1)}, f32[2048,256]{1,0:T(8,128)S(1)}) custom-call(s32[8]{0:T(128)S(1)} %get-tuple-element.43.scalars, s32[2,8]{1,0:T(2,128)S(1)} %copy-done.2, bf16[2048,128]{1,0:T(8,128)(2,1)S(1)} %get-tuple-element.44.refs_0_, bf16[1152,256]{1,0:T(8,128)(2,1)S(1)} %copy-done.1, ...), custom_call_target="tpu_custom_call", output_to_operand_aliasing={{0}: (7, {}), {1}: (8, {})} | custom-call | flops 3221225472 | bytes 786432 | tf_op jit(solution)/shard_map/attend_near/pallas_call | solution.py:293
  46.3 5.7 %collective-permute-done.5.refs_9_ = bf16[512,256]{1,0:T(8,128)(2,1)S(1)} collective-permute-done((bf16[512,256]{1,0:T(8,128)(2,1)S(1)}, bf16[512,256]{1,0:T(8,128)(2,1)S(1)}, u32[]{:S(2)}, u32[]{:S(2)}) %collective-permute-start.5) | collective-permute-done | bytes 262176 | tf_op jit(solution)/shard_map/ppermute | solution.py:398
  52.0 6.9 %collective-permute-done.7.refs_6_ = bf16[512,256]{1,0:T(8,128)(2,1)S(1)} collective-permute-done((bf16[512,256]{1,0:T(8,128)(2,1)S(1)}, bf16[512,256]{1,0:T(8,128)(2,1)S(1)}, u32[]{:S(2)}, u32[]{:S(2)}) %collective-permute-start.7) | collective-permute-done | bytes 262176 | tf_op jit(solution)/shard_map/ppermute | solution.py:364
  58.9 0.0 collective-permute-done.6.refs_7_
  58.9 0.3 collective-permute-start.9
  59.2 0.5 collective-permute-start.11
  59.7 0.0 collective-permute-done.8.refs_8_
  59.7 1.5 %collective-permute-start.10 = (bf16[640,256]{1,0:T(8,128)(2,1)S(1)}, bf16[640,256]{1,0:T(8,128)(2,1)S(1)}, u32[]{:S(2)}, u32[]{:S(2)}) collective-permute-start(bf16[640,256]{1,0:T(8,128)(2,1)S(1)} %collective-permute-done.8.refs_8_), channel_id=1, source_target_pairs={{0,4},{4,0},{8,12},{12,8},{16,20},{20,16},{24,28},{28,24},{1,5},{5... | collective-permute-start | bytes 983048 | tf_op jit(solution)/shard_map/ppermute | solution.py:364
  61.3 4.0 %collective-permute-done.9.refs_10_ = bf16[512,256]{1,0:T(8,128)(2,1)S(1)} collective-permute-done((bf16[512,256]{1,0:T(8,128)(2,1)S(1)}, bf16[512,256]{1,0:T(8,128)(2,1)S(1)}, u32[]{:S(2)}, u32[]{:S(2)}) %collective-permute-start.9) | collective-permute-done | bytes 262176 | tf_op jit(solution)/shard_map/ppermute | solution.py:364
  65.3 0.5 collective-permute-start.12
  65.8 0.0 collective-permute-done.4.refs_5_
  65.8 9.2 %attend_far.1 = (f32[2048,128]{1,0:T(8,128)S(1)}, f32[2048,256]{1,0:T(8,128)S(1)}) custom-call(s32[8]{0:T(128)S(1)} %get-tuple-element.43.scalars, s32[2,8]{1,0:T(2,128)S(1)} %copy-done.2, bf16[2048,128]{1,0:T(8,128)(2,1)S(1)} %get-tuple-element.44.refs_0_, bf16[1152,256]{1,0:T(8,128)(2,1)S(1)} %copy-done.1, ...), custom_call_target="tpu_custom_call", output_to_operand_aliasing={{0}: (13, {}), {1}: (14, {})} | custom-call | flops 4294967296 | bytes 1048576 | tf_op jit(solution)/shard_map/attend_far/pallas_call | solution.py:293
  75.0 0.0 collective-permute-done.11.refs_12_
  75.0 0.3 collective-permute-done.10.refs_11_
  75.3 6.1 %attend_tail.1 = (f32[2048,128]{1,0:T(8,128)S(1)}, f32[2048,256]{1,0:T(8,128)S(1)}) custom-call(s32[8]{0:T(128)S(1)} %get-tuple-element.43.scalars, s32[2,8]{1,0:T(2,128)S(1)} %copy-done.2, bf16[2048,128]{1,0:T(8,128)(2,1)S(1)} %get-tuple-element.44.refs_0_, bf16[1152,256]{1,0:T(8,128)(2,1)S(1)} %copy-done.1, ...), custom_call_target="tpu_custom_call", output_to_operand_aliasing={{0}: (15, {}), {1}: (16, {})} | custom-call | flops 1073741824 | bytes 262144 | tf_op jit(solution)/shard_map/attend_tail/pallas_call | solution.py:293
  81.4 0.0 collective-permute-done.12.refs_13_
  81.4 1.1 %attend_last.1 = (f32[2048,128]{1,0:T(8,128)S(1)}, f32[2048,256]{1,0:T(8,128)S(1)}, bf16[32,1024]{1,0:T(8,128)(2,1)S(1)}, bf16[32,1024]{1,0:T(8,128)(2,1)S(1)}, ...) custom-call(s32[8]{0:T(128)S(1)} %get-tuple-element.43.scalars, ...), custom_call_target="tpu_custom_call", output_to_operand_aliasing={{0}: (16, {}), {1}: (17, {})} | custom-call | tf_op jit(solution)/shard_map/attend_last/pallas_call | solution.py:293
  82.5 1.2 %collective-permute-start.13 = (bf16[32,1024]{1,0:T(8,128)(2,1)S(1)}, bf16[32,1024]{1,0:T(8,128)(2,1)S(1)}, u32[]{:S(2)}, u32[]{:S(2)}) collective-permute-start(bf16[32,1024]{1,0:T(8,128)(2,1)S(1)} %get-tuple-element.68), channel_id=1, source_target_pairs={{0,16},{1,17},{2,18},{3,19},{4,20},{5,21},{6,22},{7,23},{8,24},{9,... | collective-permute-start | bytes 196616 | tf_op jit(solution)/shard_map/ppermute | solution.py:439
  83.7 0.0 collective-permute-start.14
  83.7 1.9 %collective-permute-start.15 = (bf16[32,1024]{1,0:T(8,128)(2,1)S(1)}, bf16[32,1024]{1,0:T(8,128)(2,1)S(1)}, u32[]{:S(2)}, u32[]{:S(2)}) collective-permute-start(bf16[32,1024]{1,0:T(8,128)(2,1)S(1)} %get-tuple-element.70), channel_id=1, source_target_pairs={{0,17},{1,16},{2,19},{3,18},{4,21},{5,20},{6,23},{7,22},{8,25},{9,... | collective-permute-start | bytes 196616 | tf_op jit(solution)/shard_map/ppermute | solution.py:439
  85.6 1.1 %collective-permute-start.16 = (bf16[32,1024]{1,0:T(8,128)(2,1)S(1)}, bf16[32,1024]{1,0:T(8,128)(2,1)S(1)}, u32[]{:S(2)}, u32[]{:S(2)}) collective-permute-start(bf16[32,1024]{1,0:T(8,128)(2,1)S(1)} %get-tuple-element.71), channel_id=1, source_target_pairs={{0,2},{1,3},{2,0},{3,1},{4,6},{5,7},{6,4},{7,5},{8,10},{9,11},{10,... | collective-permute-start | bytes 196616 | tf_op jit(solution)/shard_map/ppermute | solution.py:439
  86.8 2.3 %collective-permute-start.17 = (bf16[32,1024]{1,0:T(8,128)(2,1)S(1)}, bf16[32,1024]{1,0:T(8,128)(2,1)S(1)}, u32[]{:S(2)}, u32[]{:S(2)}) collective-permute-start(bf16[32,1024]{1,0:T(8,128)(2,1)S(1)} %get-tuple-element.72), channel_id=1, source_target_pairs={{0,18},{1,19},{2,16},{3,17},{4,22},{5,23},{6,20},{7,21},{8,26},{9,... | collective-permute-start | bytes 196616 | tf_op jit(solution)/shard_map/ppermute | solution.py:439
  89.0 0.0 collective-permute-done.13.refs_1_
  89.0 1.1 %collective-permute-start.18 = (bf16[32,1024]{1,0:T(8,128)(2,1)S(1)}, bf16[32,1024]{1,0:T(8,128)(2,1)S(1)}, u32[]{:S(2)}, u32[]{:S(2)}) collective-permute-start(bf16[32,1024]{1,0:T(8,128)(2,1)S(1)} %get-tuple-element.73), channel_id=1, source_target_pairs={{0,3},{1,2},{2,1},{3,0},{4,7},{5,6},{6,5},{7,4},{8,11},{9,10},{10,... | collective-permute-start | bytes 196616 | tf_op jit(solution)/shard_map/ppermute | solution.py:439
  90.1 0.0 collective-permute-done.14.refs_2_
  90.1 1.1 %collective-permute-start.19 = (bf16[32,1024]{1,0:T(8,128)(2,1)S(1)}, bf16[32,1024]{1,0:T(8,128)(2,1)S(1)}, u32[]{:S(2)}, u32[]{:S(2)}) collective-permute-start(bf16[32,1024]{1,0:T(8,128)(2,1)S(1)} %get-tuple-element.74), channel_id=1, source_target_pairs={{0,19},{1,18},{2,17},{3,16},{4,23},{5,22},{6,21},{7,20},{8,27},{9,... | collective-permute-start | bytes 196616 | tf_op jit(solution)/shard_map/ppermute | solution.py:439
  91.2 0.6 collective-permute-done.15.refs_3_
  91.8 0.0 collective-permute-done.16.refs_4_
  91.8 4.9 %collective-permute-done.17.refs_5_ = bf16[32,1024]{1,0:T(8,128)(2,1)S(1)} collective-permute-done((bf16[32,1024]{1,0:T(8,128)(2,1)S(1)}, bf16[32,1024]{1,0:T(8,128)(2,1)S(1)}, u32[]{:S(2)}, u32[]{:S(2)}) %collective-permute-start.17) | collective-permute-done | bytes 65568 | tf_op jit(solution)/shard_map/ppermute | solution.py:439
  96.7 0.0 collective-permute-done.18.refs_6_
  96.7 1.1 %collective-permute-done.19.refs_7_ = bf16[32,1024]{1,0:T(8,128)(2,1)S(1)} collective-permute-done((bf16[32,1024]{1,0:T(8,128)(2,1)S(1)}, bf16[32,1024]{1,0:T(8,128)(2,1)S(1)}, u32[]{:S(2)}, u32[]{:S(2)}) %collective-permute-start.19) | collective-permute-done | bytes 65568 | tf_op jit(solution)/shard_map/ppermute | solution.py:439
  97.8 0.8 place_parts.1
  (2 shorter events, 0.0 us)
Async XLA Ops:
  1.1 16.2 %copy-start.2 = (s32[2,8]{1,0:T(2,128)S(1)}, s32[2,8]{1,0:T(2,128)}, u32[]{:S(2)}) copy-start(s32[2,8]{1,0:T(2,128)} %offsets.9) | copy-start | bytes 196
  1.1 16.1 %copy-start.3 = (s32[2,64]{1,0:T(2,128)S(1)}, s32[2,64]{1,0:T(2,128)}, u32[]{:S(2)}) copy-start(s32[2,64]{1,0:T(2,128)} %scalars.1) | copy-start | bytes 1540
  1.1 16.1 %collective-permute-start = (bf16[128,1024]{1,0:T(8,128)(2,1)S(1)}, bf16[128,1024]{1,0:T(8,128)(2,1)S(1)}, u32[]{:S(2)}, u32[]{:S(2)}) collective-permute-start(bf16[128,1024]{1,0:T(8,128)(2,1)S(1)} %get-tuple-element.75), channel_id=1, source_target_pairs={{0,16},{4,20},{8,24},{12,28},{16,0},{20,4},{24,8},{28,12},{1,17},{... | collective-permute-start | bytes 786440 | tf_op jit(solution)/shard_map/ppermute | solution.py:337
  11.1 25.6 %collective-permute-start.1 = (bf16[1152,256]{1,0:T(8,128)(2,1)}, bf16[1152,256]{1,0:T(8,128)(2,1)S(1)}, u32[]{:S(2)}, u32[]{:S(2)}) collective-permute-start(bf16[1152,256]{1,0:T(8,128)(2,1)} %get-tuple-element.42.refs_2_.refs_1_), channel_id=1, source_target_pairs={{0,8},{4,12},{8,0},{12,4},{16,24},{20,28},{24,16},{28,20},{1,9},{5... | collective-permute-start | bytes 1769480 | tf_op jit(solution)/shard_map/ppermute | solution.py:364
  11.7 25.1 %collective-permute-start.3 = (bf16[1152,256]{1,0:T(8,128)(2,1)}, bf16[1152,256]{1,0:T(8,128)(2,1)S(1)}, u32[]{:S(2)}, u32[]{:S(2)}) collective-permute-start(bf16[1152,256]{1,0:T(8,128)(2,1)} %get-tuple-element.42.refs_2_.refs_1_), channel_id=1, source_target_pairs={{0,4},{4,0},{8,12},{12,8},{16,20},{20,16},{24,28},{28,24},{1,5},{5... | collective-permute-start | bytes 1769480 | tf_op jit(solution)/shard_map/ppermute | solution.py:364
  17.2 17.1 %collective-permute-start.2 = (bf16[640,256]{1,0:T(8,128)(2,1)}, bf16[640,256]{1,0:T(8,128)(2,1)S(1)}, u32[]{:S(2)}, u32[]{:S(2)}) collective-permute-start(bf16[640,256]{1,0:T(8,128)(2,1)} %get-tuple-element.45), channel_id=1, source_target_pairs={{0,16},{4,20},{8,24},{12,28},{16,0},{20,4},{24,8},{28,12},{1,17},{... | collective-permute-start | bytes 983048 | tf_op jit(solution)/shard_map/ppermute | solution.py:397
  17.2 1.1 %copy-start = (bf16[1152,256]{1,0:T(8,128)(2,1)S(1)}, bf16[1152,256]{1,0:T(8,128)(2,1)}, u32[]{:S(2)}) copy-start(bf16[1152,256]{1,0:T(8,128)(2,1)} %get-tuple-element.42.refs_2_.refs_1_) | copy-start | bytes 1769476
  18.3 20.0 %copy-start.4 = (bf16[512,256]{1,0:T(8,128)(2,1)S(1)}, bf16[512,256]{1,0:T(8,128)(2,1)}, u32[]{:S(2)}) copy-start(bf16[512,256]{1,0:T(8,128)(2,1)} %get-tuple-element.52) | copy-start | bytes 786436
  18.3 23.5 %copy-start.1 = (bf16[1152,256]{1,0:T(8,128)(2,1)S(1)}, bf16[1152,256]{1,0:T(8,128)(2,1)}, u32[]{:S(2)}) copy-start(bf16[1152,256]{1,0:T(8,128)(2,1)} %get-tuple-element.42.refs_2_.refs_1_) | copy-start | bytes 1769476
  36.8 22.1 %collective-permute-start.6 = (bf16[640,256]{1,0:T(8,128)(2,1)S(1)}, bf16[640,256]{1,0:T(8,128)(2,1)S(1)}, u32[]{:S(2)}, u32[]{:S(2)}) collective-permute-start(bf16[640,256]{1,0:T(8,128)(2,1)S(1)} %collective-permute-done.2.refs_4_), channel_id=1, source_target_pairs={{0,4},{4,0},{8,12},{12,8},{16,20},{20,16},{24,28},{28,24},{1,5},{5... | collective-permute-start | bytes 983048 | tf_op jit(solution)/shard_map/ppermute | solution.py:364
  38.3 13.7 %collective-permute-start.5 = (bf16[512,256]{1,0:T(8,128)(2,1)S(1)}, bf16[512,256]{1,0:T(8,128)(2,1)S(1)}, u32[]{:S(2)}, u32[]{:S(2)}) collective-permute-start(bf16[512,256]{1,0:T(8,128)(2,1)S(1)} %copy-done.4), channel_id=1, source_target_pairs={{0,16},{4,20},{8,24},{12,28},{16,0},{20,4},{24,8},{28,12},{1,17},{... | collective-permute-start | bytes 786440 | tf_op jit(solution)/shard_map/ppermute | solution.py:398
  39.2 20.6 %collective-permute-start.8 = (bf16[640,256]{1,0:T(8,128)(2,1)S(1)}, bf16[640,256]{1,0:T(8,128)(2,1)S(1)}, u32[]{:S(2)}, u32[]{:S(2)}) collective-permute-start(bf16[640,256]{1,0:T(8,128)(2,1)S(1)} %collective-permute-done.2.refs_4_), channel_id=1, source_target_pairs={{0,8},{4,12},{8,0},{12,4},{16,24},{20,28},{24,16},{28,20},{1,9},{5... | collective-permute-start | bytes 983048 | tf_op jit(solution)/shard_map/ppermute | solution.py:364
  41.6 17.4 %collective-permute-start.7 = (bf16[512,256]{1,0:T(8,128)(2,1)S(1)}, bf16[512,256]{1,0:T(8,128)(2,1)S(1)}, u32[]{:S(2)}, u32[]{:S(2)}) collective-permute-start(bf16[512,256]{1,0:T(8,128)(2,1)S(1)} %slice.8), channel_id=1, source_target_pairs={{0,8},{4,12},{8,0},{12,4},{16,24},{20,28},{24,16},{28,20},{1,9},{5... | collective-permute-start | bytes 786440 | tf_op jit(solution)/shard_map/ppermute | solution.py:364
  41.7 24.1 %collective-permute-start.4 = (bf16[640,256]{1,0:T(8,128)(2,1)S(1)}, bf16[640,256]{1,0:T(8,128)(2,1)S(1)}, u32[]{:S(2)}, u32[]{:S(2)}) collective-permute-start(bf16[640,256]{1,0:T(8,128)(2,1)S(1)} %slice.6), channel_id=1, source_target_pairs={{0,4},{4,0},{8,12},{12,8},{16,20},{20,16},{24,28},{28,24},{1,5},{5... | collective-permute-start | bytes 983048 | tf_op jit(solution)/shard_map/ppermute | solution.py:364
  58.9 6.4 %collective-permute-start.9 = (bf16[512,256]{1,0:T(8,128)(2,1)S(1)}, bf16[512,256]{1,0:T(8,128)(2,1)S(1)}, u32[]{:S(2)}, u32[]{:S(2)}) collective-permute-start(bf16[512,256]{1,0:T(8,128)(2,1)S(1)} %collective-permute-done.5.refs_9_), channel_id=1, source_target_pairs={{0,8},{4,12},{8,0},{12,4},{16,24},{20,28},{24,16},{28,20},{1,9},{5... | collective-permute-start | bytes 786440 | tf_op jit(solution)/shard_map/ppermute | solution.py:364
  59.2 15.7 %collective-permute-start.11 = (bf16[512,256]{1,0:T(8,128)(2,1)S(1)}, bf16[512,256]{1,0:T(8,128)(2,1)S(1)}, u32[]{:S(2)}, u32[]{:S(2)}) collective-permute-start(bf16[512,256]{1,0:T(8,128)(2,1)S(1)} %collective-permute-done.5.refs_9_), channel_id=1, source_target_pairs={{0,4},{4,0},{8,12},{12,8},{16,20},{20,16},{24,28},{28,24},{1,5},{5... | collective-permute-start | bytes 786440 | tf_op jit(solution)/shard_map/ppermute | solution.py:364
  59.7 15.6 %collective-permute-start.10 = (bf16[640,256]{1,0:T(8,128)(2,1)S(1)}, bf16[640,256]{1,0:T(8,128)(2,1)S(1)}, u32[]{:S(2)}, u32[]{:S(2)}) collective-permute-start(bf16[640,256]{1,0:T(8,128)(2,1)S(1)} %collective-permute-done.8.refs_8_), channel_id=1, source_target_pairs={{0,4},{4,0},{8,12},{12,8},{16,20},{20,16},{24,28},{28,24},{1,5},{5... | collective-permute-start | bytes 983048 | tf_op jit(solution)/shard_map/ppermute | solution.py:364
  65.3 16.1 %collective-permute-start.12 = (bf16[512,256]{1,0:T(8,128)(2,1)S(1)}, bf16[512,256]{1,0:T(8,128)(2,1)S(1)}, u32[]{:S(2)}, u32[]{:S(2)}) collective-permute-start(bf16[512,256]{1,0:T(8,128)(2,1)S(1)} %collective-permute-done.9.refs_10_), channel_id=1, source_target_pairs={{0,4},{4,0},{8,12},{12,8},{16,20},{20,16},{24,28},{28,24},{1,5},{5... | collective-permute-start | bytes 786440 | tf_op jit(solution)/shard_map/ppermute | solution.py:364
  82.5 6.5 %collective-permute-start.13 = (bf16[32,1024]{1,0:T(8,128)(2,1)S(1)}, bf16[32,1024]{1,0:T(8,128)(2,1)S(1)}, u32[]{:S(2)}, u32[]{:S(2)}) collective-permute-start(bf16[32,1024]{1,0:T(8,128)(2,1)S(1)} %get-tuple-element.68), channel_id=1, source_target_pairs={{0,16},{1,17},{2,18},{3,19},{4,20},{5,21},{6,22},{7,23},{8,24},{9,... | collective-permute-start | bytes 196616 | tf_op jit(solution)/shard_map/ppermute | solution.py:439
  83.7 6.4 %collective-permute-start.14 = (bf16[32,1024]{1,0:T(8,128)(2,1)S(1)}, bf16[32,1024]{1,0:T(8,128)(2,1)S(1)}, u32[]{:S(2)}, u32[]{:S(2)}) collective-permute-start(bf16[32,1024]{1,0:T(8,128)(2,1)S(1)} %get-tuple-element.69), channel_id=1, source_target_pairs={{0,1},{1,0},{2,3},{3,2},{4,5},{5,4},{6,7},{7,6},{8,9},{9,8},{10,11... | collective-permute-start | bytes 196616 | tf_op jit(solution)/shard_map/ppermute | solution.py:439
  83.7 8.0 %collective-permute-start.15 = (bf16[32,1024]{1,0:T(8,128)(2,1)S(1)}, bf16[32,1024]{1,0:T(8,128)(2,1)S(1)}, u32[]{:S(2)}, u32[]{:S(2)}) collective-permute-start(bf16[32,1024]{1,0:T(8,128)(2,1)S(1)} %get-tuple-element.70), channel_id=1, source_target_pairs={{0,17},{1,16},{2,19},{3,18},{4,21},{5,20},{6,23},{7,22},{8,25},{9,... | collective-permute-start | bytes 196616 | tf_op jit(solution)/shard_map/ppermute | solution.py:439
  85.6 6.1 %collective-permute-start.16 = (bf16[32,1024]{1,0:T(8,128)(2,1)S(1)}, bf16[32,1024]{1,0:T(8,128)(2,1)S(1)}, u32[]{:S(2)}, u32[]{:S(2)}) collective-permute-start(bf16[32,1024]{1,0:T(8,128)(2,1)S(1)} %get-tuple-element.71), channel_id=1, source_target_pairs={{0,2},{1,3},{2,0},{3,1},{4,6},{5,7},{6,4},{7,5},{8,10},{9,11},{10,... | collective-permute-start | bytes 196616 | tf_op jit(solution)/shard_map/ppermute | solution.py:439
  86.8 9.9 %collective-permute-start.17 = (bf16[32,1024]{1,0:T(8,128)(2,1)S(1)}, bf16[32,1024]{1,0:T(8,128)(2,1)S(1)}, u32[]{:S(2)}, u32[]{:S(2)}) collective-permute-start(bf16[32,1024]{1,0:T(8,128)(2,1)S(1)} %get-tuple-element.72), channel_id=1, source_target_pairs={{0,18},{1,19},{2,16},{3,17},{4,22},{5,23},{6,20},{7,21},{8,26},{9,... | collective-permute-start | bytes 196616 | tf_op jit(solution)/shard_map/ppermute | solution.py:439
  89.0 7.7 %collective-permute-start.18 = (bf16[32,1024]{1,0:T(8,128)(2,1)S(1)}, bf16[32,1024]{1,0:T(8,128)(2,1)S(1)}, u32[]{:S(2)}, u32[]{:S(2)}) collective-permute-start(bf16[32,1024]{1,0:T(8,128)(2,1)S(1)} %get-tuple-element.73), channel_id=1, source_target_pairs={{0,3},{1,2},{2,1},{3,0},{4,7},{5,6},{6,5},{7,4},{8,11},{9,10},{10,... | collective-permute-start | bytes 196616 | tf_op jit(solution)/shard_map/ppermute | solution.py:439
  90.1 7.7 %collective-permute-start.19 = (bf16[32,1024]{1,0:T(8,128)(2,1)S(1)}, bf16[32,1024]{1,0:T(8,128)(2,1)S(1)}, u32[]{:S(2)}, u32[]{:S(2)}) collective-permute-start(bf16[32,1024]{1,0:T(8,128)(2,1)S(1)} %get-tuple-element.74), channel_id=1, source_target_pairs={{0,19},{1,18},{2,17},{3,16},{4,23},{5,22},{6,21},{7,20},{8,27},{9,... | collective-permute-start | bytes 196616 | tf_op jit(solution)/shard_map/ppermute | solution.py:439

commit v5 on v3

--- a/solution.py
+++ b/solution.py
@@ -429,7 +429,7 @@
 
     devices = range(owners * head_groups)
     placed = {0: sent[0]}
-    for k in sorted(range(1, parts), key=lambda k: (1 - k % 2, k)):
+    for k in sorted(range(1, parts), key=lambda k: (1 - k % 2, -k)):
         placed[k] = lax.ppermute(sent[k], ("ctx", "head"), [(d, partner(d, k)) for d in devices])
     return pl.pallas_call(
         functools.partial(place_kernel, head_groups, half),

time: 93.1 us -> 94.4 us (1.014)
  waiting for transfers between devices: 32.8 us -> 40.6 us
  starting transfers between devices: 25.3 us -> 18.8 us
    ppermute x7, starting transfers between devices: 9.33 us -> 5.45 us  [body(): lax.ppermute(sent[k], ('ctx', 'head'), [(d, partner(d, k)) for d in devic...]
    ppermute x9, waiting for transfers between devices: 11 us -> 14.6 us  [swap(): return lax.ppermute(x, 'ctx', [(i, i ^ bit) for i in range(owners)])]
    ppermute x9, starting transfers between devices: 10.8 us -> 8.23 us  [swap(): return lax.ppermute(x, 'ctx', [(i, i ^ bit) for i in range(owners)])]
    ppermute x7, waiting for transfers between devices: 6.47 us -> 8.6 us  [body(): lax.ppermute(sent[k], ('ctx', 'head'), [(d, partner(d, k)) for d in devic...]
    ppermute x1, waiting for transfers between devices: 11.7 us -> 13.3 us  [body(): far = {0: lax.ppermute(theirs, 'ctx', across)}]
  transfers between devices with their start and end apart: 19 -> 19, of which waited for: 7 -> 10; matrix products, arithmetic and copies ran while one was open for 0% -> 0% of each run, Pallas kernels for 31% -> 29%
where the time goes in v5:
time: 94.4 us
  waiting for transfers between devices  40.6 us (43%)
  Pallas kernels  31.5 us (33%)
  starting transfers between devices  18.8 us (20%)
  local copies, waits for them, and re-layouts  3.2 us (3%)
    pallas_call x5, Pallas kernels, attend(): pl.pallas_call(functools.partial(attend_kernel, stage), out_shape=out_sha...  25.3 us
    ppermute x9, waiting for transfers between devices, swap(): return lax.ppermute(x, 'ctx', [(i, i ^ bit) for i in range(owners)])  14.6 us
    ppermute x1, waiting for transfers between devices, body(): far = {0: lax.ppermute(theirs, 'ctx', across)}  13.3 us
    ppermute x7, waiting for transfers between devices, body(): lax.ppermute(sent[k], ('ctx', 'head'), [(d, partner(d, k)) for d in devic...  8.6 us
    ppermute x9, starting transfers between devices, swap(): return lax.ppermute(x, 'ctx', [(i, i ^ bit) for i in range(owners)])  8.23 us
    ppermute x7, starting transfers between devices, body(): lax.ppermute(sent[k], ('ctx', 'head'), [(d, partner(d, k)) for d in devic...  5.45 us
    pallas_call x1, Pallas kernels, body(): pl.pallas_call(functools.partial(collect_kernel, owners, cap), out_shape=...  5.28 us
    ppermute x1, waiting for transfers between devices, body(): q_far = lax.ppermute(send_q, 'ctx', across)  4.1 us
  transfers between devices with their start and end apart: 19, of which 10 were waited for; matrix products, arithmetic and copies ran while one was open for 0% of the time, Pallas kernels for 29%

profile of v5, /device:TPU:0, one launch (start us, length us, event | category | flops | bytes accessed | tf_op | source)
XLA Modules:
  0.0 94.4 jit_solution(16678992782845475299)
XLA Ops:
  0.0 1.1 %constant_dynamic-slice_fusion = (bf16[128,1024]{1,0:T(8,128)(2,1)S(1)}, bf16[128,1024]{1,0:T(8,128)(2,1)S(1)}) fusion(bf16[128,2048]{1,0:T(8,128)(2,1)} %param.5, s32[]{:T(128)S(6)} %select_n.13, s32[]{:T(128)S(6)} %select_n.12), kind=kLoop, calls=%fused_computation | loop fusion | bytes 1048584 | tf_op jit(solution)/shard_map/dynamic_slice | solution.py:335
  1.1 0.0 copy-start.2
  1.1 0.0 copy-start.3
  1.1 4.1 %collective-permute-start = (bf16[128,1024]{1,0:T(8,128)(2,1)S(1)}, bf16[128,1024]{1,0:T(8,128)(2,1)S(1)}, u32[]{:S(2)}, u32[]{:S(2)}) collective-permute-start(bf16[128,1024]{1,0:T(8,128)(2,1)S(1)} %get-tuple-element.69), channel_id=1, source_target_pairs={{0,16},{4,20},{8,24},{12,28},{16,0},{20,4},{24,8},{28,12},{1,17},{... | collective-permute-start | bytes 786440 | tf_op jit(solution)/shard_map/ppermute | solution.py:337
  5.2 5.3 %collect_slots.1 = (bf16[1152,256]{1,0:T(8,128)(2,1)}, bf16[640,256]{1,0:T(8,128)(2,1)}, bf16[512,256]{1,0:T(8,128)(2,1)}) custom-call(s32[2,64]{1,0:T(2,128)} %scalars.1, bf16[4096,2,256]{2,1,0:T(2,128)(2,1)} %cache.1, bf16[128,2,256]{2,1,0:T(2,128)(2,1)} %span.1), custom_call_target="tpu_custom_call" | custom-call | bytes 2097152 | tf_op jit(solution)/shard_map/collect_slots/pallas_call | solution.py:343
  10.5 1.1 %collective-permute-start.2 = (bf16[1152,256]{1,0:T(8,128)(2,1)}, bf16[1152,256]{1,0:T(8,128)(2,1)S(1)}, u32[]{:S(2)}, u32[]{:S(2)}) collective-permute-start(bf16[1152,256]{1,0:T(8,128)(2,1)} %get-tuple-element.39.refs_2_.refs_1_), channel_id=1, source_target_pairs={{0,4},{4,0},{8,12},{12,8},{16,20},{20,16},{24,28},{28,24},{1,5},{5... | collective-permute-start | bytes 1769480 | tf_op jit(solution)/shard_map/ppermute | solution.py:364
  11.6 1.5 %collective-permute-start.3 = (bf16[1152,256]{1,0:T(8,128)(2,1)}, bf16[1152,256]{1,0:T(8,128)(2,1)S(1)}, u32[]{:S(2)}, u32[]{:S(2)}) collective-permute-start(bf16[1152,256]{1,0:T(8,128)(2,1)} %get-tuple-element.39.refs_2_.refs_1_), channel_id=1, source_target_pairs={{0,8},{4,12},{8,0},{12,4},{16,24},{20,28},{24,16},{28,20},{1,9},{5... | collective-permute-start | bytes 1769480 | tf_op jit(solution)/shard_map/ppermute | solution.py:364
  13.1 4.1 %collective-permute-done.refs_1_ = bf16[128,1024]{1,0:T(8,128)(2,1)S(1)} collective-permute-done((bf16[128,1024]{1,0:T(8,128)(2,1)S(1)}, bf16[128,1024]{1,0:T(8,128)(2,1)S(1)}, u32[]{:S(2)}, u32[]{:S(2)}) %collective-permute-start) | collective-permute-done | bytes 262176 | tf_op jit(solution)/shard_map/ppermute | solution.py:337
  17.2 0.0 collective-permute-start.1
  17.2 0.0 copy-done.2
  17.2 0.0 copy-done.3
  17.2 0.0 copy-start
  17.2 1.1 %copy-done = bf16[1152,256]{1,0:T(8,128)(2,1)S(1)} copy-done((bf16[1152,256]{1,0:T(8,128)(2,1)S(1)}, bf16[1152,256]{1,0:T(8,128)(2,1)}, u32[]{:S(2)}) %copy-start) | copy-done | bytes 589848
  18.3 2.7 %attend_own.1 = (f32[2048,128]{1,0:T(8,128)S(1)}, f32[2048,256]{1,0:T(8,128)S(1)}, bf16[2048,128]{1,0:T(8,128)(2,1)S(1)}, s32[8]{0:T(128)S(1)}) custom-call(s32[2,64]{1,0:T(2,128)S(1)} %copy-done.3, s32[2,8]{1,0:T(2,128)S(1)} %copy-done.2, bf16[128,1024]{1,0:T(8,128)(2,1)S(1)} %get-tuple-element.70.refs_0_, ...), custom_call_target="tpu_custom_call" | custom-call | flops 268435456 | bytes 262144 | tf_op jit(solution)/shard_map/attend_own/pallas_call | solution.py:293
  21.0 13.3 %collective-permute-done.1.refs_4_ = bf16[640,256]{1,0:T(8,128)(2,1)S(1)} collective-permute-done((bf16[640,256]{1,0:T(8,128)(2,1)}, bf16[640,256]{1,0:T(8,128)(2,1)S(1)}, u32[]{:S(2)}, u32[]{:S(2)}) %collective-permute-start.1) | collective-permute-done | bytes 327712 | tf_op jit(solution)/shard_map/ppermute | solution.py:397
  34.3 0.0 collective-permute-done.2.refs_2_
  34.3 1.3 %collective-permute-start.6 = (bf16[640,256]{1,0:T(8,128)(2,1)S(1)}, bf16[640,256]{1,0:T(8,128)(2,1)S(1)}, u32[]{:S(2)}, u32[]{:S(2)}) collective-permute-start(bf16[640,256]{1,0:T(8,128)(2,1)S(1)} %collective-permute-done.1.refs_4_), channel_id=1, source_target_pairs={{0,4},{4,0},{8,12},{12,8},{16,20},{20,16},{24,28},{28,24},{1,5},{5... | collective-permute-start | bytes 983048 | tf_op jit(solution)/shard_map/ppermute | solution.py:364
  35.6 1.0 %collective-permute-start.5 = (bf16[512,256]{1,0:T(8,128)(2,1)}, bf16[512,256]{1,0:T(8,128)(2,1)S(1)}, u32[]{:S(2)}, u32[]{:S(2)}) collective-permute-start(bf16[512,256]{1,0:T(8,128)(2,1)} %get-tuple-element.47), channel_id=1, source_target_pairs={{0,16},{4,20},{8,24},{12,28},{16,0},{20,4},{24,8},{28,12},{1,17},{... | collective-permute-start | bytes 786440 | tf_op jit(solution)/shard_map/ppermute | solution.py:398
  36.6 3.0 %collective-permute-done.3.refs_3_ = bf16[1152,256]{1,0:T(8,128)(2,1)S(1)} collective-permute-done((bf16[1152,256]{1,0:T(8,128)(2,1)}, bf16[1152,256]{1,0:T(8,128)(2,1)S(1)}, u32[]{:S(2)}, u32[]{:S(2)}) %collective-permute-start.3) | collective-permute-done | bytes 589856 | tf_op jit(solution)/shard_map/ppermute | solution.py:364
  39.6 1.5 %collective-permute-start.4 = (bf16[1152,256]{1,0:T(8,128)(2,1)S(1)}, bf16[1152,256]{1,0:T(8,128)(2,1)S(1)}, u32[]{:S(2)}, u32[]{:S(2)}) collective-permute-start(bf16[1152,256]{1,0:T(8,128)(2,1)S(1)} %collective-permute-done.3.refs_3_), channel_id=1, source_target_pairs={{0,4},{4,0},{8,12},{12,8},{16,20},{20,16},{24,28},{28,24},{1,5},{5... | collective-permute-start | bytes 1769480 | tf_op jit(solution)/shard_map/ppermute | solution.py:364
  41.1 0.1 collective-permute-start.7
  41.2 0.0 copy-start.1
  41.2 1.1 %copy-done.1 = bf16[1152,256]{1,0:T(8,128)(2,1)S(1)} copy-done((bf16[1152,256]{1,0:T(8,128)(2,1)S(1)}, bf16[1152,256]{1,0:T(8,128)(2,1)}, u32[]{:S(2)}) %copy-start.1) | copy-done | bytes 589848
  42.3 6.3 %attend_near.1 = (f32[2048,128]{1,0:T(8,128)S(1)}, f32[2048,256]{1,0:T(8,128)S(1)}) custom-call(s32[8]{0:T(128)S(1)} %get-tuple-element.40.scalars, s32[2,8]{1,0:T(2,128)S(1)} %copy-done.2, bf16[2048,128]{1,0:T(8,128)(2,1)S(1)} %get-tuple-element.41.refs_0_, bf16[1152,256]{1,0:T(8,128)(2,1)S(1)} %copy-done.1, ...), custom_call_target="tpu_custom_call", output_to_operand_aliasing={{0}: (7, {}), {1}: (8, {})} | custom-call | flops 805306368 | bytes 786432 | tf_op jit(solution)/shard_map/attend_near/pallas_call | solution.py:293
  48.6 0.0 collective-permute-done.5.refs_8_
  48.6 0.0 collective-permute-done.6.refs_6_
  48.6 0.2 collective-permute-start.8
  48.8 5.2 %collective-permute-done.7.refs_7_ = bf16[640,256]{1,0:T(8,128)(2,1)S(1)} collective-permute-done((bf16[640,256]{1,0:T(8,128)(2,1)S(1)}, bf16[640,256]{1,0:T(8,128)(2,1)S(1)}, u32[]{:S(2)}, u32[]{:S(2)}) %collective-permute-start.7) | collective-permute-done | bytes 327712 | tf_op jit(solution)/shard_map/ppermute | solution.py:364
  54.0 0.5 collective-permute-start.9
  54.5 1.6 %collective-permute-start.10 = (bf16[512,256]{1,0:T(8,128)(2,1)S(1)}, bf16[512,256]{1,0:T(8,128)(2,1)S(1)}, u32[]{:S(2)}, u32[]{:S(2)}) collective-permute-start(bf16[512,256]{1,0:T(8,128)(2,1)S(1)} %collective-permute-done.5.refs_8_), channel_id=1, source_target_pairs={{0,4},{4,0},{8,12},{12,8},{16,20},{20,16},{24,28},{28,24},{1,5},{5... | collective-permute-start | bytes 786440 | tf_op jit(solution)/shard_map/ppermute | solution.py:364
  56.0 2.8 %collective-permute-done.8.refs_9_ = bf16[512,256]{1,0:T(8,128)(2,1)S(1)} collective-permute-done((bf16[512,256]{1,0:T(8,128)(2,1)S(1)}, bf16[512,256]{1,0:T(8,128)(2,1)S(1)}, u32[]{:S(2)}, u32[]{:S(2)}) %collective-permute-start.8) | collective-permute-done | bytes 262176 | tf_op jit(solution)/shard_map/ppermute | solution.py:364
  58.8 0.5 collective-permute-start.11
  59.3 0.0 collective-permute-done.4.refs_5_
  59.3 7.3 %attend_far.1 = (f32[2048,128]{1,0:T(8,128)S(1)}, f32[2048,256]{1,0:T(8,128)S(1)}) custom-call(s32[8]{0:T(128)S(1)} %get-tuple-element.40.scalars, s32[2,8]{1,0:T(2,128)S(1)} %copy-done.2, bf16[2048,128]{1,0:T(8,128)(2,1)S(1)} %get-tuple-element.41.refs_0_, bf16[1152,256]{1,0:T(8,128)(2,1)S(1)} %copy-done.1, ...), custom_call_target="tpu_custom_call", output_to_operand_aliasing={{0}: (12, {}), {1}: (13, {})} | custom-call | flops 1073741824 | bytes 1048576 | tf_op jit(solution)/shard_map/attend_far/pallas_call | solution.py:293
  66.6 3.6 %collective-permute-done.10.refs_11_ = bf16[512,256]{1,0:T(8,128)(2,1)S(1)} collective-permute-done((bf16[512,256]{1,0:T(8,128)(2,1)S(1)}, bf16[512,256]{1,0:T(8,128)(2,1)S(1)}, u32[]{:S(2)}, u32[]{:S(2)}) %collective-permute-start.10) | collective-permute-done | bytes 262176 | tf_op jit(solution)/shard_map/ppermute | solution.py:364
  70.3 0.0 collective-permute-done.9.refs_10_
  70.3 6.1 %attend_tail.1 = (f32[2048,128]{1,0:T(8,128)S(1)}, f32[2048,256]{1,0:T(8,128)S(1)}) custom-call(s32[8]{0:T(128)S(1)} %get-tuple-element.40.scalars, s32[2,8]{1,0:T(2,128)S(1)} %copy-done.2, bf16[2048,128]{1,0:T(8,128)(2,1)S(1)} %get-tuple-element.41.refs_0_, bf16[1152,256]{1,0:T(8,128)(2,1)S(1)} %copy-done.1, ...), custom_call_target="tpu_custom_call", output_to_operand_aliasing={{0}: (14, {}), {1}: (15, {})} | custom-call | flops 268435456 | bytes 262144 | tf_op jit(solution)/shard_map/attend_tail/pallas_call | solution.py:293
  76.3 0.0 collective-permute-done.11.refs_12_
  76.4 2.9 %attend_last.1 = (f32[2048,128]{1,0:T(8,128)S(1)}, f32[2048,256]{1,0:T(8,128)S(1)}, bf16[32,1024]{1,0:T(8,128)(2,1)S(1)}, bf16[32,1024]{1,0:T(8,128)(2,1)S(1)}, ...) custom-call(s32[8]{0:T(128)S(1)} %get-tuple-element.40.scalars, ...), custom_call_target="tpu_custom_call", output_to_operand_aliasing={{0}: (15, {}), {1}: (16, {})} | custom-call | tf_op jit(solution)/shard_map/attend_last/pallas_call | solution.py:293
  79.3 0.1 collective-permute-start.12
  79.4 0.1 collective-permute-start.13
  79.5 2.9 %collective-permute-start.14 = (bf16[32,1024]{1,0:T(8,128)(2,1)S(1)}, bf16[32,1024]{1,0:T(8,128)(2,1)S(1)}, u32[]{:S(2)}, u32[]{:S(2)}) collective-permute-start(bf16[32,1024]{1,0:T(8,128)(2,1)S(1)} %get-tuple-element.64), channel_id=1, source_target_pairs={{0,17},{1,16},{2,19},{3,18},{4,21},{5,20},{6,23},{7,22},{8,25},{9,... | collective-permute-start | bytes 196616 | tf_op jit(solution)/shard_map/ppermute | solution.py:433
  82.4 0.0 collective-permute-start.15
  82.4 1.6 %collective-permute-start.16 = (bf16[32,1024]{1,0:T(8,128)(2,1)S(1)}, bf16[32,1024]{1,0:T(8,128)(2,1)S(1)}, u32[]{:S(2)}, u32[]{:S(2)}) collective-permute-start(bf16[32,1024]{1,0:T(8,128)(2,1)S(1)} %get-tuple-element.66), channel_id=1, source_target_pairs={{0,18},{1,19},{2,16},{3,17},{4,22},{5,23},{6,20},{7,21},{8,26},{9,... | collective-permute-start | bytes 196616 | tf_op jit(solution)/shard_map/ppermute | solution.py:433
  84.0 3.2 %collective-permute-done.12.refs_1_ = bf16[32,1024]{1,0:T(8,128)(2,1)S(1)} collective-permute-done((bf16[32,1024]{1,0:T(8,128)(2,1)S(1)}, bf16[32,1024]{1,0:T(8,128)(2,1)S(1)}, u32[]{:S(2)}, u32[]{:S(2)}) %collective-permute-start.12) | collective-permute-done | bytes 65568 | tf_op jit(solution)/shard_map/ppermute | solution.py:433
  87.2 0.0 collective-permute-start.17
  87.2 0.0 collective-permute-done.13.refs_2_
  87.2 0.8 collective-permute-start.18
  88.0 0.0 collective-permute-done.14.refs_3_
  88.0 0.0 collective-permute-done.15.refs_4_
  88.0 2.4 %collective-permute-done.16.refs_5_ = bf16[32,1024]{1,0:T(8,128)(2,1)S(1)} collective-permute-done((bf16[32,1024]{1,0:T(8,128)(2,1)S(1)}, bf16[32,1024]{1,0:T(8,128)(2,1)S(1)}, u32[]{:S(2)}, u32[]{:S(2)}) %collective-permute-start.16) | collective-permute-done | bytes 65568 | tf_op jit(solution)/shard_map/ppermute | solution.py:433
  90.4 1.4 %collective-permute-done.17.refs_6_ = bf16[32,1024]{1,0:T(8,128)(2,1)S(1)} collective-permute-done((bf16[32,1024]{1,0:T(8,128)(2,1)S(1)}, bf16[32,1024]{1,0:T(8,128)(2,1)S(1)}, u32[]{:S(2)}, u32[]{:S(2)}) %collective-permute-start.17) | collective-permute-done | bytes 65568 | tf_op jit(solution)/shard_map/ppermute | solution.py:433
  91.8 1.6 %collective-permute-done.18.refs_7_ = bf16[32,1024]{1,0:T(8,128)(2,1)S(1)} collective-permute-done((bf16[32,1024]{1,0:T(8,128)(2,1)S(1)}, bf16[32,1024]{1,0:T(8,128)(2,1)S(1)}, u32[]{:S(2)}, u32[]{:S(2)}) %collective-permute-start.18) | collective-permute-done | bytes 65568 | tf_op jit(solution)/shard_map/ppermute | solution.py:433
  93.4 0.8 place_parts.1
Async XLA Ops:
  1.1 16.2 %copy-start.2 = (s32[2,8]{1,0:T(2,128)S(1)}, s32[2,8]{1,0:T(2,128)}, u32[]{:S(2)}) copy-start(s32[2,8]{1,0:T(2,128)} %offsets.9) | copy-start | bytes 196
  1.1 16.1 %copy-start.3 = (s32[2,64]{1,0:T(2,128)S(1)}, s32[2,64]{1,0:T(2,128)}, u32[]{:S(2)}) copy-start(s32[2,64]{1,0:T(2,128)} %scalars.1) | copy-start | bytes 1540
  1.1 16.1 %collective-permute-start = (bf16[128,1024]{1,0:T(8,128)(2,1)S(1)}, bf16[128,1024]{1,0:T(8,128)(2,1)S(1)}, u32[]{:S(2)}, u32[]{:S(2)}) collective-permute-start(bf16[128,1024]{1,0:T(8,128)(2,1)S(1)} %get-tuple-element.69), channel_id=1, source_target_pairs={{0,16},{4,20},{8,24},{12,28},{16,0},{20,4},{24,8},{28,12},{1,17},{... | collective-permute-start | bytes 786440 | tf_op jit(solution)/shard_map/ppermute | solution.py:337
  10.5 23.8 %collective-permute-start.2 = (bf16[1152,256]{1,0:T(8,128)(2,1)}, bf16[1152,256]{1,0:T(8,128)(2,1)S(1)}, u32[]{:S(2)}, u32[]{:S(2)}) collective-permute-start(bf16[1152,256]{1,0:T(8,128)(2,1)} %get-tuple-element.39.refs_2_.refs_1_), channel_id=1, source_target_pairs={{0,4},{4,0},{8,12},{12,8},{16,20},{20,16},{24,28},{28,24},{1,5},{5... | collective-permute-start | bytes 1769480 | tf_op jit(solution)/shard_map/ppermute | solution.py:364
  11.6 28.0 %collective-permute-start.3 = (bf16[1152,256]{1,0:T(8,128)(2,1)}, bf16[1152,256]{1,0:T(8,128)(2,1)S(1)}, u32[]{:S(2)}, u32[]{:S(2)}) collective-permute-start(bf16[1152,256]{1,0:T(8,128)(2,1)} %get-tuple-element.39.refs_2_.refs_1_), channel_id=1, source_target_pairs={{0,8},{4,12},{8,0},{12,4},{16,24},{20,28},{24,16},{28,20},{1,9},{5... | collective-permute-start | bytes 1769480 | tf_op jit(solution)/shard_map/ppermute | solution.py:364
  17.2 17.1 %collective-permute-start.1 = (bf16[640,256]{1,0:T(8,128)(2,1)}, bf16[640,256]{1,0:T(8,128)(2,1)S(1)}, u32[]{:S(2)}, u32[]{:S(2)}) collective-permute-start(bf16[640,256]{1,0:T(8,128)(2,1)} %get-tuple-element.42), channel_id=1, source_target_pairs={{0,16},{4,20},{8,24},{12,28},{16,0},{20,4},{24,8},{28,12},{1,17},{... | collective-permute-start | bytes 983048 | tf_op jit(solution)/shard_map/ppermute | solution.py:397
  17.2 1.1 %copy-start = (bf16[1152,256]{1,0:T(8,128)(2,1)S(1)}, bf16[1152,256]{1,0:T(8,128)(2,1)}, u32[]{:S(2)}) copy-start(bf16[1152,256]{1,0:T(8,128)(2,1)} %get-tuple-element.39.refs_2_.refs_1_) | copy-start | bytes 1769476
  34.3 14.2 %collective-permute-start.6 = (bf16[640,256]{1,0:T(8,128)(2,1)S(1)}, bf16[640,256]{1,0:T(8,128)(2,1)S(1)}, u32[]{:S(2)}, u32[]{:S(2)}) collective-permute-start(bf16[640,256]{1,0:T(8,128)(2,1)S(1)} %collective-permute-done.1.refs_4_), channel_id=1, source_target_pairs={{0,4},{4,0},{8,12},{12,8},{16,20},{20,16},{24,28},{28,24},{1,5},{5... | collective-permute-start | bytes 983048 | tf_op jit(solution)/shard_map/ppermute | solution.py:364
  35.6 13.0 %collective-permute-start.5 = (bf16[512,256]{1,0:T(8,128)(2,1)}, bf16[512,256]{1,0:T(8,128)(2,1)S(1)}, u32[]{:S(2)}, u32[]{:S(2)}) collective-permute-start(bf16[512,256]{1,0:T(8,128)(2,1)} %get-tuple-element.47), channel_id=1, source_target_pairs={{0,16},{4,20},{8,24},{12,28},{16,0},{20,4},{24,8},{28,12},{1,17},{... | collective-permute-start | bytes 786440 | tf_op jit(solution)/shard_map/ppermute | solution.py:398
  39.6 19.7 %collective-permute-start.4 = (bf16[1152,256]{1,0:T(8,128)(2,1)S(1)}, bf16[1152,256]{1,0:T(8,128)(2,1)S(1)}, u32[]{:S(2)}, u32[]{:S(2)}) collective-permute-start(bf16[1152,256]{1,0:T(8,128)(2,1)S(1)} %collective-permute-done.3.refs_3_), channel_id=1, source_target_pairs={{0,4},{4,0},{8,12},{12,8},{16,20},{20,16},{24,28},{28,24},{1,5},{5... | collective-permute-start | bytes 1769480 | tf_op jit(solution)/shard_map/ppermute | solution.py:364
  41.1 12.9 %collective-permute-start.7 = (bf16[640,256]{1,0:T(8,128)(2,1)S(1)}, bf16[640,256]{1,0:T(8,128)(2,1)S(1)}, u32[]{:S(2)}, u32[]{:S(2)}) collective-permute-start(bf16[640,256]{1,0:T(8,128)(2,1)S(1)} %collective-permute-done.1.refs_4_), channel_id=1, source_target_pairs={{0,8},{4,12},{8,0},{12,4},{16,24},{20,28},{24,16},{28,20},{1,9},{5... | collective-permute-start | bytes 983048 | tf_op jit(solution)/shard_map/ppermute | solution.py:364
  41.2 1.1 %copy-start.1 = (bf16[1152,256]{1,0:T(8,128)(2,1)S(1)}, bf16[1152,256]{1,0:T(8,128)(2,1)}, u32[]{:S(2)}) copy-start(bf16[1152,256]{1,0:T(8,128)(2,1)} %get-tuple-element.39.refs_2_.refs_1_) | copy-start | bytes 1769476
  48.6 10.2 %collective-permute-start.8 = (bf16[512,256]{1,0:T(8,128)(2,1)S(1)}, bf16[512,256]{1,0:T(8,128)(2,1)S(1)}, u32[]{:S(2)}, u32[]{:S(2)}) collective-permute-start(bf16[512,256]{1,0:T(8,128)(2,1)S(1)} %collective-permute-done.5.refs_8_), channel_id=1, source_target_pairs={{0,8},{4,12},{8,0},{12,4},{16,24},{20,28},{24,16},{28,20},{1,9},{5... | collective-permute-start | bytes 786440 | tf_op jit(solution)/shard_map/ppermute | solution.py:364
  54.0 16.3 %collective-permute-start.9 = (bf16[640,256]{1,0:T(8,128)(2,1)S(1)}, bf16[640,256]{1,0:T(8,128)(2,1)S(1)}, u32[]{:S(2)}, u32[]{:S(2)}) collective-permute-start(bf16[640,256]{1,0:T(8,128)(2,1)S(1)} %collective-permute-done.7.refs_7_), channel_id=1, source_target_pairs={{0,4},{4,0},{8,12},{12,8},{16,20},{20,16},{24,28},{28,24},{1,5},{5... | collective-permute-start | bytes 983048 | tf_op jit(solution)/shard_map/ppermute | solution.py:364
  54.5 15.8 %collective-permute-start.10 = (bf16[512,256]{1,0:T(8,128)(2,1)S(1)}, bf16[512,256]{1,0:T(8,128)(2,1)S(1)}, u32[]{:S(2)}, u32[]{:S(2)}) collective-permute-start(bf16[512,256]{1,0:T(8,128)(2,1)S(1)} %collective-permute-done.5.refs_8_), channel_id=1, source_target_pairs={{0,4},{4,0},{8,12},{12,8},{16,20},{20,16},{24,28},{28,24},{1,5},{5... | collective-permute-start | bytes 786440 | tf_op jit(solution)/shard_map/ppermute | solution.py:364
  58.8 17.5 %collective-permute-start.11 = (bf16[512,256]{1,0:T(8,128)(2,1)S(1)}, bf16[512,256]{1,0:T(8,128)(2,1)S(1)}, u32[]{:S(2)}, u32[]{:S(2)}) collective-permute-start(bf16[512,256]{1,0:T(8,128)(2,1)S(1)} %collective-permute-done.8.refs_9_), channel_id=1, source_target_pairs={{0,4},{4,0},{8,12},{12,8},{16,20},{20,16},{24,28},{28,24},{1,5},{5... | collective-permute-start | bytes 786440 | tf_op jit(solution)/shard_map/ppermute | solution.py:364
  79.3 7.9 %collective-permute-start.12 = (bf16[32,1024]{1,0:T(8,128)(2,1)S(1)}, bf16[32,1024]{1,0:T(8,128)(2,1)S(1)}, u32[]{:S(2)}, u32[]{:S(2)}) collective-permute-start(bf16[32,1024]{1,0:T(8,128)(2,1)S(1)} %get-tuple-element.62), channel_id=1, source_target_pairs={{0,16},{1,17},{2,18},{3,19},{4,20},{5,21},{6,22},{7,23},{8,24},{9,... | collective-permute-start | bytes 196616 | tf_op jit(solution)/shard_map/ppermute | solution.py:433
  79.4 7.8 %collective-permute-start.13 = (bf16[32,1024]{1,0:T(8,128)(2,1)S(1)}, bf16[32,1024]{1,0:T(8,128)(2,1)S(1)}, u32[]{:S(2)}, u32[]{:S(2)}) collective-permute-start(bf16[32,1024]{1,0:T(8,128)(2,1)S(1)} %get-tuple-element.63), channel_id=1, source_target_pairs={{0,1},{1,0},{2,3},{3,2},{4,5},{5,4},{6,7},{7,6},{8,9},{9,8},{10,11... | collective-permute-start | bytes 196616 | tf_op jit(solution)/shard_map/ppermute | solution.py:433
  79.5 8.5 %collective-permute-start.14 = (bf16[32,1024]{1,0:T(8,128)(2,1)S(1)}, bf16[32,1024]{1,0:T(8,128)(2,1)S(1)}, u32[]{:S(2)}, u32[]{:S(2)}) collective-permute-start(bf16[32,1024]{1,0:T(8,128)(2,1)S(1)} %get-tuple-element.64), channel_id=1, source_target_pairs={{0,17},{1,16},{2,19},{3,18},{4,21},{5,20},{6,23},{7,22},{8,25},{9,... | collective-permute-start | bytes 196616 | tf_op jit(solution)/shard_map/ppermute | solution.py:433
  82.4 5.6 %collective-permute-start.15 = (bf16[32,1024]{1,0:T(8,128)(2,1)S(1)}, bf16[32,1024]{1,0:T(8,128)(2,1)S(1)}, u32[]{:S(2)}, u32[]{:S(2)}) collective-permute-start(bf16[32,1024]{1,0:T(8,128)(2,1)S(1)} %get-tuple-element.65), channel_id=1, source_target_pairs={{0,2},{1,3},{2,0},{3,1},{4,6},{5,7},{6,4},{7,5},{8,10},{9,11},{10,... | collective-permute-start | bytes 196616 | tf_op jit(solution)/shard_map/ppermute | solution.py:433
  82.4 8.0 %collective-permute-start.16 = (bf16[32,1024]{1,0:T(8,128)(2,1)S(1)}, bf16[32,1024]{1,0:T(8,128)(2,1)S(1)}, u32[]{:S(2)}, u32[]{:S(2)}) collective-permute-start(bf16[32,1024]{1,0:T(8,128)(2,1)S(1)} %get-tuple-element.66), channel_id=1, source_target_pairs={{0,18},{1,19},{2,16},{3,17},{4,22},{5,23},{6,20},{7,21},{8,26},{9,... | collective-permute-start | bytes 196616 | tf_op jit(solution)/shard_map/ppermute | solution.py:433
  87.2 4.6 %collective-permute-start.17 = (bf16[32,1024]{1,0:T(8,128)(2,1)S(1)}, bf16[32,1024]{1,0:T(8,128)(2,1)S(1)}, u32[]{:S(2)}, u32[]{:S(2)}) collective-permute-start(bf16[32,1024]{1,0:T(8,128)(2,1)S(1)} %get-tuple-element.67), channel_id=1, source_target_pairs={{0,3},{1,2},{2,1},{3,0},{4,7},{5,6},{6,5},{7,4},{8,11},{9,10},{10,... | collective-permute-start | bytes 196616 | tf_op jit(solution)/shard_map/ppermute | solution.py:433
  87.2 6.2 %collective-permute-start.18 = (bf16[32,1024]{1,0:T(8,128)(2,1)S(1)}, bf16[32,1024]{1,0:T(8,128)(2,1)S(1)}, u32[]{:S(2)}, u32[]{:S(2)}) collective-permute-start(bf16[32,1024]{1,0:T(8,128)(2,1)S(1)} %get-tuple-element.68), channel_id=1, source_target_pairs={{0,19},{1,18},{2,17},{3,16},{4,23},{5,22},{6,21},{7,20},{8,27},{9,... | collective-permute-start | bytes 196616 | tf_op jit(solution)/shard_map/ppermute | solution.py:433
